TPU v7x, 32 devices: a whole 2x2x4 slice. The times are simulated.
32 devices in a mesh: grp: 2 (over y), seg: 4 (over z), tok: 4 (over x, core).
Axes of the slice: x: 2, y: 2, z: 4, core: 2. Of those that a mesh axis runs over, the one named last changes fastest.
Arguments:
- hidden_in: bfloat16 [4, 4096, 2048], P('grp', ('seg', 'tok')), may hold values from -6 to 6
- cotangent: bfloat16 [4, 4096, 2048], P('grp', ('seg', 'tok')), may hold values from -6 to 6
- piece_start: int32 [4, 4], P('grp', 'seg'), may hold values from 0 to 3840, as said below
- query_weight: bfloat16 [2048, 2048], P('seg', 'tok'), may hold values from -0.125 to 0.125
- key_weight: bfloat16 [2048, 2048], P('seg', 'tok'), may hold values from -0.125 to 0.125
- value_weight: bfloat16 [2048, 2048], P('seg', 'tok'), may hold values from -0.125 to 0.125
- out_weight: bfloat16 [2048, 2048], P('seg', 'tok'), may hold values from -0.375 to 0.375
- gate_weight: bfloat16 [2048, 8192], P('seg', 'tok'), may hold values from -0.125 to 0.125
- up_weight: bfloat16 [2048, 8192], P('seg', 'tok'), may hold values from -0.125 to 0.125
- down_weight: bfloat16 [2048, 8192], P('seg', 'tok'), may hold values from -0.0625 to 0.0625
- attend_gain: float32 [2048], replicated, may hold values from 0.5 to 1.5
- feed_gain: float32 [2048], replicated, may hold values from 0.5 to 1.5
- gate_logit: float32 [16], replicated, may hold values from -2 to 2
Outputs:
- output: bfloat16 [4, 4096, 2048], P('grp', ('seg', 'tok'))
- input_grad: bfloat16 [4, 4096, 2048], P('grp', ('seg', 'tok'))
- query_grad: float32 [2048, 2048], P('seg', 'tok')
- key_grad: float32 [2048, 2048], P('seg', 'tok')
- value_grad: float32 [2048, 2048], P('seg', 'tok')
- out_grad: float32 [2048, 2048], P('seg', 'tok')
- gate_grad: float32 [2048, 8192], P('seg', 'tok')
- up_grad: float32 [2048, 8192], P('seg', 'tok')
- down_grad: float32 [2048, 8192], P('seg', 'tok')
- attend_gain_grad: float32 [2048], replicated
- feed_gain_grad: float32 [2048], replicated
- gate_logit_grad: float32 [16], replicated
Inputs may be any that keep to these rules, and one draw needn't show every extreme that they name: `piece_start`: entry k of a sequence's row is the first position of that sequence's one picture piece of segment k; its 256 positions lie inside positions k * 1024 to (k + 1) * 1024 - 1.
All inputs are finite; a program needn't handle non-finite values.
Results may differ from a plain program's by a relative error of at most 0.02.
Values may be sent and summed in bfloat16 or wider, within the bound.
No kernel may reach another device: no remote copies, remote signals or barrier semaphores. Data moves between devices by JAX's collectives and lax.ppermute only.
A program may use at most 384 MiB of HBM per device.

v0:
```python
import jax
import jax.numpy as jnp
from jax import lax
from jax.sharding import PartitionSpec as P

HEADS = 16
HEAD_DIM = 128
SEG_LEN = 1024
PIECE = 256
BLOCK = 512
MICRO = 2


EPS_NORM = 1e-05
MASKED_SCORE = -1e30


def entering(value, axis, combine, identity):
    count, here = (lax.axis_size(axis), lax.axis_index(axis))
    everything = jax.tree.map(
        lambda part, kind: lax.all_gather(part.astype(kind), axis),
        value,
        (jnp.bfloat16, jnp.bfloat16),
    )
    start = jax.tree.map(
        lambda part, zero: jnp.broadcast_to(jnp.asarray(zero, part.dtype), part.shape),
        value,
        identity,
    )

    def lap(k, before):
        reached = k < here
        new = combine(
            before, jax.tree.map(lambda part, own: part[k].astype(own.dtype), everything, value)
        )
        return jax.tree.map(lambda a, b: jnp.where(reached, a, b), new, before)

    return lax.fori_loop(0, count, lap, start)


def carried_in(value, axis, join, neutral):
    count = lax.axis_size(axis)
    place = lax.axis_index(axis)
    ahead = count - 1 - place
    gathered = jax.tree.map(
        lambda a, kind: lax.all_gather(a.astype(kind), axis),
        value,
        jax.tree.map(lambda a: jnp.bfloat16 if a.dtype == jnp.float32 else a.dtype, value),
    )
    state = jax.tree.map(lambda a, e: jnp.zeros_like(a) + jnp.asarray(e, a.dtype), value, neutral)

    def one(lap, state):
        source = count - 1 - lap
        return join(
            state,
            jax.tree.map(
                lambda a, own: lax.dynamic_index_in_dim(a, source, 0, False).astype(own.dtype),
                gathered,
                value,
            ),
        )

    return lax.fori_loop(0, ahead, one, state)


def for_sending(value):
    return jax.tree.map(lambda a: a.astype(jnp.bfloat16) if a.dtype == jnp.float32 else a, value)


def root_norm(values, gain):
    return values * lax.rsqrt(jnp.mean(values * values, -1, keepdims=True) + EPS_NORM) * gain


def positive_feature(values):
    return jnp.where(values > 0, values + 1.0, jnp.exp(jnp.where(values > 0, 0.0, values)))


def feature_slope(values):
    return jnp.where(values > 0, 1.0, jnp.exp(jnp.where(values > 0, 0.0, values)))


def swish_product(gate_pre, up_pre):
    return jax.nn.silu(gate_pre) * up_pre


def add_pair(earlier, later):
    return (earlier[0] + later[0], earlier[1] + later[1])


def visible_mask(row_first, row_total, key_reach, piece_first):
    rows_at = row_first + jnp.arange(row_total, dtype=jnp.int32)[:, None]
    keys_at = jnp.arange(key_reach, dtype=jnp.int32)[None, :]
    row_in = (rows_at >= piece_first) & (rows_at < piece_first + PIECE)
    key_in = (keys_at >= piece_first) & (keys_at < piece_first + PIECE)
    return (keys_at <= rows_at) | row_in & key_in


def block_scores(queries, key_rows, block_index, piece_first):
    block_first = block_index * BLOCK
    key_reach = min(SEG_LEN, block_first + BLOCK + PIECE - 1)
    query_block = queries[block_first : block_first + BLOCK]
    scores = jnp.einsum(
        "qhd,khd->hqk", query_block, key_rows[:key_reach], preferred_element_type=jnp.float32
    ) * HEAD_DIM ** (-0.5)
    visible = visible_mask(block_first, BLOCK, key_reach, piece_first)
    return (jnp.where(visible[None], scores, MASKED_SCORE), query_block, key_reach)


def forward_pass(
    hidden_rows, piece_first, full_weights, attend_gain, feed_gain, gate_local, head_local
):
    query_full, key_full, value_full, out_full, gate_full, up_full, down_full = full_weights
    head_shape = (SEG_LEN, head_local, HEAD_DIM)
    hidden_f = hidden_rows.astype(jnp.float32)
    normed_a = root_norm(hidden_f, attend_gain).astype(jnp.bfloat16)
    gathered_a = lax.all_gather(normed_a, "tok", axis=0, tiled=True)
    queries = (
        jnp.dot(gathered_a, query_full, preferred_element_type=jnp.float32)
        .astype(jnp.bfloat16)
        .reshape(head_shape)
    )
    key_rows = (
        jnp.dot(gathered_a, key_full, preferred_element_type=jnp.float32)
        .astype(jnp.bfloat16)
        .reshape(head_shape)
    )
    values = (
        jnp.dot(gathered_a, value_full, preferred_element_type=jnp.float32)
        .astype(jnp.bfloat16)
        .reshape(head_shape)
    )
    feat_q = positive_feature(queries.astype(jnp.float32)).astype(jnp.bfloat16)
    feat_k = positive_feature(key_rows.astype(jnp.float32)).astype(jnp.bfloat16)
    contrib = jnp.einsum("khd,khe->hde", feat_k, values, preferred_element_type=jnp.float32)
    count_k = jnp.sum(feat_k.astype(jnp.float32), axis=0)
    memory, norm_mem = entering(
        (contrib, count_k), "seg", add_pair, (jnp.zeros_like(contrib), jnp.zeros_like(count_k))
    )
    memory_low = memory.astype(jnp.bfloat16)
    numerator = jnp.einsum("qhd,hde->qhe", feat_q, memory_low, preferred_element_type=jnp.float32)
    denominator = (
        1.0
        + jnp.einsum(
            "qhd,hd->qh", feat_q.astype(jnp.float32), norm_mem, precision=lax.Precision.HIGHEST
        )[..., None]
    )
    recall = numerator / denominator
    local_parts = []
    log_totals = []
    for block_index in range(SEG_LEN // BLOCK):
        scores, query_block, key_reach = block_scores(queries, key_rows, block_index, piece_first)
        row_peak = jnp.max(scores, axis=-1, keepdims=True)
        shifted = jnp.exp(scores - row_peak)
        row_total = jnp.sum(shifted, axis=-1, keepdims=True)
        prob_low = (shifted / row_total).astype(jnp.bfloat16)
        local_parts.append(
            jnp.einsum(
                "hqk,khd->qhd", prob_low, values[:key_reach], preferred_element_type=jnp.float32
            )
        )
        log_totals.append(row_peak + jnp.log(row_total))
    local_out = jnp.concatenate(local_parts, axis=0)
    gate_share = jax.nn.sigmoid(gate_local)[None, :, None]
    mixed_out = (
        (gate_share * recall + (1.0 - gate_share) * local_out)
        .astype(jnp.bfloat16)
        .reshape(SEG_LEN, -1)
    )
    attended = lax.psum_scatter(
        jnp.einsum("tc,dc->td", mixed_out, out_full, preferred_element_type=jnp.float32),
        "tok",
        scatter_dimension=0,
        tiled=True,
    )
    resid = hidden_f + attended
    normed_f = root_norm(resid, feed_gain).astype(jnp.bfloat16)
    gathered_f = lax.all_gather(normed_f, "tok", axis=0, tiled=True)
    gate_pre = jnp.dot(gathered_f, gate_full, preferred_element_type=jnp.float32)
    up_pre = jnp.dot(gathered_f, up_full, preferred_element_type=jnp.float32)
    inner_act = swish_product(gate_pre, up_pre).astype(jnp.bfloat16)
    feed_result = lax.psum_scatter(
        jnp.einsum("tf,df->td", inner_act, down_full, preferred_element_type=jnp.float32).astype(
            jnp.bfloat16
        ),
        "tok",
        scatter_dimension=0,
        tiled=True,
    ).astype(jnp.float32)
    output_rows = (resid + feed_result).astype(jnp.bfloat16)
    return {
        "output": output_rows,
        "hidden_f": hidden_f,
        "gathered_a": gathered_a,
        "queries": queries,
        "key_rows": key_rows,
        "values": values,
        "feat_q": feat_q,
        "feat_k": feat_k,
        "memory_low": memory_low,
        "norm_mem": norm_mem,
        "denominator": denominator,
        "recall": recall,
        "local_out": local_out,
        "log_totals": log_totals,
        "mixed_out": mixed_out,
        "resid": resid,
        "gathered_f": gathered_f,
        "gate_pre": gate_pre,
        "up_pre": up_pre,
        "inner_act": inner_act,
        "piece_first": piece_first,
    }


def backward_pass(saved, cot_rows, full_weights, attend_gain, feed_gain, gate_local, head_local):
    query_full, key_full, value_full, out_full, gate_full, up_full, down_full = full_weights
    cot_gathered = lax.all_gather(cot_rows, "tok", axis=0, tiled=True)
    grad_inner = jnp.dot(cot_gathered, down_full, preferred_element_type=jnp.float32)
    unused_value, swish_pull = jax.vjp(swish_product, saved["gate_pre"], saved["up_pre"])
    grad_gate_pre, grad_up_pre = swish_pull(grad_inner)
    grad_gate = grad_gate_pre.astype(jnp.bfloat16)
    grad_up = grad_up_pre.astype(jnp.bfloat16)
    down_part = jnp.einsum(
        "td,tf->df", cot_gathered, saved["inner_act"], preferred_element_type=jnp.float32
    )
    gate_part = jnp.einsum(
        "td,tf->df", saved["gathered_f"], grad_gate, preferred_element_type=jnp.float32
    )
    up_part = jnp.einsum(
        "td,tf->df", saved["gathered_f"], grad_up, preferred_element_type=jnp.float32
    )
    grad_normed_f = lax.psum_scatter(
        (
            jnp.einsum("tf,df->td", grad_gate, gate_full, preferred_element_type=jnp.float32)
            + jnp.einsum("tf,df->td", grad_up, up_full, preferred_element_type=jnp.float32)
        ).astype(jnp.bfloat16),
        "tok",
        scatter_dimension=0,
        tiled=True,
    ).astype(jnp.float32)
    unused_norm, norm_pull_f = jax.vjp(root_norm, saved["resid"], feed_gain)
    grad_resid_norm, feed_gain_part = norm_pull_f(grad_normed_f)
    grad_resid = cot_rows.astype(jnp.float32) + grad_resid_norm
    grad_att_low = grad_resid.astype(jnp.bfloat16)
    grad_att_gathered = lax.all_gather(grad_att_low, "tok", axis=0, tiled=True)
    out_part = jnp.einsum(
        "td,tc->dc", grad_att_gathered, saved["mixed_out"], preferred_element_type=jnp.float32
    )
    grad_mixed = jnp.dot(grad_att_gathered, out_full, preferred_element_type=jnp.float32).reshape(
        SEG_LEN, head_local, HEAD_DIM
    )
    gate_sig = jax.nn.sigmoid(gate_local)
    gate_share = gate_sig[None, :, None]
    recall = saved["recall"]
    gate_logit_part = (
        jnp.sum(grad_mixed * (recall - saved["local_out"]), axis=(0, 2))
        * gate_sig
        * (1.0 - gate_sig)
    )
    grad_recall = gate_share * grad_mixed
    grad_local = ((1.0 - gate_share) * grad_mixed).astype(jnp.bfloat16)
    denominator = saved["denominator"]
    grad_numer = (grad_recall / denominator).astype(jnp.bfloat16)
    grad_denom = -jnp.sum(grad_recall * recall / denominator, axis=-1)
    feat_q = saved["feat_q"]
    feat_k = saved["feat_k"]
    values = saved["values"]
    queries = saved["queries"]
    key_rows = saved["key_rows"]
    grad_feat_q = (
        jnp.einsum(
            "qhe,hde->qhd", grad_numer, saved["memory_low"], preferred_element_type=jnp.float32
        )
        + grad_denom[..., None] * saved["norm_mem"][None]
    )
    grad_memory = jnp.einsum("qhd,qhe->hde", feat_q, grad_numer, preferred_element_type=jnp.float32)
    grad_norm_mem = jnp.einsum(
        "qhd,qh->hd", feat_q.astype(jnp.float32), grad_denom, precision=lax.Precision.HIGHEST
    )
    grad_contrib, grad_count = carried_in(
        (grad_memory, grad_norm_mem),
        "seg",
        add_pair,
        (jnp.zeros_like(grad_memory), jnp.zeros_like(grad_norm_mem)),
    )
    grad_feat_k = (
        jnp.einsum(
            "khe,hde->khd",
            values.astype(jnp.float32),
            grad_contrib,
            precision=lax.Precision.HIGHEST,
        )
        + grad_count[None]
    )
    grad_values = jnp.einsum(
        "khd,hde->khe", feat_k.astype(jnp.float32), grad_contrib, precision=lax.Precision.HIGHEST
    )
    grad_keys = jnp.zeros_like(grad_values)
    query_parts = []
    score_scale = HEAD_DIM ** (-0.5)
    for block_index in range(SEG_LEN // BLOCK):
        scores, query_block, key_reach = block_scores(
            queries, key_rows, block_index, saved["piece_first"]
        )
        probs = jnp.exp(scores - saved["log_totals"][block_index])
        prob_low = probs.astype(jnp.bfloat16)
        local_block = grad_local[block_index * BLOCK : (block_index + 1) * BLOCK]
        grad_probs = jnp.einsum(
            "qhe,khe->hqk", local_block, values[:key_reach], preferred_element_type=jnp.float32
        )
        grad_scores = (
            probs * (grad_probs - jnp.sum(probs * grad_probs, axis=-1, keepdims=True))
        ).astype(jnp.bfloat16)
        query_parts.append(
            jnp.einsum(
                "hqk,khd->qhd",
                grad_scores,
                key_rows[:key_reach],
                preferred_element_type=jnp.float32,
            )
            * score_scale
        )
        pad_rows = ((0, SEG_LEN - key_reach), (0, 0), (0, 0))
        grad_keys = grad_keys + jnp.pad(
            jnp.einsum("hqk,qhd->khd", grad_scores, query_block, preferred_element_type=jnp.float32)
            * score_scale,
            pad_rows,
        )
        grad_values = grad_values + jnp.pad(
            jnp.einsum("hqk,qhe->khe", prob_low, local_block, preferred_element_type=jnp.float32),
            pad_rows,
        )
    grad_queries = jnp.concatenate(query_parts, axis=0) + grad_feat_q * feature_slope(
        queries.astype(jnp.float32)
    )
    grad_keys = grad_keys + grad_feat_k * feature_slope(key_rows.astype(jnp.float32))
    query_low = grad_queries.astype(jnp.bfloat16).reshape(SEG_LEN, -1)
    key_low = grad_keys.astype(jnp.bfloat16).reshape(SEG_LEN, -1)
    value_low = grad_values.astype(jnp.bfloat16).reshape(SEG_LEN, -1)
    gathered_a = saved["gathered_a"]
    query_part = jnp.einsum("td,tc->dc", gathered_a, query_low, preferred_element_type=jnp.float32)
    key_part = jnp.einsum("td,tc->dc", gathered_a, key_low, preferred_element_type=jnp.float32)
    value_part = jnp.einsum("td,tc->dc", gathered_a, value_low, preferred_element_type=jnp.float32)
    total = jnp.einsum("tc,dc->td", query_low, query_full, preferred_element_type=jnp.float32)
    total = total + jnp.einsum("tc,dc->td", key_low, key_full, preferred_element_type=jnp.float32)
    grad_normed_a = lax.psum_scatter(
        (
            total
            + jnp.einsum("tc,dc->td", value_low, value_full, preferred_element_type=jnp.float32)
        ).astype(jnp.bfloat16),
        "tok",
        scatter_dimension=0,
        tiled=True,
    ).astype(jnp.float32)
    unused_attend, norm_pull_a = jax.vjp(root_norm, saved["hidden_f"], attend_gain)
    grad_hidden_norm, attend_gain_part = norm_pull_a(grad_normed_a)
    input_rows = (grad_resid + grad_hidden_norm).astype(jnp.bfloat16)
    weight_parts = (query_part, key_part, value_part, out_part, gate_part, up_part, down_part)
    return (input_rows, weight_parts, (attend_gain_part, feed_gain_part, gate_logit_part))


def reduce_rows(weight_parts):
    return jax.tree.map(
        lambda part: part.astype(jnp.float32),
        lax.psum_scatter(for_sending(weight_parts), "seg", scatter_dimension=0, tiled=True),
    )


def body(
    hidden_in,
    cotangent,
    piece_start,
    query_weight,
    key_weight,
    value_weight,
    out_weight,
    gate_weight,
    up_weight,
    down_weight,
    attend_gain,
    feed_gain,
    gate_logit,
):
    full_weights = (
        lax.all_gather(query_weight, "seg", axis=0, tiled=True),
        lax.all_gather(key_weight, "seg", axis=0, tiled=True),
        lax.all_gather(value_weight, "seg", axis=0, tiled=True),
        lax.all_gather(out_weight, "seg", axis=0, tiled=True),
        lax.all_gather(gate_weight, "seg", axis=0, tiled=True),
        lax.all_gather(up_weight, "seg", axis=0, tiled=True),
        lax.all_gather(down_weight, "seg", axis=0, tiled=True),
    )
    head_local = query_weight.shape[1] // HEAD_DIM
    head_first = lax.axis_index("tok") * head_local
    gate_local = lax.dynamic_slice_in_dim(gate_logit, head_first, head_local)
    seg_first = lax.axis_index("seg") * SEG_LEN
    outputs = []
    results = []
    for micro_index in range(MICRO):
        saved = forward_pass(
            hidden_in[micro_index],
            piece_start[micro_index, 0] - seg_first,
            full_weights,
            attend_gain,
            feed_gain,
            gate_local,
            head_local,
        )
        outputs.append(saved["output"])
        results.append(
            backward_pass(
                saved,
                cotangent[micro_index],
                full_weights,
                attend_gain,
                feed_gain,
                gate_local,
                head_local,
            )
        )
    summed = results[0][1]
    for result_item in results[1:]:
        summed = jax.tree.map(jnp.add, summed, result_item[1])
    shards = reduce_rows(summed)
    small_parts = results[0][2]
    for result_item in results[1:]:
        small_parts = jax.tree.map(jnp.add, small_parts, result_item[2])
    placement = (
        jnp.arange(HEADS, dtype=jnp.int32)[None, :]
        == (head_first + jnp.arange(head_local, dtype=jnp.int32))[:, None]
    ).astype(jnp.float32)
    gate_full_grad = jnp.dot(small_parts[2], placement, precision=lax.Precision.HIGHEST)
    group_shards = jax.tree.map(
        lambda part: part.astype(jnp.float32), lax.psum(for_sending(shards), "grp")
    )
    small_sums = lax.psum((small_parts[0], small_parts[1], gate_full_grad), ("grp", "seg", "tok"))
    output_all = jnp.stack(outputs)
    input_all = jnp.stack([result_item[0] for result_item in results])
    return (output_all, input_all) + tuple(group_shards) + tuple(small_sums)


def solution(mesh):
    return jax.shard_map(
        body,
        mesh=mesh,
        in_specs=(
            P("grp", ("seg", "tok"), None),
            P("grp", ("seg", "tok"), None),
            P("grp", "seg"),
            P("seg", "tok"),
            P("seg", "tok"),
            P("seg", "tok"),
            P("seg", "tok"),
            P("seg", "tok"),
            P("seg", "tok"),
            P("seg", "tok"),
            P(),
            P(),
            P(),
        ),
        out_specs=(
            P("grp", ("seg", "tok"), None),
            P("grp", ("seg", "tok"), None),
            P("seg", "tok"),
            P("seg", "tok"),
            P("seg", "tok"),
            P("seg", "tok"),
            P("seg", "tok"),
            P("seg", "tok"),
            P("seg", "tok"),
            P(),
            P(),
            P(),
        ),
        check_vma=False,
    )
```

profile of v0, /device:TPU:0, one launch (start us, length us, event | category | flops | bytes accessed | tf_op | source)
XLA Modules:
  0.0 2415.0 jit_solution(2354189495651943098)
XLA Ops:
  21.1 37.2 %all-gather.32.cloned.1.call-done = bf16[2048,512]{1,0:T(8,128)(2,1)} async-done(((bf16[512,512]{1,0:T(8,128)(2,1)}), bf16[2048,512]{1,0:T(8,128)(2,1)}) %all-gather.32.cloned.1.call-update) | async-done | bytes 2097168 | tf_op jit(solution)/shard_map/all_gather | solution.py:385
  58.3 35.4 %all-gather.26.cloned.1.call-done = bf16[1024,2048]{1,0:T(8,128)(2,1)} async-done(((bf16[256,2048]{1,0:T(8,128)(2,1)}), bf16[1024,2048]{1,0:T(8,128)(2,1)}) %all-gather.26.cloned.1.call-update) | async-done | bytes 4194320 | tf_op jit(solution)/shard_map/all_gather | solution.py:116
  100.0 41.1 %all-gather.30.cloned.1.call-done = bf16[2048,512]{1,0:T(8,128)(2,1)} async-done(((bf16[512,512]{1,0:T(8,128)(2,1)}), bf16[2048,512]{1,0:T(8,128)(2,1)}) %all-gather.30.cloned.1.call-update) | async-done | bytes 2097168 | tf_op jit(solution)/shard_map/all_gather | solution.py:387
  148.4 38.9 %all-gather.28.cloned.1.call-done = bf16[2048,512]{1,0:T(8,128)(2,1)} async-done(((bf16[512,512]{1,0:T(8,128)(2,1)}), bf16[2048,512]{1,0:T(8,128)(2,1)}) %all-gather.28.cloned.1.call-update) | async-done | bytes 2097168 | tf_op jit(solution)/shard_map/all_gather | solution.py:386
  193.9 28.6 %all-gather.44.cloned.1.call-done = bf16[1024,2048]{1,0:T(8,128)(2,1)} async-done(((bf16[256,2048]{1,0:T(8,128)(2,1)}), bf16[1024,2048]{1,0:T(8,128)(2,1)}) %all-gather.44.cloned.1.call-update) | async-done | bytes 4194320 | tf_op jit(solution)/shard_map/all_gather | solution.py:116
  239.3 22.9 all-gather.1
  283.2 15.6 all-gather
  367.0 58.5 %reduce-scatter.16.cloned.1.call-done = f32[256,2048]{1,0:T(8,128)} async-done(((f32[1024,2048]{1,0:T(8,128)}), f32[256,2048]{1,0:T(8,128)}) %reduce-scatter.16.cloned.1.call-update) | async-done | bytes 2097168 | tf_op jit(solution)/shard_map/reduce_scatter | solution.py:169
  425.5 74.5 %reduce-scatter.20.cloned.1.call-done = f32[256,2048]{1,0:T(8,128)} async-done(((f32[1024,2048]{1,0:T(8,128)}), f32[256,2048]{1,0:T(8,128)}) %reduce-scatter.20.cloned.1.call-update) | async-done | bytes 2097168 | tf_op jit(solution)/shard_map/reduce_scatter | solution.py:169
  510.6 140.7 %all-gather.38.cloned.1.call-done = bf16[2048,2048]{1,0:T(8,128)(2,1)} async-done(((bf16[512,2048]{1,0:T(8,128)(2,1)}), bf16[2048,2048]{1,0:T(8,128)(2,1)}) %all-gather.38.cloned.1.call-update) | async-done | bytes 8388624 | tf_op jit(solution)/shard_map/all_gather | solution.py:389
  651.3 34.7 %all-gather.36.cloned.1.call-done = bf16[1024,2048]{1,0:T(8,128)(2,1)} async-done(((bf16[256,2048]{1,0:T(8,128)(2,1)}), bf16[1024,2048]{1,0:T(8,128)(2,1)}) %all-gather.36.cloned.1.call-update) | async-done | bytes 4194320 | tf_op jit(solution)/shard_map/all_gather | solution.py:177
  686.0 14.5 fusion.203
  700.5 136.7 %all-gather.40.cloned.1.call-done = bf16[2048,2048]{1,0:T(8,128)(2,1)} async-done(((bf16[512,2048]{1,0:T(8,128)(2,1)}), bf16[2048,2048]{1,0:T(8,128)(2,1)}) %all-gather.40.cloned.1.call-update) | async-done | bytes 8388624 | tf_op jit(solution)/shard_map/all_gather | solution.py:390
  837.2 14.6 fusion.204
  851.8 20.2 all-gather.52.cloned.1.call-done
  872.0 151.2 %all-gather.42.cloned.1.call-done = bf16[2048,2048]{1,0:T(8,128)(2,1)} async-done(((bf16[512,2048]{1,0:T(8,128)(2,1)}), bf16[2048,2048]{1,0:T(8,128)(2,1)}) %all-gather.42.cloned.1.call-update) | async-done | bytes 8388624 | tf_op jit(solution)/shard_map/all_gather | solution.py:391
  1023.2 21.8 multiply_convert_fusion.3
  1045.0 13.1 fusion.208
  1058.2 12.0 add_convert_fusion.6
  1070.3 42.8 %reduce-scatter.24.cloned.1.call-done = bf16[256,2048]{1,0:T(8,128)(2,1)} async-done(((bf16[1024,2048]{1,0:T(8,128)(2,1)}), bf16[256,2048]{1,0:T(8,128)(2,1)}) %reduce-scatter.24.cloned.1.call-update) | async-done | bytes 1048592 | tf_op jit(solution)/shard_map/reduce_scatter | solution.py:232
  1118.1 34.0 %all-gather.46.cloned.1.call-done = bf16[1024,2048]{1,0:T(8,128)(2,1)} async-done(((bf16[256,2048]{1,0:T(8,128)(2,1)}), bf16[1024,2048]{1,0:T(8,128)(2,1)}) %all-gather.46.cloned.1.call-update) | async-done | bytes 4194320 | tf_op jit(solution)/shard_map/all_gather | solution.py:177
  1152.1 15.6 fusion.206
  1167.7 13.3 fusion.207
  1188.1 21.2 multiply_convert_fusion.1
  1209.3 14.1 fusion.213
  1223.3 12.8 add_convert_fusion.4
  1236.2 13.9 convolution_convert_fusion
  1250.8 30.0 %reduce-scatter.28.cloned.1.call-done = bf16[256,2048]{1,0:T(8,128)(2,1)} async-done(((bf16[1024,2048]{1,0:T(8,128)(2,1)}), bf16[256,2048]{1,0:T(8,128)(2,1)}) %reduce-scatter.28.cloned.1.call-update) | async-done | bytes 1048592 | tf_op jit(solution)/shard_map/reduce_scatter | solution.py:232
  1283.3 44.4 %reduce-scatter.22.cloned.1.call-done = bf16[256,2048]{1,0:T(8,128)(2,1)} async-done(((bf16[1024,2048]{1,0:T(8,128)(2,1)}), bf16[256,2048]{1,0:T(8,128)(2,1)}) %reduce-scatter.22.cloned.1.call-update) | async-done | bytes 1048592 | tf_op jit(solution)/shard_map/reduce_scatter | solution.py:181
  1333.5 15.4 fusion.24
  1348.9 14.7 fusion.6
  1363.7 15.9 fusion.222
  1379.7 14.6 add_convert_fusion.2
  1395.0 15.7 fusion.223
  1410.8 15.4 add_convert_fusion.1
  1464.5 23.5 all-gather.3
  1488.9 22.5 all-gather.6
  1640.9 14.2 convolution_convert_fusion.1
  1655.4 59.5 %reduce-scatter.40.cloned.1.call-done = bf16[512,2048]{1,0:T(8,128)(2,1)} async-done(((bf16[2048,2048]{1,0:T(8,128)(2,1)}), bf16[512,2048]{1,0:T(8,128)(2,1)}) %reduce-scatter.40.cloned.1.call-update) | async-done | bytes 2097168 | tf_op jit(solution)/shard_map/reduce_scatter | solution.py:365
  1715.0 147.7 %reduce-scatter.42.cloned.1.call-done = bf16[512,2048]{1,0:T(8,128)(2,1)} async-done(((bf16[2048,2048]{1,0:T(8,128)(2,1)}), bf16[512,2048]{1,0:T(8,128)(2,1)}) %reduce-scatter.42.cloned.1.call-update) | async-done | bytes 2097168 | tf_op jit(solution)/shard_map/reduce_scatter | solution.py:365
  1862.6 47.5 %reduce-scatter.32.cloned.1.call-done = bf16[512,512]{1,0:T(8,128)(2,1)} async-done(((bf16[2048,512]{1,0:T(8,128)(2,1)}), bf16[512,512]{1,0:T(8,128)(2,1)}) %reduce-scatter.32.cloned.1.call-update) | async-done | bytes 524304 | tf_op jit(solution)/shard_map/reduce_scatter | solution.py:365
  1910.1 45.5 %reduce-scatter.34.cloned.1.call-done = bf16[512,512]{1,0:T(8,128)(2,1)} async-done(((bf16[2048,512]{1,0:T(8,128)(2,1)}), bf16[512,512]{1,0:T(8,128)(2,1)}) %reduce-scatter.34.cloned.1.call-update) | async-done | bytes 524304 | tf_op jit(solution)/shard_map/reduce_scatter | solution.py:365
  1955.6 45.5 %reduce-scatter.36.cloned.1.call-done = bf16[512,512]{1,0:T(8,128)(2,1)} async-done(((bf16[2048,512]{1,0:T(8,128)(2,1)}), bf16[512,512]{1,0:T(8,128)(2,1)}) %reduce-scatter.36.cloned.1.call-update) | async-done | bytes 524304 | tf_op jit(solution)/shard_map/reduce_scatter | solution.py:365
  2001.1 45.4 %reduce-scatter.38.cloned.1.call-done = bf16[512,512]{1,0:T(8,128)(2,1)} async-done(((bf16[2048,512]{1,0:T(8,128)(2,1)}), bf16[512,512]{1,0:T(8,128)(2,1)}) %reduce-scatter.38.cloned.1.call-update) | async-done | bytes 524304 | tf_op jit(solution)/shard_map/reduce_scatter | solution.py:365
  2047.4 46.2 %reduce-scatter.26.cloned.1.call-done = bf16[256,2048]{1,0:T(8,128)(2,1)} async-done(((bf16[1024,2048]{1,0:T(8,128)(2,1)}), bf16[256,2048]{1,0:T(8,128)(2,1)}) %reduce-scatter.26.cloned.1.call-update) | async-done | bytes 1048592 | tf_op jit(solution)/shard_map/reduce_scatter | solution.py:346
  2093.6 47.6 %reduce-scatter.30.cloned.1.call-done = bf16[256,2048]{1,0:T(8,128)(2,1)} async-done(((bf16[1024,2048]{1,0:T(8,128)(2,1)}), bf16[256,2048]{1,0:T(8,128)(2,1)}) %reduce-scatter.30.cloned.1.call-update) | async-done | bytes 1048592 | tf_op jit(solution)/shard_map/reduce_scatter | solution.py:346
  2144.5 40.0 %all-reduce.4 = (f32[2048]{0:T(1024)}, f32[2048]{0:T(1024)}, f32[16]{0:T(128)}) all-reduce(f32[2048]{0:T(1024)S(1)} %add.569, f32[2048]{0:T(1024)S(1)} %add.570, f32[16]{0:T(128)S(1)} %convolution_bitcast_fusion), channel_id=1, replica_groups=mesh['grp'=2,'seg'=4,'tok'=4] {'grp','seg','tok'}, use_global_device_ids=true, to_apply=%region_56.57 | all-reduce | flops 4112 | bytes 32896 | tf_op jit(solution)/shard_map/psum | solution.py:436
  2198.3 194.9 %all-reduce.8.cloned.1.call-done = (bf16[512,2048]{0,1:T(8,128)(2,1)}, bf16[512,512]{1,0:T(8,128)(2,1)}, bf16[512,512]{1,0:T(8,128)(2,1)}, bf16[512,512]{1,0:T(8...) async-done(((bf16[512,2048]{0,1:T(8,128)(2,1)}, bf16[512,512]{1,0:T(8,128)(2,1)}, bf16[512,512]{1,0:T(8,128)(2,1)}, ...) | async-done | bytes 8388624 | tf_op jit(solution)/shard_map/psum | solution.py:434
  (650 shorter events, 387.3 us)
Async XLA Ops:
  7.2 51.1 %all-gather.32.cloned.1.call-start = ((), (), s32[]{:S(2)}) async-start(), calls=%async_computation.18 | async-start | bytes 2621440 | tf_op jit(solution)/shard_map/all_gather | solution.py:385
  7.9 85.7 %all-gather.26.cloned.1.call-start = ((), (), s32[]{:S(2)}) async-start(), calls=%async_computation.15 | async-start | bytes 5242880 | tf_op jit(solution)/shard_map/all_gather | solution.py:116
  12.5 128.7 %all-gather.30.cloned.1.call-start = ((), (), s32[]{:S(2)}) async-start(), calls=%async_computation.17 | async-start | bytes 2621440 | tf_op jit(solution)/shard_map/all_gather | solution.py:387
  13.2 174.1 %all-gather.28.cloned.1.call-start = ((), (), s32[]{:S(2)}) async-start(), calls=%async_computation.16 | async-start | bytes 2621440 | tf_op jit(solution)/shard_map/all_gather | solution.py:386
  13.8 208.7 %all-gather.44.cloned.1.call-start = ((), (), s32[]{:S(2)}) async-start(), calls=%async_computation.26 | async-start | bytes 5242880 | tf_op jit(solution)/shard_map/all_gather | solution.py:116
  14.4 333.5 %all-gather.34.cloned.1.call-start = ((), (), s32[]{:S(2)}) async-start(), calls=%async_computation.19 | async-start | bytes 2621440 | tf_op jit(solution)/shard_map/all_gather | solution.py:388
  15.0 410.5 %reduce-scatter.16.cloned.1.call-start = ((), (), s32[]{:S(2)}) async-start(), calls=%async_computation.20 | async-start | bytes 10485760 | tf_op jit(solution)/shard_map/reduce_scatter | solution.py:169
  18.2 326.3 %copy-start.148 = (f32[4]{0:T(128)}, f32[4]{0:T(128)S(1)}, u32[]{:S(2)}) copy-start(f32[4]{0:T(128)S(1)} %get-tuple-element.547) | copy-start | bytes 52
  18.2 326.3 %copy-start.150 = (f32[4]{0:T(128)}, f32[4]{0:T(128)S(1)}, u32[]{:S(2)}) copy-start(f32[4]{0:T(128)S(1)} %get-tuple-element.546) | copy-start | bytes 52
  192.9 118.6 %copy-start.18 = (bf16[1024,512]{0,1:T(8,128)(2,1)}, bf16[1024,512]{0,1:T(8,128)(2,1)S(1)}, u32[]{:S(2)}) copy-start(bf16[1024,512]{0,1:T(8,128)(2,1)S(1)} %get-tuple-element.586) | copy-start | bytes 3145732
  355.6 144.4 %reduce-scatter.20.cloned.1.call-start = ((), (), s32[]{:S(2)}) async-start(), calls=%async_computation.27 | async-start | bytes 10485760 | tf_op jit(solution)/shard_map/reduce_scatter | solution.py:169
  366.0 285.3 %all-gather.38.cloned.1.call-start = ((), (), s32[]{:S(2)}) async-start(), calls=%async_computation.22 | async-start | bytes 10485760 | tf_op jit(solution)/shard_map/all_gather | solution.py:389
  366.7 138.7 %copy-start.100 = (f32[2048]{0:T(1024)S(1)}, f32[2048]{0:T(1024)}, u32[]{:S(2)}) copy-start(f32[2048]{0:T(1024)} %param.32) | copy-start | bytes 24580
  366.7 319.3 %all-gather.36.cloned.1.call-start = ((), (), s32[]{:S(2)}) async-start(), calls=%async_computation.21 | async-start | bytes 5242880 | tf_op jit(solution)/shard_map/all_gather | solution.py:177
  504.1 823.7 %copy-start.130 = (f32[256]{0:T(256)}, f32[256]{0:T(256)S(1)}, u32[]{:S(2)}) copy-start(f32[256]{0:T(256)S(1)} %fusion.168) | copy-start | bytes 3076
  506.6 330.6 %all-gather.40.cloned.1.call-start = ((), (), s32[]{:S(2)}) async-start(), calls=%async_computation.23 | async-start | bytes 10485760 | tf_op jit(solution)/shard_map/all_gather | solution.py:390
  507.4 364.6 %all-gather.52.cloned.1.call-start = ((), (), s32[]{:S(2)}) async-start(), calls=%async_computation.43 | async-start | bytes 5242880 | tf_op jit(solution)/shard_map/all_gather | solution.py:217
  509.8 513.4 %all-gather.42.cloned.1.call-start = ((), (), s32[]{:S(2)}) async-start(), calls=%async_computation.24 | async-start | bytes 10485760 | tf_op jit(solution)/shard_map/all_gather | solution.py:391
  510.5 602.6 %reduce-scatter.24.cloned.1.call-start = ((), (), s32[]{:S(2)}) async-start(), calls=%async_computation.30 | async-start | bytes 5242880 | tf_op jit(solution)/shard_map/reduce_scatter | solution.py:232
  1070.2 81.9 %all-gather.46.cloned.1.call-start = ((), (), s32[]{:S(2)}) async-start(), calls=%async_computation.28 | async-start | bytes 5242880 | tf_op jit(solution)/shard_map/all_gather | solution.py:177
  1070.3 257.5 %copy-start.132 = (f32[256]{0:T(256)}, f32[256]{0:T(256)S(1)}, u32[]{:S(2)}) copy-start(f32[256]{0:T(256)S(1)} %fusion.170) | copy-start | bytes 3076
  1117.4 70.6 %all-gather.54.cloned.1.call-start = ((), (), s32[]{:S(2)}) async-start(), calls=%async_computation.44 | async-start | bytes 5242880 | tf_op jit(solution)/shard_map/all_gather | solution.py:217
  1118.0 162.8 %reduce-scatter.28.cloned.1.call-start = ((), (), s32[]{:S(2)}) async-start(), calls=%async_computation.33 | async-start | bytes 5242880 | tf_op jit(solution)/shard_map/reduce_scatter | solution.py:232
  1236.1 91.6 %reduce-scatter.22.cloned.1.call-start = ((), (), s32[]{:S(2)}) async-start(), calls=%async_computation.29 | async-start | bytes 5242880 | tf_op jit(solution)/shard_map/reduce_scatter | solution.py:181
  1250.2 176.8 %all-gather.50.cloned.1.call-start = ((), (), s32[]{:S(2)}) async-start(), calls=%async_computation.34 | async-start | bytes 5242880 | tf_op jit(solution)/shard_map/all_gather | solution.py:245
  1332.8 99.5 %all-gather.48.cloned.1.call-start = ((), (), s32[]{:S(2)}) async-start(), calls=%async_computation.31 | async-start | bytes 5242880 | tf_op jit(solution)/shard_map/all_gather | solution.py:245
  1333.4 322.0 %reduce-scatter.44.cloned.1.call-start = ((), (), s32[]{:S(2)}) async-start(), calls=%async_computation.42 | async-start | bytes 10485760 | tf_op jit(solution)/shard_map/reduce_scatter | solution.py:365
  1363.6 351.3 %reduce-scatter.40.cloned.1.call-start = ((), (), s32[]{:S(2)}) async-start(), calls=%async_computation.40 | async-start | bytes 10485760 | tf_op jit(solution)/shard_map/reduce_scatter | solution.py:365
  1394.3 468.3 %reduce-scatter.42.cloned.1.call-start = ((), (), s32[]{:S(2)}) async-start(), calls=%async_computation.41 | async-start | bytes 10485760 | tf_op jit(solution)/shard_map/reduce_scatter | solution.py:365
  1426.2 483.9 %reduce-scatter.32.cloned.1.call-start = ((), (), s32[]{:S(2)}) async-start(), calls=%async_computation.36 | async-start | bytes 2621440 | tf_op jit(solution)/shard_map/reduce_scatter | solution.py:365
  1441.5 83.2 %copy-start.31 = (bf16[1024,4,128]{0,2,1:T(8,128)(2,1)}, bf16[1024,4,128]{0,2,1:T(8,128)(2,1)S(1)}, u32[]{:S(2)}) copy-start(bf16[1024,4,128]{0,2,1:T(8,128)(2,1)S(1)} %get-tuple-element.578) | copy-start | bytes 3145732
  1558.6 397.0 %reduce-scatter.34.cloned.1.call-start = ((), (), s32[]{:S(2)}) async-start(), calls=%async_computation.37 | async-start | bytes 2621440 | tf_op jit(solution)/shard_map/reduce_scatter | solution.py:365
  1582.6 418.5 %reduce-scatter.36.cloned.1.call-start = ((), (), s32[]{:S(2)}) async-start(), calls=%async_computation.38 | async-start | bytes 2621440 | tf_op jit(solution)/shard_map/reduce_scatter | solution.py:365
  1606.0 440.5 %reduce-scatter.38.cloned.1.call-start = ((), (), s32[]{:S(2)}) async-start(), calls=%async_computation.39 | async-start | bytes 2621440 | tf_op jit(solution)/shard_map/reduce_scatter | solution.py:365
  1615.7 477.9 %reduce-scatter.26.cloned.1.call-start = ((), (), s32[]{:S(2)}) async-start(), calls=%async_computation.32 | async-start | bytes 5242880 | tf_op jit(solution)/shard_map/reduce_scatter | solution.py:346
  1627.9 513.3 %reduce-scatter.30.cloned.1.call-start = ((), (), s32[]{:S(2)}) async-start(), calls=%async_computation.35 | async-start | bytes 5242880 | tf_op jit(solution)/shard_map/reduce_scatter | solution.py:346
  1640.9 548.2 %reduce-scatter.18.cloned.1.call-start = ((), (), s32[]{:S(2)}) async-start(), calls=%async_computation.25 | async-start | bytes 5242880 | tf_op jit(solution)/shard_map/reduce_scatter | solution.py:181
  1655.1 738.2 %all-reduce.8.cloned.1.call-start = ((), (), s32[]{:S(2)}) async-start(), calls=%async_computation.45 | async-start | bytes 16777216 | tf_op jit(solution)/shard_map/psum | solution.py:434
  2046.5 94.8 %copy-start.5 = (bf16[2,256,2048]{2,1,0:T(8,128)(2,1)S(1)}, bf16[2,256,2048]{2,1,0:T(8,128)(2,1)}, u32[]{:S(2)}) copy-start(bf16[2,256,2048]{2,1,0:T(8,128)(2,1)} %param.21) | copy-start | bytes 6291460
  2046.5 94.7 %copy-start.103 = (f32[2048]{0:T(1024)S(1)}, f32[2048]{0:T(1024)}, u32[]{:S(2)}) copy-start(f32[2048]{0:T(1024)} %param.31) | copy-start | bytes 24580
  2046.5 94.7 %copy-start.135 = (f32[256]{0:T(256)S(1)}, f32[256]{0:T(256)}, u32[]{:S(2)}) copy-start(f32[256]{0:T(256)} %copy-done.134) | copy-start | bytes 3076
  2046.5 94.7 %copy-start.137 = (f32[256]{0:T(256)S(1)}, f32[256]{0:T(256)}, u32[]{:S(2)}) copy-start(f32[256]{0:T(256)} %copy-done.136) | copy-start | bytes 3076
  2047.4 137.1 %copy-start.139 = (f32[256]{0:T(256)S(1)}, f32[256]{0:T(256)}, u32[]{:S(2)}) copy-start(f32[256]{0:T(256)} %copy-done.138) | copy-start | bytes 3076
  2047.4 137.1 %copy-start.141 = (f32[256]{0:T(256)S(1)}, f32[256]{0:T(256)}, u32[]{:S(2)}) copy-start(f32[256]{0:T(256)} %copy-done.140) | copy-start | bytes 3076
  2047.4 141.6 %copy-start.26 = (bf16[256,2048]{1,0:T(8,128)(2,1)S(1)}, bf16[256,2048]{1,0:T(8,128)(2,1)}, u32[]{:S(2)}) copy-start(bf16[256,2048]{1,0:T(8,128)(2,1)} %reduce-scatter.24.cloned.1.call-done) | copy-start | bytes 3145732
  2047.4 141.6 %copy-start.101 = (f32[2048]{0:T(1024)S(1)}, f32[2048]{0:T(1024)}, u32[]{:S(2)}) copy-start(f32[2048]{0:T(1024)} %param.32) | copy-start | bytes 24580
  2047.4 141.6 %copy-start.131 = (f32[256]{0:T(256)S(1)}, f32[256]{0:T(256)}, u32[]{:S(2)}) copy-start(f32[256]{0:T(256)} %copy-done.130) | copy-start | bytes 3076
  2047.4 141.6 %copy-start.145 = (f32[256]{0:T(256)S(1)}, f32[256]{0:T(256)}, u32[]{:S(2)}) copy-start(f32[256]{0:T(256)} %copy-done.144) | copy-start | bytes 3076
  (182 other events, 1425.9 us)
Sparse Core Ops, SparseCore 0:
  9.6 48.6 all-gather.31
  60.4 33.1 all-gather.25
  95.2 45.9 all-gather.29
  142.6 44.6 all-gather.27
  189.3 33.1 all-gather.43
  223.9 54.3 all-gather.33
  355.8 69.6 reduce-scatter.15
  428.2 71.7 reduce-scatter.19
  501.6 149.6 all-gather.37
  653.2 32.6 all-gather.35
  687.6 149.6 all-gather.39
  839.2 32.6 all-gather.51
  873.5 149.6 all-gather.41
  1070.3 42.7 reduce-scatter.23
  1117.6 34.4 all-gather.45
  1153.6 34.4 all-gather.53
  1236.3 44.5 reduce-scatter.27
  1283.2 44.5 reduce-scatter.21
  1333.0 34.4 all-gather.49
  1369.0 34.4 all-gather.47
  1406.0 161.2 reduce-scatter.43
  1569.8 145.1 reduce-scatter.39
  1717.4 145.1 reduce-scatter.41
  1865.5 44.5 reduce-scatter.31
  1912.4 43.1 reduce-scatter.33
  1957.9 43.1 reduce-scatter.35
  2003.2 43.1 reduce-scatter.37
  2049.7 43.8 reduce-scatter.25
  2096.7 44.4 reduce-scatter.29
  2143.8 45.2 reduce-scatter.17
  2192.1 201.1 all-reduce.7
where the time goes:
time: 2420 us
  waiting for transfers between devices  1650 us (68%)
  matrix products  455 us (19%)
  blocking collectives  163 us (7%)
  other arithmetic  83.2 us (3%)
  local copies, waits for them, and re-layouts  45.3 us (2%)
    reduce_scatter x7, waiting for transfers between devices, reduce_rows(): lax.psum_scatter(for_sending(weight_parts), 'seg', scatter_dimension=0, t...  391 us
    psum x1, waiting for transfers between devices, body(): lax.psum(for_sending(shards), 'grp')  195 us
    all_gather x1, waiting for transfers between devices, body(): lax.all_gather(down_weight, 'seg', axis=0, tiled=True)  151 us
    all_gather x1, waiting for transfers between devices, body(): lax.all_gather(gate_weight, 'seg', axis=0, tiled=True)  141 us
    all_gather x1, waiting for transfers between devices, body(): lax.all_gather(up_weight, 'seg', axis=0, tiled=True)  137 us
    reduce_scatter x2, waiting for transfers between devices, forward_pass(): lax.psum_scatter(jnp.einsum('tc,dc->td', mixed_out, out_full, preferred_e...  133 us
    reduce_scatter x2, waiting for transfers between devices, backward_pass(): lax.psum_scatter((total + jnp.einsum('tc,dc->td', value_low, value_full,...  93.8 us
    reduce_scatter x2, waiting for transfers between devices, backward_pass(): lax.psum_scatter((jnp.einsum('tf,df->td', grad_gate, gate_full, preferred...  72.8 us
  transfers between devices with their start and end apart: 31, of which 27 were waited for; matrix products, arithmetic and copies ran while one was open for 17% of the time, Pallas kernels for 0%

commit v1 on v0

v1 whole, which is shorter than its diff:
```python
import jax
import jax.numpy as jnp
from jax import lax
from jax.experimental import pallas as pl
from jax.experimental.pallas import tpu as pltpu
from jax.sharding import PartitionSpec as P

HEADS = 16
HEAD_DIM = 128
SEG_LEN = 1024
PIECE = 256
VMEM_BYTES = 60 * 1024 * 1024
MICRO = 2


EPS_NORM = 1e-05
MASKED_SCORE = -1e30


class Line:
    def __init__(self, token):
        self.token = token

    def hold(self, value):
        value, self.token = lax.optimization_barrier((value, self.token))
        return value

    def __call__(self, step, *inputs):
        return self.hold(step(*self.hold(inputs)))


def tok_bits():
    return [1 << k for k in range(lax.axis_size("tok").bit_length() - 1)]


def tok_swap(value, bit):
    count = lax.axis_size("tok")
    return lax.ppermute(value, "tok", [(k, k ^ bit) for k in range(count)])


def tok_at(bit):
    return jnp.where((lax.axis_index("tok") & bit) == 0, 0, 1)


def grp_swap(value):
    return lax.ppermute(value, "grp", [(0, 1), (1, 0)])


def tok_pieces(rows, bits):
    pieces = {0: rows}
    for bit in reversed(bits):
        for at in sorted(pieces):
            pieces[at | bit] = tok_swap(pieces[at], bit)
    return pieces


class FirstPiece:
    def __init__(self, rows, bits):
        self.rows = rows
        self.bits = bits
        self.got = tok_swap(rows, bits[-1])

    def rest(self, line):
        pieces = {0: self.rows, self.bits[-1]: line.hold(self.got)}
        for bit in reversed(self.bits[:-1]):
            for at in sorted(pieces):
                pieces[at | bit] = tok_swap(pieces[at], bit)
        return pieces


def added(kept, got):
    return kept.astype(jnp.float32) + got.astype(jnp.float32)


class Scatter:
    def __init__(self, kept, sent):
        self.bits = tok_bits()
        self.terms = (kept, tok_swap(sent, self.bits[0]))

    def go_on(self, line):
        def cut(*terms):
            half = terms[0].shape[0] // 2
            return sum(term[half:].astype(jnp.float32) for term in terms).astype(jnp.bfloat16)

        for bit in self.bits[1:]:
            got = tok_swap(line(cut, *self.terms), bit)
            half = got.shape[0]
            self.terms = tuple(term[:half] for term in self.terms) + (got,)


def total_of(terms):
    return sum(term.astype(jnp.float32) for term in terms)


def tok_order(bits):
    order = [0]
    for bit in reversed(bits):
        order = order + [at | bit for at in order]
    return order


def kernel_params():
    return pltpu.CompilerParams(vmem_limit_bytes=VMEM_BYTES)


def kernel_cost(flops, *arrays):
    moved = sum(a.size * a.dtype.itemsize for a in arrays)
    return pl.CostEstimate(flops=flops, transcendentals=0, bytes_accessed=moved)


def any_space():
    return pl.BlockSpec(memory_space=pl.ANY)


def kept_block(shape):
    return pl.BlockSpec(shape, lambda *at: (0,) * len(shape), pipeline_mode=pl.Buffered(1))


def place(pieces, spots):
    rows, width = pieces[0].shape[-2:]
    total = sum(p.shape[0] for p in pieces)

    def kernel(spots_ref, *refs):
        *ins, out, held, arrive, leave = refs
        copies = []
        for ref in ins:
            for j in range(ref.shape[0]):
                at = len(copies)
                start = pl.multiple_of(spots_ref[at] * rows, rows)
                copies.append(
                    (
                        pltpu.make_async_copy(ref.at[j], held.at[at], arrive.at[at]),
                        pltpu.make_async_copy(
                            held.at[at], out.at[pl.ds(start, rows)], leave.at[at]
                        ),
                    )
                )
        for first, _ in copies:
            first.start()
        for first, then in copies:
            first.wait()
            then.start()
        for _, then in copies:
            then.wait()

    out = jax.ShapeDtypeStruct((total * rows, width), pieces[0].dtype)
    return pl.pallas_call(
        kernel,
        in_specs=[pl.BlockSpec(memory_space=pltpu.SMEM)] + [any_space()] * len(pieces),
        out_specs=any_space(),
        out_shape=out,
        scratch_shapes=[
            pltpu.VMEM((total, rows, width), pieces[0].dtype),
            pltpu.SemaphoreType.DMA((total,)),
            pltpu.SemaphoreType.DMA((total,)),
        ],
        compiler_params=kernel_params(),
        cost_estimate=kernel_cost(0, out, out),
    )(spots, *pieces)


def over_pieces(pieces, which, extra, extra_specs, outs, compute, flops):
    rows, width = pieces[0].shape[-2:]
    total = rows * len(pieces)
    block = max(rows, min(512, total))
    each = block // rows

    def kernel(*refs):
        ins = refs[: len(pieces)]
        others = refs[len(pieces) : len(pieces) + len(extra)]
        results = refs[len(pieces) + len(extra) : -2]
        held, arrive = refs[-2:]
        step = pl.program_id(0)

        def copy(at, ref):
            return pltpu.make_async_copy(
                ref.at[which], held.at[pl.ds(at * rows, rows)], arrive.at[at]
            )

        @pl.when(step == 0)
        def start_all():
            for at, ref in enumerate(ins):
                copy(at, ref).start()

        for part in range(each):
            copy(step * each + part, ins[0]).wait()
        x = held[pl.ds(pl.multiple_of(step * block, block), block)]
        results[0][...] = x
        compute(x, others, results[1:])

    row_spec = lambda n: pl.BlockSpec((block, n), lambda i: (i, 0))
    shapes = [jax.ShapeDtypeStruct((total, n), jnp.bfloat16) for n in (width,) + tuple(outs)]
    return pl.pallas_call(
        kernel,
        grid=(total // block,),
        in_specs=[any_space()] * len(pieces) + [spec(row_spec) for spec in extra_specs],
        out_specs=[row_spec(s.shape[1]) for s in shapes],
        out_shape=shapes,
        scratch_shapes=[
            pltpu.VMEM((total, width), pieces[0].dtype),
            pltpu.SemaphoreType.DMA((len(pieces),)),
        ],
        compiler_params=kernel_params(),
        cost_estimate=kernel_cost(flops, *shapes, *extra),
    )(*pieces, *extra)


def feed_forward(pieces, which, weight):
    hidden = weight.shape[1] // 2
    total = len(pieces) * pieces[0].shape[-2]

    def compute(x, others, results):
        both = jnp.dot(x, others[0][...], preferred_element_type=jnp.float32)
        gate, up = (both[:, :hidden], both[:, hidden:])
        results[0][...] = both.astype(jnp.bfloat16)
        results[1][...] = (gate * jax.nn.sigmoid(gate) * up).astype(jnp.bfloat16)

    return over_pieces(
        pieces,
        which,
        (weight,),
        (lambda row_spec: kept_block(weight.shape),),
        (2 * hidden, hidden),
        compute,
        2 * total * weight.size,
    )


def feed_backward(pieces, which, weight, both):
    hidden = weight.shape[1]
    total = len(pieces) * pieces[0].shape[-2]

    def compute(x, others, results):
        grad = jnp.dot(x, others[0][...], preferred_element_type=jnp.float32)
        gate = others[1][:, :hidden].astype(jnp.float32)
        up = others[1][:, hidden:].astype(jnp.float32)
        sig = jax.nn.sigmoid(gate)
        results[0][:, :hidden] = (grad * up * sig * (1.0 + gate * (1.0 - sig))).astype(jnp.bfloat16)
        results[0][:, hidden:] = (grad * gate * sig).astype(jnp.bfloat16)

    return over_pieces(
        pieces,
        which,
        (weight, both),
        (lambda row_spec: kept_block(weight.shape), lambda row_spec: row_spec(2 * hidden)),
        (2 * hidden,),
        compute,
        2 * total * weight.size,
    )


def products_cut(lefts, weights, order):
    total, width = (lefts[0].shape[0], weights[0].shape[0])
    steps = order.shape[0]
    rows = total // steps
    half = steps // 2
    pairs = len(lefts)

    def kernel(order_ref, *refs):
        out = 0.0
        for left, weight in zip(refs[:pairs], refs[pairs : 2 * pairs]):
            out = out + lax.dot_general(
                left[...],
                weight[...],
                (((1,), (1,)), ((), ())),
                preferred_element_type=jnp.float32,
            )
        sent_ref, kept_ref = refs[2 * pairs :]
        step = pl.program_id(0)

        @pl.when(step < half)
        def first_part():
            sent_ref[...] = out.astype(jnp.bfloat16)

        @pl.when(step >= half)
        def second_part():
            kept_ref[...] = out.astype(jnp.bfloat16)

    part = jax.ShapeDtypeStruct((total // 2, width), jnp.bfloat16)
    sent, kept = pl.pallas_call(
        kernel,
        grid_spec=pltpu.PrefetchScalarGridSpec(
            num_scalar_prefetch=1,
            grid=(steps,),
            in_specs=[
                pl.BlockSpec(
                    (rows, left.shape[1]), lambda i, at: (at[lax.rem(i + half, steps)], 0)
                )
                for left in lefts
            ]
            + [kept_block(weight.shape) for weight in weights],
            out_specs=[
                pl.BlockSpec((rows, width), lambda i, at: (jnp.minimum(i, half - 1), 0)),
                pl.BlockSpec((rows, width), lambda i, at: (jnp.maximum(i - half, 0), 0)),
            ],
        ),
        out_shape=[part, part],
        compiler_params=kernel_params(),
        cost_estimate=kernel_cost(
            sum(2 * total * weight.size for weight in weights), part, part, *lefts, *weights
        ),
    )(order, *lefts, *weights)
    return (kept, sent)


def grad_product(rows_of, columns_of):
    pairs = len(rows_of)
    total, width = rows_of[0].shape
    columns = columns_of[0].shape[1]
    block = 256

    def kernel(*refs):
        out = 0.0
        for left, right in zip(refs[:pairs], refs[pairs : 2 * pairs]):
            out = out + lax.dot_general(
                left[...],
                right[...],
                (((0,), (0,)), ((), ())),
                preferred_element_type=jnp.float32,
            )
        refs[-1][...] = out.astype(jnp.bfloat16)

    out = jax.ShapeDtypeStruct((width, columns), jnp.bfloat16)
    return pl.pallas_call(
        kernel,
        grid=(width // block,),
        in_specs=[pl.BlockSpec((total, block), lambda i: (0, i))] * pairs
        + [kept_block((total, columns))] * pairs,
        out_specs=pl.BlockSpec((block, columns), lambda i: (i, 0)),
        out_shape=out,
        compiler_params=kernel_params(),
        cost_estimate=kernel_cost(
            2 * pairs * total * width * columns, out, *rows_of, *columns_of
        ),
    )(*rows_of, *columns_of)


def seg_send(value, counts, step):
    size = lax.axis_size("seg")
    packed = jnp.concatenate([value, counts], axis=1).astype(jnp.bfloat16)
    return [
        lax.ppermute(
            packed,
            "seg",
            [(k, k + step * far) for k in range(size) if 0 <= k + step * far < size],
        )
        for far in range(1, size)
    ]


def seg_sum(arrived):
    total = sum(part.astype(jnp.float32) for part in arrived)
    return (total[:, :-1], total[:, -1:])


def column_half(weight, which):
    half = weight.shape[1] // 2
    return lax.dynamic_slice_in_dim(weight, which * half, half, 1)


def seg_gather(value):
    return lax.all_gather(value, "seg", axis=0, tiled=True)


def other_segments(gathered):
    size, here = (lax.axis_size("seg"), lax.axis_index("seg"))
    rows = gathered.shape[0] // size
    return jnp.concatenate(
        [
            lax.dynamic_slice_in_dim(gathered, lax.rem(here + k, size) * rows, rows, 0)
            for k in range(1, size)
        ],
        axis=0,
    )


def in_order(got, own):
    size, here = (lax.axis_size("seg"), lax.axis_index("seg"))
    turned = jnp.concatenate([got, own], axis=0)
    rows = own.shape[0]
    return jnp.concatenate(
        [
            lax.dynamic_slice_in_dim(turned, lax.rem(size + k - here - 1, size) * rows, rows, 0)
            for k in range(size)
        ],
        axis=0,
    )


def seg_scatter(value):
    return lax.psum_scatter(value, "seg", scatter_dimension=0, tiled=True)


def whole_columns(own, rest):
    first = lax.axis_index("grp") == 0
    return jnp.where(
        first, jnp.concatenate([own, rest], axis=1), jnp.concatenate([rest, own], axis=1)
    ).astype(jnp.float32)


def whole_sum(own, far):
    half = own.shape[1] // 2
    turned = jnp.concatenate([far[:, half:], far[:, :half]], axis=1)
    total = added(own, turned)
    first = lax.axis_index("grp") == 0
    return jnp.where(first, total, jnp.concatenate([total[:, half:], total[:, :half]], axis=1))


def times(left, right):
    return jnp.dot(left, right, preferred_element_type=jnp.float32)


def times_rows(left, right):
    return jnp.einsum("tc,dc->td", left, right, preferred_element_type=jnp.float32)


def weight_grad(rows, columns):
    return jnp.einsum("td,tc->dc", rows, columns, preferred_element_type=jnp.float32)


def root_norm(values, gain):
    return values * lax.rsqrt(jnp.mean(values * values, -1, keepdims=True) + EPS_NORM) * gain


def positive_feature(values):
    return jnp.where(values > 0, values + 1.0, jnp.exp(jnp.where(values > 0, 0.0, values)))


def feature_slope(values):
    return jnp.where(values > 0, 1.0, jnp.exp(jnp.where(values > 0, 0.0, values)))


def dot_as(left, right, dims):
    return lax.dot_general(left, right, (dims, ((), ())), preferred_element_type=jnp.float32)


ROWS_COLUMNS = ((1,), (0,))
BY_COLUMNS = ((1,), (1,))
BY_ROWS = ((0,), (0,))


def head_call(kernel, ins, outs, flops, scratch=()):
    def spec(shape, kind):
        if kind == "smem":
            return pl.BlockSpec(memory_space=pltpu.SMEM)
        if kind == "all":
            return kept_block(shape)
        if kind == "columns":
            return pl.BlockSpec((shape[0], HEAD_DIM), lambda i: (0, i))
        return pl.BlockSpec((1,) + shape[1:], lambda i: (i, 0, 0))

    heads = [s.shape[0] for s, kind in outs if kind == "heads"] + [
        s.shape[1] // HEAD_DIM for s, kind in outs if kind == "columns"
    ]
    return pl.pallas_call(
        kernel,
        grid=(heads[0],),
        in_specs=[spec(a.shape, kind) for a, kind in ins],
        out_specs=[spec(s.shape, kind) for s, kind in outs],
        out_shape=[s for s, kind in outs],
        scratch_shapes=list(scratch),
        compiler_params=kernel_params(),
        cost_estimate=kernel_cost(
            flops, *[a for a, kind in ins if kind != "smem"], *[s for s, kind in outs]
        ),
    )(*[a for a, kind in ins])


def low_feature(values):
    return positive_feature(values.astype(jnp.float32)).astype(jnp.bfloat16)


def like(shape, dtype):
    return jax.ShapeDtypeStruct(shape, dtype)


def features(key_rows, values):
    heads = key_rows.shape[1] // HEAD_DIM

    def kernel(key_ref, value_ref, contrib_ref, count_ref):
        feat_k = low_feature(key_ref[...])
        contrib_ref[0] = dot_as(feat_k, value_ref[...], BY_ROWS)
        count_ref[0] = jnp.sum(feat_k.astype(jnp.float32), axis=0, keepdims=True)

    return head_call(
        kernel,
        [(key_rows, "columns"), (values, "columns")],
        [
            (like((heads, HEAD_DIM, HEAD_DIM), jnp.float32), "heads"),
            (like((heads, 1, HEAD_DIM), jnp.float32), "heads"),
        ],
        2 * SEG_LEN * heads * HEAD_DIM**2,
    )


def reach_of(at):
    return min(SEG_LEN, (at + 2) * PIECE)


def masked_scores(query_block, keys, at, piece_first):
    scores = dot_as(query_block, keys, BY_COLUMNS) * HEAD_DIM ** (-0.5)
    rows_at = at * PIECE + lax.broadcasted_iota(jnp.int32, scores.shape, 0)
    keys_at = lax.broadcasted_iota(jnp.int32, scores.shape, 1)
    row_in = (rows_at >= piece_first) & (rows_at < piece_first + PIECE)
    key_in = (keys_at >= piece_first) & (keys_at < piece_first + PIECE)
    return jnp.where((keys_at <= rows_at) | (row_in & key_in), scores, MASKED_SCORE)


def local_flops(heads, products):
    return products * 2 * heads * HEAD_DIM * PIECE * sum(reach_of(k) for k in range(SEG_LEN // PIECE))


def local_attention(queries, key_rows, values, piece_first):
    heads = queries.shape[1] // HEAD_DIM

    def kernel(first_ref, query_ref, key_ref, value_ref, out_ref, log_ref):
        first = first_ref[0]
        for at in range(SEG_LEN // PIECE):
            rows = slice(at * PIECE, (at + 1) * PIECE)
            reach = reach_of(at)
            scores = masked_scores(query_ref[rows, :], key_ref[:reach, :], at, first)
            peak = jnp.max(scores, axis=-1, keepdims=True)
            shifted = jnp.exp(scores - peak)
            total = jnp.sum(shifted, axis=-1, keepdims=True)
            probs = (shifted * (1.0 / total)).astype(jnp.bfloat16)
            out_ref[rows, :] = dot_as(probs, value_ref[:reach, :], ROWS_COLUMNS)
            log_ref[0, rows, :] = peak + jnp.log(total)

    return head_call(
        kernel,
        [
            (piece_first[None], "smem"),
            (queries, "columns"),
            (key_rows, "columns"),
            (values, "columns"),
        ],
        [
            (like(queries.shape, jnp.float32), "columns"),
            (like((heads, SEG_LEN, 1), jnp.float32), "heads"),
        ],
        local_flops(heads, 2),
    )


def recalled(feat_q, memory, norm_mem):
    numerator = dot_as(feat_q, memory.astype(jnp.bfloat16), ROWS_COLUMNS)
    denominator = 1.0 + jnp.sum(feat_q.astype(jnp.float32) * norm_mem, axis=-1, keepdims=True)
    return (numerator / denominator, denominator)


def mixing(queries, local_out, memory, norm_mem, share):
    heads = queries.shape[1] // HEAD_DIM

    def kernel(share_ref, query_ref, local_ref, memory_ref, norm_ref, out_ref):
        part = share_ref[pl.program_id(0)]
        recall, unused = recalled(low_feature(query_ref[...]), memory_ref[0], norm_ref[0])
        out_ref[...] = (part * recall + (1.0 - part) * local_ref[...]).astype(jnp.bfloat16)

    return head_call(
        kernel,
        [
            (share, "smem"),
            (queries, "columns"),
            (local_out, "columns"),
            (memory, "heads"),
            (norm_mem, "heads"),
        ],
        [(like(queries.shape, jnp.bfloat16), "columns")],
        2 * SEG_LEN * heads * HEAD_DIM**2,
    )[0]


def memory_backward(grad_att, out_full, queries, local_out, memory, norm_mem, share):
    heads = queries.shape[1] // HEAD_DIM

    def kernel(
        share_ref,
        grad_ref,
        weight_ref,
        query_ref,
        local_ref,
        memory_ref,
        norm_ref,
        logit_ref,
        grad_local_ref,
        grad_query_ref,
        grad_memory_ref,
        grad_norm_ref,
    ):
        part = share_ref[pl.program_id(0)]
        queries_f = query_ref[...].astype(jnp.float32)
        feat_q = low_feature(query_ref[...])
        recall, denominator = recalled(feat_q, memory_ref[0], norm_ref[0])
        grad_mixed = dot_as(grad_ref[...], weight_ref[...], ROWS_COLUMNS)
        logit_ref[0] = jnp.sum(grad_mixed * (recall - local_ref[...]), axis=0, keepdims=True)
        grad_local_ref[...] = ((1.0 - part) * grad_mixed).astype(jnp.bfloat16)
        grad_scaled = part * grad_mixed / denominator
        grad_numer = grad_scaled.astype(jnp.bfloat16)
        grad_denom = -jnp.sum(grad_scaled * recall, axis=-1, keepdims=True)
        grad_feat = (
            dot_as(grad_numer, memory_ref[0].astype(jnp.bfloat16), BY_COLUMNS)
            + grad_denom * norm_ref[0]
        )
        grad_query_ref[...] = grad_feat * feature_slope(queries_f)
        grad_memory_ref[0] = dot_as(feat_q, grad_numer, BY_ROWS)
        grad_norm_ref[0] = jnp.sum(feat_q.astype(jnp.float32) * grad_denom, axis=0, keepdims=True)

    square = like((heads, HEAD_DIM, HEAD_DIM), jnp.float32)
    row = like((heads, 1, HEAD_DIM), jnp.float32)
    return head_call(
        kernel,
        [
            (share, "smem"),
            (grad_att, "all"),
            (out_full, "columns"),
            (queries, "columns"),
            (local_out, "columns"),
            (memory, "heads"),
            (norm_mem, "heads"),
        ],
        [
            (row, "heads"),
            (like(queries.shape, jnp.bfloat16), "columns"),
            (like(queries.shape, jnp.float32), "columns"),
            (square, "heads"),
            (row, "heads"),
        ],
        2 * grad_att.size * queries.shape[1] + 6 * SEG_LEN * heads * HEAD_DIM**2,
    )


def local_backward(
    queries, key_rows, values, log_totals, grad_local, grad_query, grad_contrib, grad_count, piece_first
):
    heads = queries.shape[1] // HEAD_DIM

    def kernel(
        first_ref,
        query_ref,
        key_ref,
        value_ref,
        log_ref,
        local_ref,
        memory_ref,
        contrib_ref,
        count_ref,
        query_out,
        key_out,
        value_out,
        key_sum,
        value_sum,
    ):
        first = first_ref[0]
        scale = HEAD_DIM ** (-0.5)
        keys = key_ref[...]
        contrib = contrib_ref[0].astype(jnp.bfloat16)
        grad_feat = dot_as(value_ref[...], contrib, BY_COLUMNS) + count_ref[0]
        key_sum[...] = grad_feat * feature_slope(keys.astype(jnp.float32))
        value_sum[...] = dot_as(low_feature(keys), contrib, ROWS_COLUMNS)
        for at in range(SEG_LEN // PIECE):
            rows = slice(at * PIECE, (at + 1) * PIECE)
            reach = reach_of(at)
            query_block = query_ref[rows, :]
            local_block = local_ref[rows, :]
            scores = masked_scores(query_block, key_ref[:reach, :], at, first)
            probs = jnp.exp(scores - log_ref[0, rows, :])
            grad_probs = dot_as(local_block, value_ref[:reach, :], BY_COLUMNS)
            weighed = probs * grad_probs
            mean = jnp.sum(weighed, axis=-1, keepdims=True)
            grad_scores = (weighed - probs * mean).astype(jnp.bfloat16)
            query_out[rows, :] = (
                dot_as(grad_scores, key_ref[:reach, :], ROWS_COLUMNS) * scale + memory_ref[rows, :]
            ).astype(jnp.bfloat16)
            key_sum[:reach, :] += dot_as(grad_scores, query_block, BY_ROWS) * scale
            value_sum[:reach, :] += dot_as(probs.astype(jnp.bfloat16), local_block, BY_ROWS)
        key_out[...] = key_sum[...].astype(jnp.bfloat16)
        value_out[...] = value_sum[...].astype(jnp.bfloat16)

    out = (like(queries.shape, jnp.bfloat16), "columns")
    return head_call(
        kernel,
        [
            (piece_first[None], "smem"),
            (queries, "columns"),
            (key_rows, "columns"),
            (values, "columns"),
            (log_totals, "heads"),
            (grad_local, "columns"),
            (grad_query, "columns"),
            (grad_contrib, "heads"),
            (grad_count, "heads"),
        ],
        [out, out, out],
        local_flops(heads, 5),
        [pltpu.VMEM((SEG_LEN, HEAD_DIM), jnp.float32)] * 2,
    )


def body(
    hidden_in,
    cotangent,
    piece_start,
    query_weight,
    key_weight,
    value_weight,
    out_weight,
    gate_weight,
    up_weight,
    down_weight,
    attend_gain,
    feed_gain,
    gate_logit,
):
    line = Line(attend_gain)
    group = lax.axis_index("grp")
    count, rows, width = hidden_in.shape
    micros = range(count)
    columns = query_weight.shape[1]
    half = columns // 2
    head_local = columns // HEAD_DIM
    head_turn = group * (head_local // 2)
    heads_here = lax.axis_index("tok") * head_local + lax.rem(
        jnp.arange(head_local, dtype=jnp.int32) + head_turn, head_local
    )
    placement = (
        jnp.arange(HEADS, dtype=jnp.int32)[None, :] == heads_here[:, None]
    ).astype(jnp.float32)
    gate_local = jnp.sum(placement * gate_logit[None, :], axis=1)
    share = jax.nn.sigmoid(gate_local)
    piece_first = [piece_start[m, 0] - lax.axis_index("seg") * SEG_LEN for m in micros]

    def halves(*weights):
        return jnp.concatenate([column_half(w, group) for w in weights], axis=1)

    def other_halves(*weights):
        return jnp.concatenate([column_half(w, 1 - group) for w in weights], axis=1)

    bits = tok_bits()
    here = lax.axis_index("tok")
    order = tok_order(bits)
    spots = jnp.array(order, jnp.int32) ^ here.astype(jnp.int32)
    in_turn = jnp.arange(2 * len(order), dtype=jnp.int32)

    pair_weights = (query_weight, key_weight)
    pair_mine = seg_gather(line(halves, *pair_weights))
    normed_a = line(
        lambda x: root_norm(x.astype(jnp.float32), attend_gain).astype(jnp.bfloat16), hidden_in
    )
    attend_pieces = FirstPiece(normed_a, bits)
    cot_swapped = grp_swap(cotangent)
    value_mine = seg_gather(line(halves, value_weight))
    out_mine = seg_gather(line(halves, out_weight))
    feed_mine = seg_gather(line(halves, gate_weight, up_weight))
    down_mine = seg_gather(line(halves, down_weight))
    pair_other = line(other_halves, *pair_weights)
    value_other = line(other_halves, value_weight)
    out_other = line(other_halves, out_weight)
    cot_swapped = line.hold(cot_swapped)
    attend_pieces = attend_pieces.rest(line)
    cot_pieces = FirstPiece(line.hold(cotangent), bits)
    pair_got = grp_swap(line(other_segments, pair_mine))
    gathered_a = line(
        lambda *p: place(
            p, jnp.concatenate([jnp.stack([s + m * len(order) for m in micros]) for s in spots])
        ),
        *[attend_pieces[at] for at in order],
    )
    gathered_a = [gathered_a[m * SEG_LEN : (m + 1) * SEG_LEN] for m in micros]
    value_got = grp_swap(line(other_segments, value_mine))

    def with_other(mine, got, own, pieces):
        rest = in_order(got, own)
        return tuple(
            jnp.concatenate([part[:, k * half : (k + 1) * half] for part in (mine, rest)], axis=1)
            for k in range(pieces)
        )

    def project(g, *weights):
        return tuple(
            tuple(times(g[m], w).astype(jnp.bfloat16) for m in micros) for w in weights
        )

    query_full, key_full = line(lambda *a: with_other(*a, 2), pair_mine, pair_got, pair_other)
    queries, key_rows = line(project, gathered_a, query_full, key_full)
    cot_pieces = cot_pieces.rest(line)
    cot_far = FirstPiece(cot_swapped, bits)
    (value_full,) = line(lambda *a: with_other(*a, 1), value_mine, value_got, value_other)
    (values,) = line(project, gathered_a, value_full)
    out_got = grp_swap(line(other_segments, out_mine))

    contrib, count_k = zip(*[line(features, key_rows[m], values[m]) for m in micros])
    arrived = seg_send(jnp.concatenate(contrib), jnp.concatenate(count_k), 1)
    local = [
        line(local_attention, queries[m], key_rows[m], values[m], piece_first[m]) for m in micros
    ]
    (out_full,) = line(lambda *a: with_other(*a, 1), out_mine, out_got, out_other)
    cot_far = cot_far.rest(line)
    memory, norm_mem = line(seg_sum, arrived)
    memory = [memory[m * head_local : (m + 1) * head_local] for m in micros]
    norm_mem = [norm_mem[m * head_local : (m + 1) * head_local] for m in micros]
    mixes = []
    attended = []
    for m in micros:
        mixes.append(line(mixing, queries[m], local[m][0], memory[m], norm_mem[m], share))
        attended.append(
            Scatter(*line(lambda a, w: products_cut([a], [w], spots), mixes[m], out_full))
        )
        attended[m].go_on(line)

    def after_attention(x, terms):
        resid = x.astype(jnp.float32) + total_of(terms)
        return (resid, root_norm(resid, feed_gain).astype(jnp.bfloat16))

    resid = []
    feed_pieces = []
    for m in micros:
        rows_m, normed_f = line(after_attention, hidden_in[m], attended[m].terms)
        resid.append(rows_m)
        swapped = grp_swap(normed_f[None])
        feed_pieces.append((tok_pieces(normed_f[None], bits), tok_pieces(swapped, bits)))
        if m == 0:
            feed_mine = line.hold(feed_mine)

    def interleaved(own, far):
        return [pieces[at] for at in order for pieces in (own, far)]

    feed_in = []
    products = []
    inner_act = []
    for m in micros:
        rows_m, both, inner = line(
            lambda w, *p: feed_forward(p, 0, w), feed_mine, *interleaved(*feed_pieces[m])
        )
        feed_in.append(rows_m)
        products.append(both)
        inner_act.append(inner)

    cot_all = []
    grad_products = []
    grad_normed = []

    def backward(m):
        rows_m, grads = line(
            lambda w, both, *p: feed_backward(p, m, w, both),
            down_mine,
            products[m],
            *interleaved(cot_pieces, cot_far),
        )
        cot_all.append(rows_m)
        grad_products.append(grads)

    def backward_rows(m):
        grad_normed.append(
            Scatter(
                *line(
                    lambda a, w: products_cut([a], [w], in_turn), grad_products[m], feed_mine
                )
            )
        )

    def own_and_far(terms):
        total = total_of(terms)
        half = total.shape[0] // 2
        return (total[:half], total[half:].astype(jnp.bfloat16))

    def after_feed_grad(rows_m, own, far, cot):
        unused_norm, pull = jax.vjp(root_norm, rows_m, feed_gain)
        grad_norm, gain_part = pull(added(own, far))
        grad_resid = cot.astype(jnp.float32) + grad_norm
        return (grad_resid, gain_part, grad_resid.astype(jnp.bfloat16))

    grad_parts = []
    grad_resid = []
    feed_gain_parts = []
    att_pieces = []

    def finish_rows(m):
        own, far = line(own_and_far, grad_normed[m].terms)
        grad_parts.append((own, grp_swap(far)))

    def finish_feed(m):
        rows_m, gain_part, low = line(after_feed_grad, resid[m], *grad_parts[m], cotangent[m])
        grad_resid.append(rows_m)
        feed_gain_parts.append(gain_part)
        att_pieces.append(tok_pieces(low[None], bits))

    feed_out = []

    def feed_result(m):
        feed_out.append(
            Scatter(
                *line(lambda a, w: products_cut([a], [w], in_turn), inner_act[m], down_mine)
            )
        )

    backward(0)
    backward_rows(0)
    backward(1)
    down_grad = seg_scatter(line(grad_product, cot_all, inner_act))
    grad_normed[0].go_on(line)
    backward_rows(1)
    feed_grad = seg_scatter(line(grad_product, feed_in, grad_products))
    grad_normed[1].go_on(line)
    finish_rows(0)
    feed_result(0)
    finish_rows(1)
    finish_feed(0)
    feed_result(1)
    finish_feed(1)

    grad_att = []
    mem_back = []
    for m in micros:
        grad_att.append(
            line(lambda *p: place(p, spots), *[att_pieces[m][at] for at in order])
        )
        mem_back.append(
            line(
                memory_backward,
                grad_att[m],
                out_full,
                queries[m],
                local[m][0],
                memory[m],
                norm_mem[m],
                share,
            )
        )
    logit_parts, grad_local, grad_query, grad_memory, grad_norm_mem = zip(*mem_back)
    back_arrived = seg_send(jnp.concatenate(grad_memory), jnp.concatenate(grad_norm_mem), -1)
    for m in micros:
        feed_out[m].go_on(line)
    down_grad = line.hold(down_grad)
    down_rest = grp_swap(down_grad)

    def half_grad(which, rows_of, *columns_of):
        return sum(
            weight_grad(
                a,
                jnp.concatenate(
                    [
                        c[m] if which is None else c[m][:, which * half : (which + 1) * half]
                        for c in columns_of
                    ],
                    axis=1,
                ),
            )
            for m, a in enumerate(rows_of)
        )

    mixed_rows = mixes
    out_far = grp_swap(
        line(lambda a, b: half_grad(1, a, b).astype(jnp.bfloat16), grad_att, mixed_rows)
    )
    out_grad = seg_scatter(
        line(
            lambda a, b, far: (half_grad(0, a, b) + far.astype(jnp.float32)).astype(jnp.bfloat16),
            grad_att,
            mixed_rows,
            out_far,
        )
    )
    feed_parts = []
    for m in micros:
        own, far = line(own_and_far, feed_out[m].terms)
        feed_parts.append((own, grp_swap(far)))
    grad_contrib, grad_count = line(seg_sum, back_arrived)
    feed_grad = line.hold(feed_grad)
    feed_rest = grp_swap(feed_grad)
    low_grads = []
    for m in micros:
        low_grads.append(
            line(
                local_backward,
                queries[m],
                key_rows[m],
                values[m],
                local[m][1],
                grad_local[m],
                grad_query[m],
                grad_contrib[m * head_local : (m + 1) * head_local],
                grad_count[m * head_local : (m + 1) * head_local],
                piece_first[m],
            )
        )
    query_low, key_low, value_low = zip(*low_grads)
    gathered_list = gathered_a
    query_sum = seg_scatter(
        line(lambda a, b: half_grad(None, a, b).astype(jnp.bfloat16), gathered_list, query_low)
    )
    pair_far = grp_swap(
        line(
            lambda *a: half_grad(1, *a).astype(jnp.bfloat16), gathered_list, key_low, value_low
        )
    )
    grad_normed_a = []
    for m in micros:
        grad_normed_a.append(
            Scatter(
                *line(
                    lambda a, b, c, wa, wb, wc: products_cut([a, b, c], [wa, wb, wc], spots),
                    query_low[m],
                    key_low[m],
                    value_low[m],
                    query_full,
                    key_full,
                    value_full,
                )
            )
        )
    for m in micros:
        grad_normed_a[m].go_on(line)
    out_grad = line.hold(out_grad)
    out_rest = grp_swap(out_grad)
    pair_grad = seg_scatter(
        line(
            lambda far, *a: (half_grad(0, *a) + far.astype(jnp.float32)).astype(jnp.bfloat16),
            pair_far,
            gathered_list,
            key_low,
            value_low,
        )
    )

    def after_attend_grad(x, terms, grad, gain):
        unused_norm, pull = jax.vjp(root_norm, x.astype(jnp.float32), gain)
        grad_norm, gain_part = pull(total_of(terms))
        return ((grad + grad_norm).astype(jnp.bfloat16), gain_part)

    input_rows = []
    attend_gain_parts = []
    for m in micros:
        grad_rows, gain_part = line(
            after_attend_grad, hidden_in[m], grad_normed_a[m].terms, grad_resid[m], line.token
        )
        input_rows.append(grad_rows)
        attend_gain_parts.append(gain_part)
    gate_logit_part = jnp.sum(sum(logit_parts), axis=(1, 2)) * share * (1.0 - share)
    gate_full_grad = jnp.sum(placement * gate_logit_part[:, None], axis=0)
    small = line(
        lambda a, b, c: jnp.concatenate([sum(a), sum(b), c])[None],
        attend_gain_parts,
        feed_gain_parts,
        gate_full_grad,
    )
    out_out = line(whole_columns, out_grad, out_rest)
    down_out = line(whole_columns, down_grad, down_rest)
    feed_half = gate_weight.shape[1] // 2
    gate_out, up_out = line(
        lambda a, b: tuple(
            whole_columns(*[part[:, k * feed_half : (k + 1) * feed_half] for part in (a, b)])
            for k in range(2)
        ),
        feed_grad,
        feed_rest,
    )
    query_sum = line.hold(query_sum)
    query_rest = grp_swap(query_sum)
    for axis in ("tok", "seg", "grp"):
        size = lax.axis_size(axis)
        for bit in [1 << k for k in range(size.bit_length() - 1)]:
            other = lax.ppermute(small, axis, [(k, k ^ bit) for k in range(size)])
            small = line(jnp.add, small, other)
    output_rows = [
        line(
            lambda r, own, far: (r + added(own, far)).astype(jnp.bfloat16), resid[m], *feed_parts[m]
        )
        for m in micros
    ]
    query_grad = line(whole_sum, query_sum, query_rest)
    pair_rest = grp_swap(pair_grad)
    key_grad, value_grad = line(
        lambda a, b: tuple(
            whole_columns(*[part[:, k * half : (k + 1) * half] for part in (a, b)])
            for k in range(2)
        ),
        pair_grad,
        pair_rest,
    )
    small_sums = (small[0, :width], small[0, width : 2 * width], small[0, 2 * width :])
    return (
        (jnp.stack(output_rows), jnp.stack(input_rows))
        + (query_grad, key_grad, value_grad)
        + (out_out, gate_out, up_out, down_out)
        + small_sums
    )


def solution(mesh):
    return jax.shard_map(
        body,
        mesh=mesh,
        in_specs=(
            P("grp", ("seg", "tok"), None),
            P("grp", ("seg", "tok"), None),
            P("grp", "seg"),
            P("seg", "tok"),
            P("seg", "tok"),
            P("seg", "tok"),
            P("seg", "tok"),
            P("seg", "tok"),
            P("seg", "tok"),
            P("seg", "tok"),
            P(),
            P(),
            P(),
        ),
        out_specs=(
            P("grp", ("seg", "tok"), None),
            P("grp", ("seg", "tok"), None),
            P("seg", "tok"),
            P("seg", "tok"),
            P("seg", "tok"),
            P("seg", "tok"),
            P("seg", "tok"),
            P("seg", "tok"),
            P("seg", "tok"),
            P(),
            P(),
            P(),
        ),
        check_vma=False,
    )
```

time: 2420 us -> 1160 us (0.48)
  waiting for transfers between devices: 1650 us -> 393 us
  matrix products: 455 us -> 55.4 us
  Pallas kernels: 0 us -> 393 us
  blocking collectives: 163 us -> 0 us
  starting transfers between devices: 2.76 us -> 81.3 us
  other arithmetic: 83.2 us -> 125 us
  local copies, waits for them, and re-layouts: 45.3 us -> 85.9 us
    reduce_scatter x15 -> x5, waiting for transfers between devices: 740 us -> 0.05 us  [seg_scatter(): return lax.psum_scatter(value, 'seg', scatter_dimension=0, tiled=True)]
    all_gather x15 -> x5, waiting for transfers between devices: 706 us -> 0.61 us  [seg_gather(): return lax.all_gather(value, 'seg', axis=0, tiled=True)]
    dot_general x83 -> x16, matrix products: 455 us -> 55.4 us  [the longest x10 35.6 us: weight_grad(): jnp.einsum('td,tc->dc', rows, columns, preferred_element_type=jnp.float32)]
    pallas_call x0 -> x27, Pallas kernels: none -> 393 us  [the longest x8 125 us: products_cut(): pl.pallas_call(kernel, grid_spec=pltpu.PrefetchScalarGridSpec(num_scalar_...]
    ppermute x0 -> x71, waiting for transfers between devices: none -> 393 us  [the longest x43 215 us: tok_swap(): return lax.ppermute(value, 'tok', [(k, k ^ bit) for k in range(count)])]
    psum x1 -> x0, waiting for transfers between devices: 195 us -> none  [body(): lax.psum(for_sending(shards), 'grp')]
    all_gather x8 -> x0, blocking collectives: 123 us -> none  [the longest x4 65.7 us: carried_in(): lax.all_gather(a.astype(kind), axis)]
    ppermute x0 -> x71, starting transfers between devices: none -> 80.5 us  [the longest x43 24.7 us: tok_swap(): return lax.ppermute(value, 'tok', [(k, k ^ bit) for k in range(count)])]
  transfers between devices with their start and end apart: 31 -> 81, of which waited for: 27 -> 28; matrix products, arithmetic and copies ran while one was open for 17% -> 21% of each run, Pallas kernels for 0% -> 29%
where the time goes in v1:
time: 1160 us; the launch traced here: 1150 us
  waiting for transfers between devices  393 us (34%)
  Pallas kernels  393 us (34%)
  other arithmetic  125 us (11%)
  local copies, waits for them, and re-layouts  85.9 us (7%)
  starting transfers between devices  81.3 us (7%)
  matrix products  55.4 us (5%)
  between operations  20.2 us (2%)
    ppermute x43, waiting for transfers between devices, tok_swap(): return lax.ppermute(value, 'tok', [(k, k ^ bit) for k in range(count)])  215 us
    ppermute x17, waiting for transfers between devices, grp_swap(): return lax.ppermute(value, 'grp', [(0, 1), (1, 0)])  175 us
    pallas_call x8, Pallas kernels, products_cut(): pl.pallas_call(kernel, grid_spec=pltpu.PrefetchScalarGridSpec(num_scalar_...  125 us
    pallas_call x10, Pallas kernels, head_call(): pl.pallas_call(kernel, grid=(heads[0],), in_specs=[spec(a.shape, kind) fo...  99 us
    pallas_call x4, Pallas kernels, over_pieces(): pl.pallas_call(kernel, grid=(total // block,), in_specs=[any_space()] * l...  85.9 us
    pallas_call x2, Pallas kernels, grad_product(): pl.pallas_call(kernel, grid=(width // block,), in_specs=[pl.BlockSpec((to...  68.2 us
    dot_general x10, matrix products, weight_grad(): jnp.einsum('td,tc->dc', rows, columns, preferred_element_type=jnp.float32)  35.6 us
    convert_element_type x8, other arithmetic, cut(): sum((term[half:].astype(jnp.float32) for term in terms))  27.4 us
  transfers between devices with their start and end apart: 81, of which 28 were waited for; matrix products, arithmetic and copies ran while one was open for 21% of the time, Pallas kernels for 29%

profile of v1, /device:TPU:0, one launch (start us, length us, event | category | flops | bytes accessed | tf_op | source)
XLA Modules:
  0.0 1153.9 jit_solution(14707778986505256437)
XLA Ops:
  25.6 37.7 %collective-permute-done.1.refs_1_ = bf16[2,256,2048]{2,1,0:T(8,128)(2,1)} collective-permute-done((bf16[2,256,2048]{2,1,0:T(8,128)(2,1)}, bf16[2,256,2048]{2,1,0:T(8,128)(2,1)}, u32[]{:S(2)}, u32[]{:S(2)}) %collective-permute-start.1) | collective-permute-done | bytes 2097184 | tf_op jit(solution)/shard_map/ppermute | solution.py:46
  79.9 7.2 shard_map.229
  94.4 10.9 collective-permute-done.4
  125.5 8.2 maximum_maximum_fusion.refs_5_
  157.6 4.5 collective-permute-start.8
  164.1 12.7 %shard_map.232 = (f32[1024,512]{1,0:T(8,128)}, f32[4,1024,1]{2,1,0:T(8,128)}) custom-call(s32[1]{0:T(128)} %bitcast.2.first_ref, bf16[1024,512]{1,0:T(8,128)(2,1)} %convolution_convert_fusion.5.query_ref, bf16[1024,512]{1,0:T(8,128)(2,1)} %convolution_convert_fusion.3.key_ref, bf16[1024,512]{1,0:T(8,128)(2,1)} %convolution_convert_fusion.1.value_ref), custom_call_target="tpu_custom_call" | custom-call | flops 1744830464 | bytes 5259264 | tf_op jit(solution)/shard_map/pallas_call | solution.py:455
  176.8 12.2 %shard_map.233 = (f32[1024,512]{1,0:T(8,128)}, f32[4,1024,1]{2,1,0:T(8,128)}) custom-call(s32[1]{0:T(128)} %bitcast.4.first_ref, bf16[1024,512]{1,0:T(8,128)(2,1)} %convolution_convert_fusion.4.query_ref, bf16[1024,512]{1,0:T(8,128)(2,1)} %convolution_convert_fusion.2.key_ref, bf16[1024,512]{1,0:T(8,128)(2,1)} %convolution_convert_fusion.value_ref), custom_call_target="tpu_custom_call" | custom-call | flops 1744830464 | bytes 5259264 | tf_op jit(solution)/shard_map/pallas_call | solution.py:455
  190.4 8.9 maximum_maximum_fusion.1.refs_1_.weight_ref
  206.2 7.5 shard_map.235
  225.8 7.7 shard_map.237
  239.6 19.7 %collective-permute-done.13 = bf16[256,2048]{1,0:T(8,128)(2,1)S(1)} collective-permute-done((bf16[256,2048]{1,0:T(8,128)(2,1)}, bf16[256,2048]{1,0:T(8,128)(2,1)S(1)}, u32[]{:S(2)}, u32[]{:S(2)}) %collective-permute-start.13) | collective-permute-done | bytes 1048608 | tf_op jit(solution)/shard_map/ppermute | solution.py:38
  268.8 19.0 %collective-permute-done.15.refs_1_ = bf16[1,256,2048]{2,1,0:T(8,128)(2,1)} collective-permute-done((bf16[1,256,2048]{2,1,0:T(8,128)(2,1)}, bf16[1,256,2048]{2,1,0:T(8,128)(2,1)}, u32[]{:S(2)}, u32[]{:S(2)}) %collective-permute-start.15) | collective-permute-done | bytes 1048608 | tf_op jit(solution)/shard_map/ppermute | solution.py:46
  294.1 18.0 %collective-permute-done.16.refs_2_ = bf16[1,256,2048]{2,1,0:T(8,128)(2,1)} collective-permute-done((bf16[1,256,2048]{2,1,0:T(8,128)(2,1)}, bf16[1,256,2048]{2,1,0:T(8,128)(2,1)}, u32[]{:S(2)}, u32[]{:S(2)}) %collective-permute-start.16) | collective-permute-done | bytes 1048608 | tf_op jit(solution)/shard_map/ppermute | solution.py:38
  313.6 21.0 %collective-permute-done.17.refs_3_ = bf16[1,256,2048]{2,1,0:T(8,128)(2,1)} collective-permute-done((bf16[1,256,2048]{2,1,0:T(8,128)(2,1)}, bf16[1,256,2048]{2,1,0:T(8,128)(2,1)}, u32[]{:S(2)}, u32[]{:S(2)}) %collective-permute-start.17) | collective-permute-done | bytes 1048608 | tf_op jit(solution)/shard_map/ppermute | solution.py:38
  336.6 20.3 %collective-permute-done.28.refs_2_ = bf16[1,256,2048]{2,1,0:T(8,128)(2,1)S(1)} collective-permute-done((bf16[1,256,2048]{2,1,0:T(8,128)(2,1)S(1)}, bf16[1,256,2048]{2,1,0:T(8,128)(2,1)S(1)}, u32[]{:S(2)}, u32[]{:S(2)}) %collective-permute-start.28) | collective-permute-done | bytes 1048608 | tf_op jit(solution)/shard_map/ppermute | solution.py:38
  357.6 20.3 %collective-permute-done.29.refs_3_ = bf16[1,256,2048]{2,1,0:T(8,128)(2,1)} collective-permute-done((bf16[1,256,2048]{2,1,0:T(8,128)(2,1)S(1)}, bf16[1,256,2048]{2,1,0:T(8,128)(2,1)}, u32[]{:S(2)}, u32[]{:S(2)}) %collective-permute-start.29) | collective-permute-done | bytes 1048608 | tf_op jit(solution)/shard_map/ppermute | solution.py:38
  380.4 25.0 %shard_map.238 = (bf16[2048,2048]{1,0:T(8,128)(2,1)}, bf16[2048,2048]{1,0:T(8,128)(2,1)}, bf16[2048,1024]{1,0:T(8,128)(2,1)}) custom-call(bf16[1,256,2048]{2,1,0:T(8,128)(2,1)} %bitcast.5.refs_0_, bf16[1,256,2048]{2,1,0:T(8,128)(2,1)} %collective-permute-done.15.refs_1_, bf16[1,256,2048]{2,1,0:T(8,128)(2,1)} %collective-permute-done.16.refs_2_, ...), custom_call_target="tpu_custom_call" | custom-call | flops 17179869184 | bytes 29360128 | tf_op jit(solution)/shard_map/pallas_call | solution.py:193
  405.4 25.0 %shard_map.239 = (bf16[2048,2048]{1,0:T(8,128)(2,1)}, bf16[2048,2048]{1,0:T(8,128)(2,1)}, bf16[2048,1024]{1,0:T(8,128)(2,1)}) custom-call(bf16[1,256,2048]{2,1,0:T(8,128)(2,1)} %bitcast.60, bf16[1,256,2048]{2,1,0:T(8,128)(2,1)} %copy-done.86, bf16[1,256,2048]{2,1,0:T(8,128)(2,1)} %copy-done.87, bf16[1,256,2048]{2,1,0:T(8,128)(2,1)} %collective-permute-done.29.refs_3_, ...), custom_call_target="tpu_custom_call" | custom-call | flops 17179869184 | bytes 29360128 | tf_op jit(solution)/shard_map/pallas_call | solution.py:193
  430.4 17.8 %shard_map.240 = (bf16[2048,2048]{1,0:T(8,128)(2,1)}, bf16[2048,2048]{1,0:T(8,128)(2,1)}) custom-call(bf16[2,256,2048]{2,1,0:T(8,128)(2,1)} %refs_0_.1, bf16[2,256,2048]{2,1,0:T(8,128)(2,1)} %collective-permute-done.1.refs_1_, bf16[2,256,2048]{2,1,0:T(8,128)(2,1)} %collective-permute-done.6.refs_2_, bf16[2,256,2048]{2,1,0:T(8,128)(2,1)} %collective-permute-done.10.refs_3_, ...), custom_call_target="tpu_custom_call" | custom-call | flops 8589934592 | bytes 29360128 | tf_op jit(solution)/shard_map/pallas_call | solution.py:193
  448.8 25.9 %shard_map.241 = (bf16[1024,2048]{1,0:T(8,128)(2,1)}, bf16[1024,2048]{1,0:T(8,128)(2,1)}) custom-call(s32[8]{0:T(128)} %iota.20.order_ref, bf16[2048,2048]{1,0:T(8,128)(2,1)} %get-tuple-element.943.refs_0_.refs_2_, bf16[2048,2048]{1,0:T(8,128)(2,1)} %all-gather.12.cloned.1.call-done.refs_8_.refs_1_), custom_call_target="tpu_custom_call" | custom-call | flops 17179869184 | bytes 25165824 | tf_op jit(solution)/shard_map/pallas_call | solution.py:280
  474.7 18.2 %shard_map.242 = (bf16[2048,2048]{1,0:T(8,128)(2,1)}, bf16[2048,2048]{1,0:T(8,128)(2,1)}) custom-call(bf16[2,256,2048]{2,1,0:T(8,128)(2,1)} %refs_0_.1, bf16[2,256,2048]{2,1,0:T(8,128)(2,1)} %collective-permute-done.1.refs_1_, bf16[2,256,2048]{2,1,0:T(8,128)(2,1)} %collective-permute-done.6.refs_2_, bf16[2,256,2048]{2,1,0:T(8,128)(2,1)} %collective-permute-done.10.refs_3_, ...), custom_call_target="tpu_custom_call" | custom-call | flops 8589934592 | bytes 29360128 | tf_op jit(solution)/shard_map/pallas_call | solution.py:193
  493.0 23.9 %shard_map.243 = bf16[2048,1024]{1,0:T(8,128)(2,1)} custom-call(bf16[2048,2048]{1,0:T(8,128)(2,1)} %get-tuple-element.919.refs_0_, bf16[2048,2048]{1,0:T(8,128)(2,1)} %get-tuple-element.920.refs_1_, bf16[2048,1024]{1,0:T(8,128)(2,1)} %get-tuple-element.956.refs_2_.refs_0_, bf16[2048,1024]{1,0:T(8,128)(2,1)} %get-tuple-element.981.refs_3_.refs_0_), custom_call_target="tpu_custom_call" | custom-call | flops 17179869184 | bytes 29360128 | tf_op jit(solution)/shard_map/pallas_call | solution.py:324
  517.0 4.4 add_convert_fusion.6
  522.0 25.8 %shard_map.244 = (bf16[1024,2048]{1,0:T(8,128)(2,1)}, bf16[1024,2048]{1,0:T(8,128)(2,1)}) custom-call(s32[8]{0:T(128)} %iota.21.order_ref, bf16[2048,2048]{1,0:T(8,128)(2,1)} %get-tuple-element.944.refs_0_.refs_3_, bf16[2048,2048]{1,0:T(8,128)(2,1)} %all-gather.12.cloned.1.call-done.refs_8_.refs_1_), custom_call_target="tpu_custom_call" | custom-call | flops 17179869184 | bytes 25165824 | tf_op jit(solution)/shard_map/pallas_call | solution.py:280
  548.2 44.3 %shard_map.245 = bf16[2048,2048]{1,0:T(8,128)(2,1)} custom-call(bf16[2048,2048]{1,0:T(8,128)(2,1)} %get-tuple-element.941.refs_0_, bf16[2048,2048]{1,0:T(8,128)(2,1)} %get-tuple-element.942.refs_1_, bf16[2048,2048]{1,0:T(8,128)(2,1)} %get-tuple-element.943.refs_0_.refs_2_, bf16[2048,2048]{1,0:T(8,128)(2,1)} %get-tuple-element.944.refs_0_.refs_3_), custom_call_target="tpu_custom_call" | custom-call | flops 34359738368 | bytes 41943040 | tf_op jit(solution)/shard_map/pallas_call | solution.py:324
  606.6 34.6 %collective-permute-done.35 = bf16[512,2048]{1,0:T(8,128)(2,1)S(1)} collective-permute-done((bf16[512,2048]{1,0:T(8,128)(2,1)}, bf16[512,2048]{1,0:T(8,128)(2,1)S(1)}, u32[]{:S(2)}, u32[]{:S(2)}) %collective-permute-start.35) | collective-permute-done | bytes 2097184 | tf_op jit(solution)/shard_map/ppermute | solution.py:38
  647.3 15.9 %shard_map.246 = (bf16[1024,2048]{1,0:T(8,128)(2,1)}, bf16[1024,2048]{1,0:T(8,128)(2,1)}) custom-call(s32[8]{0:T(128)} %iota.19.order_ref, bf16[2048,1024]{1,0:T(8,128)(2,1)} %get-tuple-element.956.refs_2_.refs_0_, bf16[2048,1024]{1,0:T(8,128)(2,1)} %all-gather.14.cloned.1.call-done.refs_8_.refs_1_), custom_call_target="tpu_custom_call" | custom-call | flops 8589934592 | bytes 16777216 | tf_op jit(solution)/shard_map/pallas_call | solution.py:280
  665.0 20.5 %collective-permute-done.38 = bf16[512,2048]{1,0:T(8,128)(2,1)} collective-permute-done((bf16[512,2048]{1,0:T(8,128)(2,1)}, bf16[512,2048]{1,0:T(8,128)(2,1)}, u32[]{:S(2)}, u32[]{:S(2)}) %collective-permute-start.38) | collective-permute-done | bytes 2097184 | tf_op jit(solution)/shard_map/ppermute | solution.py:38
  699.3 15.8 %shard_map.247 = (bf16[1024,2048]{1,0:T(8,128)(2,1)}, bf16[1024,2048]{1,0:T(8,128)(2,1)}) custom-call(s32[8]{0:T(128)} %iota.22.order_ref, bf16[2048,1024]{1,0:T(8,128)(2,1)} %get-tuple-element.981.refs_3_.refs_0_, bf16[2048,1024]{1,0:T(8,128)(2,1)} %all-gather.14.cloned.1.call-done.refs_8_.refs_1_), custom_call_target="tpu_custom_call" | custom-call | flops 8589934592 | bytes 16777216 | tf_op jit(solution)/shard_map/pallas_call | solution.py:280
  725.8 24.0 %collective-permute-done.41.refs_1_ = bf16[1,256,2048]{2,1,0:T(8,128)(2,1)} collective-permute-done((bf16[1,256,2048]{2,1,0:T(8,128)(2,1)}, bf16[1,256,2048]{2,1,0:T(8,128)(2,1)}, u32[]{:S(2)}, u32[]{:S(2)}) %collective-permute-start.41) | collective-permute-done | bytes 1048608 | tf_op jit(solution)/shard_map/ppermute | solution.py:38
  753.8 10.9 shard_map.249
  769.7 11.0 shard_map.251
  780.8 4.6 add_convert_fusion.4
  812.8 9.3 collective-permute-done.49
  828.5 15.4 %collective-permute-done.62 = bf16[512,1024]{1,0:T(8,128)(2,1)} collective-permute-done((bf16[512,1024]{1,0:T(8,128)(2,1)S(1)}, bf16[512,1024]{1,0:T(8,128)(2,1)}, u32[]{:S(2)}, u32[]{:S(2)}) %collective-permute-start.62) | collective-permute-done | bytes 1048608 | tf_op jit(solution)/shard_map/ppermute | solution.py:46
  853.6 25.1 %collective-permute-done.51 = bf16[512,2048]{1,0:T(8,128)(2,1)} collective-permute-done((bf16[512,2048]{1,0:T(8,128)(2,1)}, bf16[512,2048]{1,0:T(8,128)(2,1)}, u32[]{:S(2)}, u32[]{:S(2)}) %collective-permute-start.51) | collective-permute-done | bytes 2097184 | tf_op jit(solution)/shard_map/ppermute | solution.py:38
  888.8 17.7 %shard_map.252 = (bf16[1024,512]{1,0:T(8,128)(2,1)}, bf16[1024,512]{1,0:T(8,128)(2,1)}, bf16[1024,512]{1,0:T(8,128)(2,1)}) custom-call(s32[1]{0:T(128)} %bitcast.14.first_ref, bf16[1024,512]{1,0:T(8,128)(2,1)} %convolution_convert_fusion.5.query_ref, bf16[1024,512]{1,0:T(8,128)(2,1)} %convolution_convert_fusion.3.key_ref, ...), custom_call_target="tpu_custom_call" | custom-call | flops 4362076160 | bytes 9717760 | tf_op jit(solution)/shard_map/pallas_call | solution.py:455
  906.5 17.5 %shard_map.253 = (bf16[1024,512]{1,0:T(8,128)(2,1)}, bf16[1024,512]{1,0:T(8,128)(2,1)}, bf16[1024,512]{1,0:T(8,128)(2,1)}) custom-call(s32[1]{0:T(128)} %bitcast.15.first_ref, bf16[1024,512]{1,0:T(8,128)(2,1)} %convolution_convert_fusion.4.query_ref, bf16[1024,512]{1,0:T(8,128)(2,1)} %convolution_convert_fusion.2.key_ref, ...), custom_call_target="tpu_custom_call" | custom-call | flops 4362076160 | bytes 9717760 | tf_op jit(solution)/shard_map/pallas_call | solution.py:455
  924.1 5.0 fusion.77
  935.2 4.7 fusion.23
  943.7 13.2 %shard_map.254 = (bf16[512,2048]{1,0:T(8,128)(2,1)}, bf16[512,2048]{1,0:T(8,128)(2,1)}) custom-call(s32[4]{0:T(128)} %copy-done.79, bf16[1024,512]{1,0:T(8,128)(2,1)} %get-tuple-element.1152.refs_0_, bf16[1024,512]{1,0:T(8,128)(2,1)} %get-tuple-element.1190.refs_1_, bf16[1024,512]{1,0:T(8,128)(2,1)} %get-tuple-element.1191.refs_2_, ...), custom_call_target="tpu_custom_call" | custom-call | flops 6442450944 | bytes 13631488 | tf_op jit(solution)/shard_map/pallas_call | solution.py:280
  956.9 13.1 %shard_map.255 = (bf16[512,2048]{1,0:T(8,128)(2,1)}, bf16[512,2048]{1,0:T(8,128)(2,1)}) custom-call(s32[4]{0:T(128)} %copy-done.79, bf16[1024,512]{1,0:T(8,128)(2,1)} %get-tuple-element.1164.refs_0_, bf16[1024,512]{1,0:T(8,128)(2,1)} %get-tuple-element.1193.refs_1_, bf16[1024,512]{1,0:T(8,128)(2,1)} %get-tuple-element.1194.refs_2_, ...), custom_call_target="tpu_custom_call" | custom-call | flops 6442450944 | bytes 13631488 | tf_op jit(solution)/shard_map/pallas_call | solution.py:280
  991.4 32.3 %collective-permute-done.58 = bf16[2048,512]{1,0:T(8,128)(2,1)} collective-permute-done((bf16[2048,512]{1,0:T(8,128)(2,1)}, bf16[2048,512]{1,0:T(8,128)(2,1)}, u32[]{:S(2)}, u32[]{:S(2)}) %collective-permute-start.58) | collective-permute-done | bytes 2097184 | tf_op jit(solution)/shard_map/ppermute | solution.py:46
  1026.6 4.9 fusion.34
  1039.3 28.4 %collective-permute-done.61 = bf16[512,2048]{1,0:T(8,128)(2,1)} collective-permute-done((bf16[512,2048]{1,0:T(8,128)(2,1)}, bf16[512,2048]{1,0:T(8,128)(2,1)}, u32[]{:S(2)}, u32[]{:S(2)}) %collective-permute-start.61) | collective-permute-done | bytes 2097184 | tf_op jit(solution)/shard_map/ppermute | solution.py:46
  1089.7 14.6 %collective-permute-start.68 = (f32[1,4112]{1,0:T(1,128)S(1)}, f32[1,4112]{1,0:T(1,128)S(1)}, u32[]{:S(2)}, u32[]{:S(2)}) collective-permute-start(f32[1,4112]{1,0:T(1,128)S(1)} %add.445), channel_id=1, source_target_pairs={{0,4},{4,0},{8,12},{12,8},{1,5},{5,1},{9,13},{13,9},{2,6},{6,2},{1... | collective-permute-start | bytes 49352 | tf_op jit(solution)/shard_map/ppermute | solution.py:1062
  1119.9 10.7 collective-permute-done.64
  1133.6 10.8 collective-permute-done.65
  (544 shorter events, 327.6 us)
Async XLA Ops:
  7.2 57.9 %all-gather.6.cloned.1.call-start = ((), (), s32[]{:S(2)}) async-start(), calls=%async_computation.5 | async-start | bytes 2621440 | tf_op jit(solution)/shard_map/all_gather | solution.py:362
  9.3 78.3 %all-gather.8.cloned.1.call-start = ((), (), s32[]{:S(2)}) async-start(), calls=%async_computation.6 | async-start | bytes 1310720 | tf_op jit(solution)/shard_map/all_gather | solution.py:362
  14.3 126.1 %all-gather.10.cloned.1.call-start = ((), (), s32[]{:S(2)}) async-start(), calls=%async_computation.7 | async-start | bytes 1310720 | tf_op jit(solution)/shard_map/all_gather | solution.py:362
  14.3 49.0 %collective-permute-start.1 = (bf16[2,256,2048]{2,1,0:T(8,128)(2,1)}, bf16[2,256,2048]{2,1,0:T(8,128)(2,1)}, u32[]{:S(2)}, u32[]{:S(2)}) collective-permute-start(bf16[2,256,2048]{2,1,0:T(8,128)(2,1)} %refs_0_.1), channel_id=1, source_target_pairs={{0,16},{16,0},{1,17},{17,1},{2,18},{18,2},{3,19},{19,3},{4,20},{20... | collective-permute-start | bytes 6291464 | tf_op jit(solution)/shard_map/ppermute | solution.py:46
  17.4 47.4 %collective-permute-start = (bf16[2,256,2048]{2,1,0:T(8,128)(2,1)}, bf16[2,256,2048]{2,1,0:T(8,128)(2,1)}, u32[]{:S(2)}, u32[]{:S(2)}) collective-permute-start(bf16[2,256,2048]{2,1,0:T(8,128)(2,1)} %fusion.2.refs_0_), channel_id=1, source_target_pairs={{0,2},{1,3},{2,0},{3,1},{4,6},{5,7},{6,4},{7,5},{8,10},{9,11},{10,... | collective-permute-start | bytes 6291464 | tf_op jit(solution)/shard_map/ppermute | solution.py:38
  18.9 59.7 %collective-permute-start.2 = (bf16[2,256,2048]{2,1,0:T(8,128)(2,1)}, bf16[2,256,2048]{2,1,0:T(8,128)(2,1)}, u32[]{:S(2)}, u32[]{:S(2)}) collective-permute-start(bf16[2,256,2048]{2,1,0:T(8,128)(2,1)} %fusion.2.refs_0_), channel_id=1, source_target_pairs={{0,1},{1,0},{2,3},{3,2},{4,5},{5,4},{6,7},{7,6},{8,9},{9,8},{10,11... | collective-permute-start | bytes 6291464 | tf_op jit(solution)/shard_map/ppermute | solution.py:38
  19.6 269.7 %all-gather.12.cloned.1.call-start = ((), (), s32[]{:S(2)}) async-start(), calls=%async_computation.8 | async-start | bytes 10485760 | tf_op jit(solution)/shard_map/all_gather | solution.py:362
  64.8 365.6 %all-gather.14.cloned.1.call-start = ((), (), s32[]{:S(2)}) async-start(), calls=%async_computation.9 | async-start | bytes 5242880 | tf_op jit(solution)/shard_map/all_gather | solution.py:362
  76.5 48.8 %collective-permute-start.6 = (bf16[2,256,2048]{2,1,0:T(8,128)(2,1)}, bf16[2,256,2048]{2,1,0:T(8,128)(2,1)}, u32[]{:S(2)}, u32[]{:S(2)}) collective-permute-start(bf16[2,256,2048]{2,1,0:T(8,128)(2,1)} %refs_0_.1), channel_id=1, source_target_pairs={{0,2},{1,3},{2,0},{3,1},{4,6},{5,7},{6,4},{7,5},{8,10},{9,11},{10,... | collective-permute-start | bytes 6291464 | tf_op jit(solution)/shard_map/ppermute | solution.py:38
  78.2 121.1 %collective-permute-start.10 = (bf16[2,256,2048]{2,1,0:T(8,128)(2,1)}, bf16[2,256,2048]{2,1,0:T(8,128)(2,1)}, u32[]{:S(2)}, u32[]{:S(2)}) collective-permute-start(bf16[2,256,2048]{2,1,0:T(8,128)(2,1)} %collective-permute-done.1.refs_1_), channel_id=1, source_target_pairs={{0,2},{1,3},{2,0},{3,1},{4,6},{5,7},{6,4},{7,5},{8,10},{9,11},{10,... | collective-permute-start | bytes 6291464 | tf_op jit(solution)/shard_map/ppermute | solution.py:38
  141.6 47.3 %collective-permute-start.11 = (bf16[1536,256]{1,0:T(8,128)(2,1)S(1)}, bf16[1536,256]{1,0:T(8,128)(2,1)}, u32[]{:S(2)}, u32[]{:S(2)}) collective-permute-start(bf16[1536,256]{1,0:T(8,128)(2,1)S(1)} %pad_maximum_fusion.8), channel_id=1, source_target_pairs={{0,16},{16,0},{1,17},{17,1},{2,18},{18,2},{3,19},{19,3},{4,20},{20... | collective-permute-start | bytes 2359304 | tf_op jit(solution)/shard_map/ppermute | solution.py:46
  154.1 45.2 %collective-permute-start.7 = (bf16[8,129,128]{2,1,0:T(8,128)(2,1)S(1)}, bf16[8,129,128]{2,1,0:T(8,128)(2,1)S(1)}, u32[]{:S(2)}, u32[]{:S(2)}) collective-permute-start(bf16[8,129,128]{2,1,0:T(8,128)(2,1)S(1)} %maximum_maximum_fusion.2), channel_id=1, source_target_pairs={{0,4},{4,8},{8,12},{1,5},{5,9},{9,13},{2,6},{6,10},{10,14},{3,7},{... | collective-permute-start | bytes 792584 | tf_op jit(solution)/shard_map/ppermute | solution.py:342
  157.6 41.7 %collective-permute-start.8 = (bf16[8,129,128]{2,1,0:T(8,128)(2,1)S(1)}, bf16[8,129,128]{2,1,0:T(8,128)(2,1)S(1)}, u32[]{:S(2)}, u32[]{:S(2)}) collective-permute-start(bf16[8,129,128]{2,1,0:T(8,128)(2,1)S(1)} %maximum_maximum_fusion.2), channel_id=1, source_target_pairs={{0,8},{4,12},{1,9},{5,13},{2,10},{6,14},{3,11},{7,15},{16,24},{20,... | collective-permute-start | bytes 792584 | tf_op jit(solution)/shard_map/ppermute | solution.py:342
  264.8 524.9 %reduce-scatter.6.cloned.1.call-start = ((), (), s32[]{:S(2)}) async-start(), calls=%async_computation.10 | async-start | bytes 5242880 | tf_op jit(solution)/shard_map/reduce_scatter | solution.py:391
  267.2 44.9 %collective-permute-start.16 = (bf16[1,256,2048]{2,1,0:T(8,128)(2,1)}, bf16[1,256,2048]{2,1,0:T(8,128)(2,1)}, u32[]{:S(2)}, u32[]{:S(2)}) collective-permute-start(bf16[1,256,2048]{2,1,0:T(8,128)(2,1)} %bitcast.5.refs_0_), channel_id=1, source_target_pairs={{0,2},{1,3},{2,0},{3,1},{4,6},{5,7},{6,4},{7,5},{8,10},{9,11},{10,... | collective-permute-start | bytes 3145736 | tf_op jit(solution)/shard_map/ppermute | solution.py:38
  267.7 44.4 %collective-permute-start.18 = (bf16[1,256,2048]{2,1,0:T(8,128)(2,1)}, bf16[1,256,2048]{2,1,0:T(8,128)(2,1)}, u32[]{:S(2)}, u32[]{:S(2)}) collective-permute-start(bf16[1,256,2048]{2,1,0:T(8,128)(2,1)} %bitcast.5.refs_0_), channel_id=1, source_target_pairs={{0,1},{1,0},{2,3},{3,2},{4,5},{5,4},{6,7},{7,6},{8,9},{9,8},{10,11... | collective-permute-start | bytes 3145736 | tf_op jit(solution)/shard_map/ppermute | solution.py:38
  287.8 46.8 %collective-permute-start.17 = (bf16[1,256,2048]{2,1,0:T(8,128)(2,1)}, bf16[1,256,2048]{2,1,0:T(8,128)(2,1)}, u32[]{:S(2)}, u32[]{:S(2)}) collective-permute-start(bf16[1,256,2048]{2,1,0:T(8,128)(2,1)} %collective-permute-done.15.refs_1_), channel_id=1, source_target_pairs={{0,2},{1,3},{2,0},{3,1},{4,6},{5,7},{6,4},{7,5},{8,10},{9,11},{10,... | collective-permute-start | bytes 3145736 | tf_op jit(solution)/shard_map/ppermute | solution.py:38
  289.3 45.3 %collective-permute-start.19 = (bf16[1,256,2048]{2,1,0:T(8,128)(2,1)}, bf16[1,256,2048]{2,1,0:T(8,128)(2,1)}, u32[]{:S(2)}, u32[]{:S(2)}) collective-permute-start(bf16[1,256,2048]{2,1,0:T(8,128)(2,1)} %collective-permute-done.15.refs_1_), channel_id=1, source_target_pairs={{0,1},{1,0},{2,3},{3,2},{4,5},{5,4},{6,7},{7,6},{8,9},{9,8},{10,11... | collective-permute-start | bytes 3145736 | tf_op jit(solution)/shard_map/ppermute | solution.py:38
  292.5 42.6 %collective-permute-start.27 = (bf16[1,256,2048]{2,1,0:T(8,128)(2,1)S(1)}, bf16[1,256,2048]{2,1,0:T(8,128)(2,1)S(1)}, u32[]{:S(2)}, u32[]{:S(2)}) collective-permute-start(bf16[1,256,2048]{2,1,0:T(8,128)(2,1)S(1)} %bitcast.57), channel_id=1, source_target_pairs={{0,16},{16,0},{1,17},{17,1},{2,18},{18,2},{3,19},{19,3},{4,20},{20... | collective-permute-start | bytes 3145736 | tf_op jit(solution)/shard_map/ppermute | solution.py:46
  312.1 44.8 %collective-permute-start.28 = (bf16[1,256,2048]{2,1,0:T(8,128)(2,1)S(1)}, bf16[1,256,2048]{2,1,0:T(8,128)(2,1)S(1)}, u32[]{:S(2)}, u32[]{:S(2)}) collective-permute-start(bf16[1,256,2048]{2,1,0:T(8,128)(2,1)S(1)} %bitcast.58), channel_id=1, source_target_pairs={{0,2},{1,3},{2,0},{3,1},{4,6},{5,7},{6,4},{7,5},{8,10},{9,11},{10,... | collective-permute-start | bytes 3145736 | tf_op jit(solution)/shard_map/ppermute | solution.py:38
  335.1 42.8 %collective-permute-start.29 = (bf16[1,256,2048]{2,1,0:T(8,128)(2,1)S(1)}, bf16[1,256,2048]{2,1,0:T(8,128)(2,1)}, u32[]{:S(2)}, u32[]{:S(2)}) collective-permute-start(bf16[1,256,2048]{2,1,0:T(8,128)(2,1)S(1)} %collective-permute-done.27.refs_1_), channel_id=1, source_target_pairs={{0,2},{1,3},{2,0},{3,1},{4,6},{5,7},{6,4},{7,5},{8,10},{9,11},{10,... | collective-permute-start | bytes 3145736 | tf_op jit(solution)/shard_map/ppermute | solution.py:38
  336.6 41.3 %collective-permute-start.31 = (bf16[1,256,2048]{2,1,0:T(8,128)(2,1)S(1)}, bf16[1,256,2048]{2,1,0:T(8,128)(2,1)S(1)}, u32[]{:S(2)}, u32[]{:S(2)}) collective-permute-start(bf16[1,256,2048]{2,1,0:T(8,128)(2,1)S(1)} %collective-permute-done.27.refs_1_), channel_id=1, source_target_pairs={{0,1},{1,0},{2,3},{3,2},{4,5},{5,4},{6,7},{7,6},{8,9},{9,8},{10,11... | collective-permute-start | bytes 3145736 | tf_op jit(solution)/shard_map/ppermute | solution.py:38
  357.0 73.4 %collective-permute-start.23 = (bf16[2,256,2048]{2,1,0:T(8,128)(2,1)}, bf16[2,256,2048]{2,1,0:T(8,128)(2,1)}, u32[]{:S(2)}, u32[]{:S(2)}) collective-permute-start(bf16[2,256,2048]{2,1,0:T(8,128)(2,1)} %refs_0_.1), channel_id=1, source_target_pairs={{0,1},{1,0},{2,3},{3,2},{4,5},{5,4},{6,7},{7,6},{8,9},{9,8},{10,11... | collective-permute-start | bytes 6291464 | tf_op jit(solution)/shard_map/ppermute | solution.py:38
  357.5 72.9 %collective-permute-start.24 = (bf16[2,256,2048]{2,1,0:T(8,128)(2,1)}, bf16[2,256,2048]{2,1,0:T(8,128)(2,1)}, u32[]{:S(2)}, u32[]{:S(2)}) collective-permute-start(bf16[2,256,2048]{2,1,0:T(8,128)(2,1)} %collective-permute-done.1.refs_1_), channel_id=1, source_target_pairs={{0,1},{1,0},{2,3},{3,2},{4,5},{5,4},{6,7},{7,6},{8,9},{9,8},{10,11... | collective-permute-start | bytes 6291464 | tf_op jit(solution)/shard_map/ppermute | solution.py:38
  377.9 52.5 %collective-permute-start.25 = (bf16[2,256,2048]{2,1,0:T(8,128)(2,1)}, bf16[2,256,2048]{2,1,0:T(8,128)(2,1)}, u32[]{:S(2)}, u32[]{:S(2)}) collective-permute-start(bf16[2,256,2048]{2,1,0:T(8,128)(2,1)} %collective-permute-done.6.refs_2_), channel_id=1, source_target_pairs={{0,1},{1,0},{2,3},{3,2},{4,5},{5,4},{6,7},{7,6},{8,9},{9,8},{10,11... | collective-permute-start | bytes 6291464 | tf_op jit(solution)/shard_map/ppermute | solution.py:38
  377.9 52.5 %collective-permute-start.26 = (bf16[2,256,2048]{2,1,0:T(8,128)(2,1)}, bf16[2,256,2048]{2,1,0:T(8,128)(2,1)}, u32[]{:S(2)}, u32[]{:S(2)}) collective-permute-start(bf16[2,256,2048]{2,1,0:T(8,128)(2,1)} %collective-permute-done.10.refs_3_), channel_id=1, source_target_pairs={{0,1},{1,0},{2,3},{3,2},{4,5},{5,4},{6,7},{7,6},{8,9},{9,8},{10,11... | collective-permute-start | bytes 6291464 | tf_op jit(solution)/shard_map/ppermute | solution.py:38
  516.9 371.9 %reduce-scatter.8.cloned.1.call-start = ((), (), s32[]{:S(2)}) async-start(), calls=%async_computation.11 | async-start | bytes 10485760 | tf_op jit(solution)/shard_map/reduce_scatter | solution.py:391
  547.7 46.4 %collective-permute-start.36 = (bf16[1024,2048]{1,0:T(8,128)(2,1)}, bf16[1024,2048]{1,0:T(8,128)(2,1)}, u32[]{:S(2)}, u32[]{:S(2)}) collective-permute-start(bf16[1024,2048]{1,0:T(8,128)(2,1)} %get-tuple-element.937), channel_id=1, source_target_pairs={{0,1},{1,0},{2,3},{3,2},{4,5},{5,4},{6,7},{7,6},{8,9},{9,8},{10,11... | collective-permute-start | bytes 12582920 | tf_op jit(solution)/shard_map/ppermute | solution.py:38
  592.5 399.0 %reduce-scatter.10.cloned.1.call-start = ((), (), s32[]{:S(2)}) async-start(), calls=%async_computation.12 | async-start | bytes 1310720 | tf_op jit(solution)/shard_map/reduce_scatter | solution.py:391
  592.5 48.8 %collective-permute-start.35 = (bf16[512,2048]{1,0:T(8,128)(2,1)}, bf16[512,2048]{1,0:T(8,128)(2,1)S(1)}, u32[]{:S(2)}, u32[]{:S(2)}) collective-permute-start(bf16[512,2048]{1,0:T(8,128)(2,1)} %add_convert_fusion.6), channel_id=1, source_target_pairs={{0,2},{1,3},{2,0},{3,1},{4,6},{5,7},{6,4},{7,5},{8,10},{9,11},{10,... | collective-permute-start | bytes 6291464 | tf_op jit(solution)/shard_map/ppermute | solution.py:38
  598.5 86.9 %collective-permute-start.38 = (bf16[512,2048]{1,0:T(8,128)(2,1)}, bf16[512,2048]{1,0:T(8,128)(2,1)}, u32[]{:S(2)}, u32[]{:S(2)}) collective-permute-start(bf16[512,2048]{1,0:T(8,128)(2,1)} %add_convert_fusion.5), channel_id=1, source_target_pairs={{0,2},{1,3},{2,0},{3,1},{4,6},{5,7},{6,4},{7,5},{8,10},{9,11},{10,... | collective-permute-start | bytes 6291464 | tf_op jit(solution)/shard_map/ppermute | solution.py:38
  645.2 45.5 %collective-permute-start.40 = (bf16[256,2048]{1,0:T(8,128)(2,1)}, bf16[256,2048]{1,0:T(8,128)(2,1)S(1)}, u32[]{:S(2)}, u32[]{:S(2)}) collective-permute-start(bf16[256,2048]{1,0:T(8,128)(2,1)} %slice.433), channel_id=1, source_target_pairs={{0,16},{16,0},{1,17},{17,1},{2,18},{18,2},{3,19},{19,3},{4,20},{20... | collective-permute-start | bytes 3145736 | tf_op jit(solution)/shard_map/ppermute | solution.py:46
  663.2 117.6 %collective-permute-start.37 = (bf16[1024,2048]{1,0:T(8,128)(2,1)}, bf16[1024,2048]{1,0:T(8,128)(2,1)}, u32[]{:S(2)}, u32[]{:S(2)}) collective-permute-start(bf16[1024,2048]{1,0:T(8,128)(2,1)} %get-tuple-element.962), channel_id=1, source_target_pairs={{0,1},{1,0},{2,3},{3,2},{4,5},{5,4},{6,7},{7,6},{8,9},{9,8},{10,11... | collective-permute-start | bytes 12582920 | tf_op jit(solution)/shard_map/ppermute | solution.py:38
  715.1 70.8 %collective-permute-start.48 = (bf16[1024,2048]{1,0:T(8,128)(2,1)}, bf16[1024,2048]{1,0:T(8,128)(2,1)}, u32[]{:S(2)}, u32[]{:S(2)}) collective-permute-start(bf16[1024,2048]{1,0:T(8,128)(2,1)} %get-tuple-element.1043), channel_id=1, source_target_pairs={{0,1},{1,0},{2,3},{3,2},{4,5},{5,4},{6,7},{7,6},{8,9},{9,8},{10,11... | collective-permute-start | bytes 12582920 | tf_op jit(solution)/shard_map/ppermute | solution.py:38
  725.3 39.5 %collective-permute-start.42 = (bf16[1,256,2048]{2,1,0:T(8,128)(2,1)}, bf16[1,256,2048]{2,1,0:T(8,128)(2,1)S(1)}, u32[]{:S(2)}, u32[]{:S(2)}) collective-permute-start(bf16[1,256,2048]{2,1,0:T(8,128)(2,1)} %bitcast.10.refs_0_), channel_id=1, source_target_pairs={{0,1},{1,0},{2,3},{3,2},{4,5},{5,4},{6,7},{7,6},{8,9},{9,8},{10,11... | collective-permute-start | bytes 3145736 | tf_op jit(solution)/shard_map/ppermute | solution.py:38
  785.4 59.8 %collective-permute-start.47 = (bf16[512,2048]{1,0:T(8,128)(2,1)}, bf16[512,2048]{1,0:T(8,128)(2,1)}, u32[]{:S(2)}, u32[]{:S(2)}) collective-permute-start(bf16[512,2048]{1,0:T(8,128)(2,1)} %add_convert_fusion.4), channel_id=1, source_target_pairs={{0,2},{1,3},{2,0},{3,1},{4,6},{5,7},{6,4},{7,5},{8,10},{9,11},{10,... | collective-permute-start | bytes 6291464 | tf_op jit(solution)/shard_map/ppermute | solution.py:38
  805.7 73.0 %collective-permute-start.51 = (bf16[512,2048]{1,0:T(8,128)(2,1)}, bf16[512,2048]{1,0:T(8,128)(2,1)}, u32[]{:S(2)}, u32[]{:S(2)}) collective-permute-start(bf16[512,2048]{1,0:T(8,128)(2,1)} %add_convert_fusion.3), channel_id=1, source_target_pairs={{0,2},{1,3},{2,0},{3,1},{4,6},{5,7},{6,4},{7,5},{8,10},{9,11},{10,... | collective-permute-start | bytes 6291464 | tf_op jit(solution)/shard_map/ppermute | solution.py:38
  808.1 76.5 %collective-permute-start.53 = (bf16[8,129,128]{2,1,0:T(8,128)(2,1)S(1)}, bf16[8,129,128]{2,1,0:T(8,128)(2,1)}, u32[]{:S(2)}, u32[]{:S(2)}) collective-permute-start(bf16[8,129,128]{2,1,0:T(8,128)(2,1)S(1)} %maximum_maximum_fusion.3), channel_id=1, source_target_pairs={{4,0},{8,4},{12,8},{5,1},{9,5},{13,9},{6,2},{10,6},{14,10},{7,3},{... | collective-permute-start | bytes 792584 | tf_op jit(solution)/shard_map/ppermute | solution.py:342
  822.1 62.5 %collective-permute-start.54 = (bf16[8,129,128]{2,1,0:T(8,128)(2,1)S(1)}, bf16[8,129,128]{2,1,0:T(8,128)(2,1)}, u32[]{:S(2)}, u32[]{:S(2)}) collective-permute-start(bf16[8,129,128]{2,1,0:T(8,128)(2,1)S(1)} %maximum_maximum_fusion.3), channel_id=1, source_target_pairs={{8,0},{12,4},{9,1},{13,5},{10,2},{14,6},{11,3},{15,7},{24,16},{28,... | collective-permute-start | bytes 792584 | tf_op jit(solution)/shard_map/ppermute | solution.py:342
  843.9 40.7 %collective-permute-start.55 = (bf16[8,129,128]{2,1,0:T(8,128)(2,1)S(1)}, bf16[8,129,128]{2,1,0:T(8,128)(2,1)}, u32[]{:S(2)}, u32[]{:S(2)}) collective-permute-start(bf16[8,129,128]{2,1,0:T(8,128)(2,1)S(1)} %maximum_maximum_fusion.3), channel_id=1, source_target_pairs={{12,0},{13,1},{14,2},{15,3},{28,16},{29,17},{30,18},{31,19}} | collective-permute-start | bytes 792584 | tf_op jit(solution)/shard_map/ppermute | solution.py:342
  845.2 272.0 %reduce-scatter.12.cloned.1.call-start = ((), (), s32[]{:S(2)}) async-start(), calls=%async_computation.13 | async-start | bytes 2621440 | tf_op jit(solution)/shard_map/reduce_scatter | solution.py:391
  852.1 122.8 %collective-permute-start.50 = (bf16[256,2048]{1,0:T(8,128)(2,1)}, bf16[256,2048]{1,0:T(8,128)(2,1)}, u32[]{:S(2)}, u32[]{:S(2)}) collective-permute-start(bf16[256,2048]{1,0:T(8,128)(2,1)} %slice.431), channel_id=1, source_target_pairs={{0,16},{16,0},{1,17},{17,1},{2,18},{18,2},{3,19},{19,3},{4,20},{20... | collective-permute-start | bytes 3145736 | tf_op jit(solution)/shard_map/ppermute | solution.py:46
  887.3 91.0 %collective-permute-start.52 = (bf16[256,2048]{1,0:T(8,128)(2,1)}, bf16[256,2048]{1,0:T(8,128)(2,1)}, u32[]{:S(2)}, u32[]{:S(2)}) collective-permute-start(bf16[256,2048]{1,0:T(8,128)(2,1)} %slice.430), channel_id=1, source_target_pairs={{0,16},{16,0},{1,17},{17,1},{2,18},{18,2},{3,19},{19,3},{4,20},{20... | collective-permute-start | bytes 3145736 | tf_op jit(solution)/shard_map/ppermute | solution.py:46
  974.9 48.8 %collective-permute-start.58 = (bf16[2048,512]{1,0:T(8,128)(2,1)}, bf16[2048,512]{1,0:T(8,128)(2,1)}, u32[]{:S(2)}, u32[]{:S(2)}) collective-permute-start(bf16[2048,512]{1,0:T(8,128)(2,1)} %add_convert_fusion.1), channel_id=1, source_target_pairs={{0,16},{16,0},{1,17},{17,1},{2,18},{18,2},{3,19},{19,3},{4,20},{20... | collective-permute-start | bytes 6291464 | tf_op jit(solution)/shard_map/ppermute | solution.py:46
  975.4 156.5 %reduce-scatter.14.cloned.1.call-start = ((), (), s32[]{:S(2)}) async-start(), calls=%async_computation.14 | async-start | bytes 2621440 | tf_op jit(solution)/shard_map/reduce_scatter | solution.py:391
  984.7 83.0 %collective-permute-start.61 = (bf16[512,2048]{1,0:T(8,128)(2,1)}, bf16[512,2048]{1,0:T(8,128)(2,1)}, u32[]{:S(2)}, u32[]{:S(2)}) collective-permute-start(bf16[512,2048]{1,0:T(8,128)(2,1)} %reduce-scatter.8.cloned.1.call-done), channel_id=1, source_target_pairs={{0,16},{16,0},{1,17},{17,1},{2,18},{18,2},{3,19},{19,3},{4,20},{20... | collective-permute-start | bytes 6291464 | tf_op jit(solution)/shard_map/ppermute | solution.py:46
  1026.0 46.1 %collective-permute-start.57 = (bf16[256,2048]{1,0:T(8,128)(2,1)}, bf16[256,2048]{1,0:T(8,128)(2,1)}, u32[]{:S(2)}, u32[]{:S(2)}) collective-permute-start(bf16[256,2048]{1,0:T(8,128)(2,1)} %add_convert_fusion.8), channel_id=1, source_target_pairs={{0,2},{1,3},{2,0},{3,1},{4,6},{5,7},{6,4},{7,5},{8,10},{9,11},{10,... | collective-permute-start | bytes 3145736 | tf_op jit(solution)/shard_map/ppermute | solution.py:38
  1038.1 39.8 %collective-permute-start.60 = (bf16[256,2048]{1,0:T(8,128)(2,1)}, bf16[256,2048]{1,0:T(8,128)(2,1)}, u32[]{:S(2)}, u32[]{:S(2)}) collective-permute-start(bf16[256,2048]{1,0:T(8,128)(2,1)} %add_convert_fusion.7), channel_id=1, source_target_pairs={{0,2},{1,3},{2,0},{3,1},{4,6},{5,7},{6,4},{7,5},{8,10},{9,11},{10,... | collective-permute-start | bytes 3145736 | tf_op jit(solution)/shard_map/ppermute | solution.py:38
  (135 other events, 1899.4 us)
Sparse Core Ops, SparseCore 0:
  10.2 48.6 all-gather.5
  61.0 26.6 all-gather.7
  89.8 27.4 all-gather.9
  119.3 162.7 all-gather.11
  283.5 88.9 all-gather.13
  517.0 90.5 reduce-scatter.5
  610.1 144.9 reduce-scatter.7
  845.3 42.1 reduce-scatter.9
  975.6 57.2 reduce-scatter.11
  1067.9 57.5 reduce-scatter.13

commit v2 on v1

--- a/solution.py
+++ b/solution.py
@@ -54,6 +54,34 @@
     return pieces
 
 
+def joined(near, far, bit):
+    return {**near, **{at | bit: piece for at, piece in far.items()}}
+
+
+class BothGroups:
+    def __init__(self, rows, bits, over_tok=None):
+        self.low, self.high = (bits[:-1], bits[-1])
+        self.tok_first = over_tok is not None
+        self.rows = rows
+        self.swapped = tok_swap(over_tok if self.tok_first else rows, self.high)
+        self.got = grp_swap(rows)
+
+    def go_on(self, line):
+        if self.tok_first:
+            self.swapped = line.hold(self.swapped)
+            self.late = grp_swap(self.swapped)
+        else:
+            self.late = tok_swap(self.got, self.high)
+        self.own = joined(
+            tok_pieces(self.rows, self.low), tok_pieces(self.swapped, self.low), self.high
+        )
+        self.far = tok_pieces(self.got, self.low)
+
+    def finish(self, line):
+        late = tok_pieces(line.hold(self.late), self.low)
+        return (self.own, joined(self.far, late, self.high))
+
+
 class FirstPiece:
     def __init__(self, rows, bits):
         self.rows = rows
@@ -79,17 +107,18 @@
 
     def go_on(self, line):
         def cut(*terms):
-            half = terms[0].shape[0] // 2
-            return sum(term[half:].astype(jnp.float32) for term in terms).astype(jnp.bfloat16)
+            rows = terms[-1].shape[0]
+            return sum(term[rows // 2 : rows].astype(jnp.float32) for term in terms).astype(
+                jnp.bfloat16
+            )
 
         for bit in self.bits[1:]:
-            got = tok_swap(line(cut, *self.terms), bit)
-            half = got.shape[0]
-            self.terms = tuple(term[:half] for term in self.terms) + (got,)
+            self.terms = self.terms + (tok_swap(line(cut, *self.terms), bit),)
 
 
 def total_of(terms):
-    return sum(term.astype(jnp.float32) for term in terms)
+    rows = terms[-1].shape[0]
+    return sum(term[:rows].astype(jnp.float32) for term in terms)
 
 
 def tok_order(bits):
@@ -116,17 +145,18 @@
     return pl.BlockSpec(shape, lambda *at: (0,) * len(shape), pipeline_mode=pl.Buffered(1))
 
 
-def place(pieces, spots):
+def place(pieces, order, here):
     rows, width = pieces[0].shape[-2:]
     total = sum(p.shape[0] for p in pieces)
 
-    def kernel(spots_ref, *refs):
+    def kernel(here_ref, *refs):
         *ins, out, held, arrive, leave = refs
         copies = []
-        for ref in ins:
+        for mask, ref in zip(order, ins):
             for j in range(ref.shape[0]):
                 at = len(copies)
-                start = pl.multiple_of(spots_ref[at] * rows, rows)
+                spot = j * len(order) + (here_ref[0] ^ mask)
+                start = pl.multiple_of(spot * rows, rows)
                 copies.append(
                     (
                         pltpu.make_async_copy(ref.at[j], held.at[at], arrive.at[at]),
@@ -156,7 +186,7 @@
         ],
         compiler_params=kernel_params(),
         cost_estimate=kernel_cost(0, out, out),
-    )(spots, *pieces)
+    )(here, *pieces)
 
 
 def over_pieces(pieces, which, extra, extra_specs, outs, compute, flops):
@@ -303,36 +333,54 @@
     return (kept, sent)
 
 
-def grad_product(rows_of, columns_of):
-    pairs = len(rows_of)
+def grad_product(rows_of, columns_of, which=None, far=None):
+    sets = len(columns_of)
+    count = len(rows_of)
     total, width = rows_of[0].shape
-    columns = columns_of[0].shape[1]
+    columns = columns_of[0][0].shape[1]
+    part, at = (columns, 0) if which is None else (columns // 2, which)
     block = 256
+    narrow = part % 128 != 0
 
     def kernel(*refs):
-        out = 0.0
-        for left, right in zip(refs[:pairs], refs[pairs : 2 * pairs]):
-            out = out + lax.dot_general(
-                left[...],
-                right[...],
-                (((0,), (0,)), ((), ())),
-                preferred_element_type=jnp.float32,
-            )
-        refs[-1][...] = out.astype(jnp.bfloat16)
-
-    out = jax.ShapeDtypeStruct((width, columns), jnp.bfloat16)
+        rows = refs[:count]
+        for k in range(sets):
+            out = 0.0
+            for left, right in zip(rows, refs[count + k * count : count + (k + 1) * count]):
+                right = right[:, at * part : (at + 1) * part] if narrow else right[...]
+                out = out + lax.dot_general(
+                    left[...],
+                    right,
+                    (((0,), (0,)), ((), ())),
+                    preferred_element_type=jnp.float32,
+                )
+            cut = slice(k * part, (k + 1) * part)
+            if far is not None:
+                out = out + refs[-2][:, cut].astype(jnp.float32)
+            refs[-1][:, cut] = out.astype(jnp.bfloat16)
+
+    out = jax.ShapeDtypeStruct((width, sets * part), jnp.bfloat16)
+    flat_columns = [c for columns_set in columns_of for c in columns_set]
+    column_spec = pl.BlockSpec(
+        (total, columns) if narrow else (total, part),
+        lambda i: (0, 0 if narrow else at),
+        pipeline_mode=pl.Buffered(1),
+    )
+    out_spec = pl.BlockSpec((block, sets * part), lambda i: (i, 0))
+    extra = [] if far is None else [far]
     return pl.pallas_call(
         kernel,
         grid=(width // block,),
-        in_specs=[pl.BlockSpec((total, block), lambda i: (0, i))] * pairs
-        + [kept_block((total, columns))] * pairs,
-        out_specs=pl.BlockSpec((block, columns), lambda i: (i, 0)),
+        in_specs=[pl.BlockSpec((total, block), lambda i: (0, i))] * count
+        + [column_spec] * len(flat_columns)
+        + [out_spec] * len(extra),
+        out_specs=out_spec,
         out_shape=out,
         compiler_params=kernel_params(),
         cost_estimate=kernel_cost(
-            2 * pairs * total * width * columns, out, *rows_of, *columns_of
+            2 * count * total * width * part * sets, out, *rows_of, *flat_columns
         ),
-    )(*rows_of, *columns_of)
+    )(*rows_of, *flat_columns, *extra)
 
 
 def seg_send(value, counts, step):
@@ -374,17 +422,39 @@
     )
 
 
-def in_order(got, own):
-    size, here = (lax.axis_size("seg"), lax.axis_index("seg"))
-    turned = jnp.concatenate([got, own], axis=0)
-    rows = own.shape[0]
-    return jnp.concatenate(
-        [
-            lax.dynamic_slice_in_dim(turned, lax.rem(size + k - here - 1, size) * rows, rows, 0)
-            for k in range(size)
-        ],
-        axis=0,
-    )
+def with_other(mine, got, own, pieces):
+    size = mine.shape[0] // own.shape[0]
+    rows, half = (own.shape[0], own.shape[1] // pieces)
+    here = lax.axis_index("seg").astype(jnp.int32)[None]
+
+    def kernel(here_ref, mine_ref, got_ref, own_ref, *outs):
+        is_own = pl.program_id(0) == here_ref[0]
+        rest = jnp.where(is_own, own_ref[...], got_ref[...])
+        for k, out in enumerate(outs):
+            cut = slice(k * half, (k + 1) * half)
+            out[:, :half] = mine_ref[:, cut]
+            out[:, half:] = rest[:, cut]
+
+    def got_block(i, at):
+        return (jnp.minimum(lax.rem(i + size - at[0] - 1 + size, size), size - 2), 0)
+
+    out = jax.ShapeDtypeStruct((mine.shape[0], 2 * half), mine.dtype)
+    return pl.pallas_call(
+        kernel,
+        grid_spec=pltpu.PrefetchScalarGridSpec(
+            num_scalar_prefetch=1,
+            grid=(size,),
+            in_specs=[
+                pl.BlockSpec((rows, own.shape[1]), lambda i, at: (i, 0)),
+                pl.BlockSpec((rows, own.shape[1]), got_block),
+                pl.BlockSpec((rows, own.shape[1]), lambda i, at: (0, 0)),
+            ],
+            out_specs=[pl.BlockSpec((rows, 2 * half), lambda i, at: (i, 0))] * pieces,
+        ),
+        out_shape=[out] * pieces,
+        compiler_params=kernel_params(),
+        cost_estimate=kernel_cost(0, mine, mine, mine, mine),
+    )(here, mine, got, own)
 
 
 def seg_scatter(value):
@@ -629,9 +699,7 @@
     )
 
 
-def local_backward(
-    queries, key_rows, values, log_totals, grad_local, grad_query, grad_contrib, grad_count, piece_first
-):
+def local_backward(queries, key_rows, values, log_totals, grad_local, grad_query, piece_first):
     heads = queries.shape[1] // HEAD_DIM
 
     def kernel(
@@ -642,24 +710,16 @@
         log_ref,
         local_ref,
         memory_ref,
-        contrib_ref,
-        count_ref,
         query_out,
         key_out,
         value_out,
-        key_sum,
-        value_sum,
     ):
         first = first_ref[0]
         scale = HEAD_DIM ** (-0.5)
-        keys = key_ref[...]
-        contrib = contrib_ref[0].astype(jnp.bfloat16)
-        grad_feat = dot_as(value_ref[...], contrib, BY_COLUMNS) + count_ref[0]
-        key_sum[...] = grad_feat * feature_slope(keys.astype(jnp.float32))
-        value_sum[...] = dot_as(low_feature(keys), contrib, ROWS_COLUMNS)
         for at in range(SEG_LEN // PIECE):
             rows = slice(at * PIECE, (at + 1) * PIECE)
             reach = reach_of(at)
+            known = reach_of(at - 1) if at > 0 else 0
             query_block = query_ref[rows, :]
             local_block = local_ref[rows, :]
             scores = masked_scores(query_block, key_ref[:reach, :], at, first)
@@ -671,12 +731,16 @@
             query_out[rows, :] = (
                 dot_as(grad_scores, key_ref[:reach, :], ROWS_COLUMNS) * scale + memory_ref[rows, :]
             ).astype(jnp.bfloat16)
-            key_sum[:reach, :] += dot_as(grad_scores, query_block, BY_ROWS) * scale
-            value_sum[:reach, :] += dot_as(probs.astype(jnp.bfloat16), local_block, BY_ROWS)
-        key_out[...] = key_sum[...].astype(jnp.bfloat16)
-        value_out[...] = value_sum[...].astype(jnp.bfloat16)
-
-    out = (like(queries.shape, jnp.bfloat16), "columns")
+            for out, part in (
+                (key_out, dot_as(grad_scores, query_block, BY_ROWS) * scale),
+                (value_out, dot_as(probs.astype(jnp.bfloat16), local_block, BY_ROWS)),
+            ):
+                if known > 0:
+                    out[:known, :] += part[:known]
+                if known < reach:
+                    out[known:reach, :] = part[known:]
+
+    wide = (like(queries.shape, jnp.float32), "columns")
     return head_call(
         kernel,
         [
@@ -687,12 +751,38 @@
             (log_totals, "heads"),
             (grad_local, "columns"),
             (grad_query, "columns"),
+        ],
+        [(like(queries.shape, jnp.bfloat16), "columns"), wide, wide],
+        local_flops(heads, 5),
+    )
+
+
+def with_memory(key_rows, values, key_sum, value_sum, grad_contrib, grad_count):
+    heads = key_rows.shape[1] // HEAD_DIM
+
+    def kernel(key_ref, value_ref, key_sum, value_sum, contrib_ref, count_ref, key_out, value_out):
+        keys = key_ref[...]
+        contrib = contrib_ref[0].astype(jnp.bfloat16)
+        grad_feat = dot_as(value_ref[...], contrib, BY_COLUMNS) + count_ref[0]
+        slope = feature_slope(keys.astype(jnp.float32))
+        key_out[...] = (key_sum[...] + grad_feat * slope).astype(jnp.bfloat16)
+        value_out[...] = (
+            value_sum[...] + dot_as(low_feature(keys), contrib, ROWS_COLUMNS)
+        ).astype(jnp.bfloat16)
+
+    out = (like(key_rows.shape, jnp.bfloat16), "columns")
+    return head_call(
+        kernel,
+        [
+            (key_rows, "columns"),
+            (values, "columns"),
+            (key_sum, "columns"),
+            (value_sum, "columns"),
             (grad_contrib, "heads"),
             (grad_count, "heads"),
         ],
-        [out, out, out],
-        local_flops(heads, 5),
-        [pltpu.VMEM((SEG_LEN, HEAD_DIM), jnp.float32)] * 2,
+        [out, out],
+        4 * SEG_LEN * heads * HEAD_DIM**2,
     )
 
 
@@ -738,7 +828,8 @@
     bits = tok_bits()
     here = lax.axis_index("tok")
     order = tok_order(bits)
-    spots = jnp.array(order, jnp.int32) ^ here.astype(jnp.int32)
+    here = here.astype(jnp.int32)[None]
+    spots = jnp.array(order, jnp.int32) ^ here
     in_turn = jnp.arange(2 * len(order), dtype=jnp.int32)
 
     pair_weights = (query_weight, key_weight)
@@ -760,20 +851,11 @@
     cot_pieces = FirstPiece(line.hold(cotangent), bits)
     pair_got = grp_swap(line(other_segments, pair_mine))
     gathered_a = line(
-        lambda *p: place(
-            p, jnp.concatenate([jnp.stack([s + m * len(order) for m in micros]) for s in spots])
-        ),
+        lambda *p: place(p, order, here),
         *[attend_pieces[at] for at in order],
     )
     gathered_a = [gathered_a[m * SEG_LEN : (m + 1) * SEG_LEN] for m in micros]
     value_got = grp_swap(line(other_segments, value_mine))
-
-    def with_other(mine, got, own, pieces):
-        rest = in_order(got, own)
-        return tuple(
-            jnp.concatenate([part[:, k * half : (k + 1) * half] for part in (mine, rest)], axis=1)
-            for k in range(pieces)
-        )
 
     def project(g, *weights):
         return tuple(
@@ -790,9 +872,7 @@
 
     contrib, count_k = zip(*[line(features, key_rows[m], values[m]) for m in micros])
     arrived = seg_send(jnp.concatenate(contrib), jnp.concatenate(count_k), 1)
-    local = [
-        line(local_attention, queries[m], key_rows[m], values[m], piece_first[m]) for m in micros
-    ]
+    local = [line(local_attention, queries[0], key_rows[0], values[0], piece_first[0])]
     (out_full,) = line(lambda *a: with_other(*a, 1), out_mine, out_got, out_other)
     cot_far = cot_far.rest(line)
     memory, norm_mem = line(seg_sum, arrived)
@@ -800,11 +880,18 @@
     norm_mem = [norm_mem[m * head_local : (m + 1) * head_local] for m in micros]
     mixes = []
     attended = []
+
+    def mixed_rows(m):
+        mixes.append(line(mixing, queries[m], local[m][0], memory[m], norm_mem[m], share))
+        return line(lambda a, w: products_cut([a], [w], spots), mixes[m], out_full)
+
     for m in micros:
-        mixes.append(line(mixing, queries[m], local[m][0], memory[m], norm_mem[m], share))
-        attended.append(
-            Scatter(*line(lambda a, w: products_cut([a], [w], spots), mixes[m], out_full))
-        )
+        if m > 0:
+            local.append(line(local_attention, queries[m], key_rows[m], values[m], piece_first[m]))
+        cut = mixed_rows(m)
+        if m > 0:
+            cut, attended[m - 1].terms = line.hold((cut, attended[m - 1].terms))
+        attended.append(Scatter(*cut))
         attended[m].go_on(line)
 
     def after_attention(x, terms):
@@ -816,10 +903,13 @@
     for m in micros:
         rows_m, normed_f = line(after_attention, hidden_in[m], attended[m].terms)
         resid.append(rows_m)
-        swapped = grp_swap(normed_f[None])
-        feed_pieces.append((tok_pieces(normed_f[None], bits), tok_pieces(swapped, bits)))
-        if m == 0:
-            feed_mine = line.hold(feed_mine)
+        over_tok = None
+        if m + 1 < count:
+            over_tok, attended[m + 1].terms = line.hold((normed_f[None], attended[m + 1].terms))
+        feed_pieces.append(BothGroups(normed_f[None], bits, over_tok))
+    for pieces in feed_pieces:
+        pieces.go_on(line)
+    feed_mine = line.hold(feed_mine)
 
     def interleaved(own, far):
         return [pieces[at] for at in order for pieces in (own, far)]
@@ -829,7 +919,7 @@
     inner_act = []
     for m in micros:
         rows_m, both, inner = line(
-            lambda w, *p: feed_forward(p, 0, w), feed_mine, *interleaved(*feed_pieces[m])
+            lambda w, *p: feed_forward(p, 0, w), feed_mine, *interleaved(*feed_pieces[m].finish(line))
         )
         feed_in.append(rows_m)
         products.append(both)
@@ -850,13 +940,7 @@
         grad_products.append(grads)
 
     def backward_rows(m):
-        grad_normed.append(
-            Scatter(
-                *line(
-                    lambda a, w: products_cut([a], [w], in_turn), grad_products[m], feed_mine
-                )
-            )
-        )
+        return line(lambda a, w: products_cut([a], [w], in_turn), grad_products[m], feed_mine)
 
     def own_and_far(terms):
         total = total_of(terms)
@@ -882,37 +966,49 @@
         rows_m, gain_part, low = line(after_feed_grad, resid[m], *grad_parts[m], cotangent[m])
         grad_resid.append(rows_m)
         feed_gain_parts.append(gain_part)
-        att_pieces.append(tok_pieces(low[None], bits))
+        att_pieces.append(FirstPiece(low[None], bits))
 
     feed_out = []
 
     def feed_result(m):
-        feed_out.append(
-            Scatter(
-                *line(lambda a, w: products_cut([a], [w], in_turn), inner_act[m], down_mine)
-            )
-        )
+        return line(lambda a, w: products_cut([a], [w], in_turn), inner_act[m], down_mine)
 
     backward(0)
-    backward_rows(0)
+    grad_normed.append(Scatter(*backward_rows(0)))
     backward(1)
-    down_grad = seg_scatter(line(grad_product, cot_all, inner_act))
     grad_normed[0].go_on(line)
-    backward_rows(1)
-    feed_grad = seg_scatter(line(grad_product, feed_in, grad_products))
+    down_raw = line(lambda a, b: grad_product(a, [b]), cot_all, inner_act)
+    cut = backward_rows(1)
+    down_raw, cut, grad_normed[0].terms = line.hold((down_raw, cut, grad_normed[0].terms))
+    grad_normed.append(Scatter(*cut))
+    down_grad = seg_scatter(down_raw)
+    finish_rows(0)
     grad_normed[1].go_on(line)
-    finish_rows(0)
-    feed_result(0)
+    feed_raw = line(lambda a, b: grad_product(a, [b]), feed_in, grad_products)
+    feed_raw, grad_normed[1].terms, grad_parts[0] = line.hold(
+        (feed_raw, grad_normed[1].terms, grad_parts[0])
+    )
+    feed_grad = seg_scatter(feed_raw)
     finish_rows(1)
     finish_feed(0)
-    feed_result(1)
+    cut = feed_result(0)
+    cut, grad_parts[1], att_pieces[0].got = line.hold((cut, grad_parts[1], att_pieces[0].got))
     finish_feed(1)
+    att_pieces[0] = att_pieces[0].rest(line)
+    feed_out.append(Scatter(*cut))
+    down_grad = line.hold(down_grad)
+    down_rest = grp_swap(down_grad)
 
     grad_att = []
     mem_back = []
     for m in micros:
+        if m > 0:
+            feed_out[m - 1].go_on(line)
+            cut = feed_result(m)
+            att_pieces[m] = att_pieces[m].rest(line)
+            feed_out.append(Scatter(*line.hold(cut)))
         grad_att.append(
-            line(lambda *p: place(p, spots), *[att_pieces[m][at] for at in order])
+            line(lambda *p: place(p, order, here), *[att_pieces[m][at] for at in order])
         )
         mem_back.append(
             line(
@@ -928,48 +1024,12 @@
         )
     logit_parts, grad_local, grad_query, grad_memory, grad_norm_mem = zip(*mem_back)
     back_arrived = seg_send(jnp.concatenate(grad_memory), jnp.concatenate(grad_norm_mem), -1)
-    for m in micros:
-        feed_out[m].go_on(line)
-    down_grad = line.hold(down_grad)
-    down_rest = grp_swap(down_grad)
-
-    def half_grad(which, rows_of, *columns_of):
-        return sum(
-            weight_grad(
-                a,
-                jnp.concatenate(
-                    [
-                        c[m] if which is None else c[m][:, which * half : (which + 1) * half]
-                        for c in columns_of
-                    ],
-                    axis=1,
-                ),
-            )
-            for m, a in enumerate(rows_of)
-        )
-
-    mixed_rows = mixes
-    out_far = grp_swap(
-        line(lambda a, b: half_grad(1, a, b).astype(jnp.bfloat16), grad_att, mixed_rows)
-    )
-    out_grad = seg_scatter(
-        line(
-            lambda a, b, far: (half_grad(0, a, b) + far.astype(jnp.float32)).astype(jnp.bfloat16),
-            grad_att,
-            mixed_rows,
-            out_far,
-        )
-    )
-    feed_parts = []
-    for m in micros:
-        own, far = line(own_and_far, feed_out[m].terms)
-        feed_parts.append((own, grp_swap(far)))
-    grad_contrib, grad_count = line(seg_sum, back_arrived)
-    feed_grad = line.hold(feed_grad)
-    feed_rest = grp_swap(feed_grad)
-    low_grads = []
-    for m in micros:
-        low_grads.append(
+    out_far = grp_swap(line(lambda a, b: grad_product(a, [b], 1), grad_att, mixes))
+    feed_out[-1].go_on(line)
+    local_back = []
+
+    def local_grad(m):
+        local_back.append(
             line(
                 local_backward,
                 queries[m],
@@ -978,21 +1038,44 @@
                 local[m][1],
                 grad_local[m],
                 grad_query[m],
-                grad_contrib[m * head_local : (m + 1) * head_local],
-                grad_count[m * head_local : (m + 1) * head_local],
                 piece_first[m],
             )
         )
-    query_low, key_low, value_low = zip(*low_grads)
-    gathered_list = gathered_a
-    query_sum = seg_scatter(
-        line(lambda a, b: half_grad(None, a, b).astype(jnp.bfloat16), gathered_list, query_low)
+
+    local_grad(0)
+    down_out = line(whole_columns, down_grad, down_rest)
+    local_grad(1)
+    query_low, key_sums, value_sums = zip(*local_back)
+    feed_parts = []
+    for m in micros:
+        own, far = line(own_and_far, feed_out[m].terms)
+        feed_parts.append((own, grp_swap(far)))
+    query_raw = line(lambda a, b: grad_product(a, [b]), gathered_a, query_low)
+    grad_contrib, grad_count = line(seg_sum, back_arrived)
+    out_raw = line(lambda a, b, far: grad_product(a, [b], 0, far), grad_att, mixes, out_far)
+    feed_grad, out_raw = line.hold((feed_grad, out_raw))
+    feed_half = gate_weight.shape[1] // 2
+    gate_grad, up_grad = (feed_grad[:, :feed_half], feed_grad[:, feed_half:])
+    gate_rest = grp_swap(gate_grad)
+    out_grad = seg_scatter(out_raw)
+    key_low, value_low = zip(
+        *[
+            line(
+                with_memory,
+                key_rows[m],
+                values[m],
+                key_sums[m],
+                value_sums[m],
+                grad_contrib[m * head_local : (m + 1) * head_local],
+                grad_count[m * head_local : (m + 1) * head_local],
+            )
+            for m in micros
+        ]
     )
     pair_far = grp_swap(
-        line(
-            lambda *a: half_grad(1, *a).astype(jnp.bfloat16), gathered_list, key_low, value_low
-        )
-    )
+        line(lambda a, c, d: grad_product(a, [c, d], 1), gathered_a, key_low, value_low)
+    )
+    query_sum = seg_scatter(query_raw)
     grad_normed_a = []
     for m in micros:
         grad_normed_a.append(
@@ -1008,33 +1091,36 @@
                 )
             )
         )
+    pair_far, out_grad = line.hold((pair_far, out_grad))
+    pair_raw = line(
+        lambda far, a, c, d: grad_product(a, [c, d], 0, far),
+        pair_far,
+        gathered_a,
+        key_low,
+        value_low,
+    )
+    pair_grad = seg_scatter(pair_raw)
+    up_rest = grp_swap(line.hold(up_grad))
+    out_rest = grp_swap(out_grad)
     for m in micros:
         grad_normed_a[m].go_on(line)
-    out_grad = line.hold(out_grad)
-    out_rest = grp_swap(out_grad)
-    pair_grad = seg_scatter(
-        line(
-            lambda far, *a: (half_grad(0, *a) + far.astype(jnp.float32)).astype(jnp.bfloat16),
-            pair_far,
-            gathered_list,
-            key_low,
-            value_low,
-        )
-    )
+    gate_out = line(whole_columns, gate_grad, gate_rest)
 
     def after_attend_grad(x, terms, grad, gain):
         unused_norm, pull = jax.vjp(root_norm, x.astype(jnp.float32), gain)
         grad_norm, gain_part = pull(total_of(terms))
         return ((grad + grad_norm).astype(jnp.bfloat16), gain_part)
 
+    gain, line.token = (line.token, out_grad)
     input_rows = []
     attend_gain_parts = []
     for m in micros:
         grad_rows, gain_part = line(
-            after_attend_grad, hidden_in[m], grad_normed_a[m].terms, grad_resid[m], line.token
+            after_attend_grad, hidden_in[m], grad_normed_a[m].terms, grad_resid[m], gain
         )
         input_rows.append(grad_rows)
         attend_gain_parts.append(gain_part)
+    feed_parts = line.hold(feed_parts)
     gate_logit_part = jnp.sum(sum(logit_parts), axis=(1, 2)) * share * (1.0 - share)
     gate_full_grad = jnp.sum(placement * gate_logit_part[:, None], axis=0)
     small = line(
@@ -1043,32 +1129,34 @@
         feed_gain_parts,
         gate_full_grad,
     )
-    out_out = line(whole_columns, out_grad, out_rest)
-    down_out = line(whole_columns, down_grad, down_rest)
-    feed_half = gate_weight.shape[1] // 2
-    gate_out, up_out = line(
-        lambda a, b: tuple(
-            whole_columns(*[part[:, k * feed_half : (k + 1) * feed_half] for part in (a, b)])
-            for k in range(2)
-        ),
-        feed_grad,
-        feed_rest,
-    )
+    small_steps = [
+        (axis, 1 << k)
+        for axis in ("tok", "seg", "grp")
+        for k in range(lax.axis_size(axis).bit_length() - 1)
+    ]
+
+    def add_small(small, axis, bit):
+        size = lax.axis_size(axis)
+        other = lax.ppermute(small, axis, [(k, k ^ bit) for k in range(size)])
+        return line(jnp.add, small, other)
+
+    for axis, bit in small_steps[:-3]:
+        small = add_small(small, axis, bit)
     query_sum = line.hold(query_sum)
     query_rest = grp_swap(query_sum)
-    for axis in ("tok", "seg", "grp"):
-        size = lax.axis_size(axis)
-        for bit in [1 << k for k in range(size.bit_length() - 1)]:
-            other = lax.ppermute(small, axis, [(k, k ^ bit) for k in range(size)])
-            small = line(jnp.add, small, other)
+    pair_grad, small = line.hold((pair_grad, small))
+    pair_rest = grp_swap(pair_grad)
+    up_out = line(whole_columns, up_grad, up_rest)
+    small = add_small(small, *small_steps[-3])
     output_rows = [
         line(
             lambda r, own, far: (r + added(own, far)).astype(jnp.bfloat16), resid[m], *feed_parts[m]
         )
         for m in micros
     ]
+    small = add_small(small, *small_steps[-2])
     query_grad = line(whole_sum, query_sum, query_rest)
-    pair_rest = grp_swap(pair_grad)
+    small = add_small(small, *small_steps[-1])
     key_grad, value_grad = line(
         lambda a, b: tuple(
             whole_columns(*[part[:, k * half : (k + 1) * half] for part in (a, b)])
@@ -1077,6 +1165,7 @@
         pair_grad,
         pair_rest,
     )
+    out_out = whole_columns(line.token, out_rest)
     small_sums = (small[0, :width], small[0, width : 2 * width], small[0, 2 * width :])
     return (
         (jnp.stack(output_rows), jnp.stack(input_rows))

time: 1160 us -> 1010 us (0.87)
  waiting for transfers between devices: 393 us -> 247 us
  Pallas kernels: 393 us -> 467 us
  matrix products: 55.4 us -> 26 us
  local copies, waits for them, and re-layouts: 85.9 us -> 57.1 us
  other arithmetic: 125 us -> 105 us
    ppermute x43 -> x42, waiting for transfers between devices: 215 us -> 97.2 us  [tok_swap(): return lax.ppermute(value, 'tok', [(k, k ^ bit) for k in range(count)])]
    ppermute x17 -> x19, waiting for transfers between devices: 175 us -> 118 us  [grp_swap(): return lax.ppermute(value, 'grp', [(0, 1), (1, 0)])]
    pallas_call x2 -> x7, Pallas kernels: 68.2 us -> 118 us  [grad_product(): pl.pallas_call(kernel, grid=(width // block,), in_specs=[pl.BlockSpec((to...]
    dot_general x10 -> x0, matrix products: 35.6 us -> none  [weight_grad(): jnp.einsum('td,tc->dc', rows, columns, preferred_element_type=jnp.float32)]
    slice x29 -> x1, local copies, waits for them, and re-layouts: 29.8 us -> 2.68 us  [body(): gate_grad, up_grad = (feed_grad[:, :feed_half], feed_grad[:, feed_half:])]
    concatenate x5 -> x0, other arithmetic: 17.5 us -> none  [the longest x4 17.4 us: with_other(): jnp.concatenate([part[:, k * half:(k + 1) * half] for part in (mine, rest...]
    ppermute x6, waiting for transfers between devices: 0.02 us -> 15.4 us  [seg_send(): lax.ppermute(packed, 'seg', [(k, k + step * far) for k in range(size) if...]
    pallas_call x0 -> x3, Pallas kernels: none -> 12.9 us  [with_other(): pl.pallas_call(kernel, grid_spec=pltpu.PrefetchScalarGridSpec(num_scalar_...]
  transfers between devices with their start and end apart: 81 -> 82, of which waited for: 28 -> 30; matrix products, arithmetic and copies ran while one was open for 21% -> 16% of each run, Pallas kernels for 29% -> 42%
where the time goes in v2:
time: 1010 us; the launch traced here: 998 us
  Pallas kernels  467 us (46%)
  waiting for transfers between devices  247 us (24%)
  other arithmetic  105 us (10%)
  starting transfers between devices  78.5 us (8%)
  local copies, waits for them, and re-layouts  57.1 us (6%)
  matrix products  26 us (3%)
  between operations  17 us (2%)
    pallas_call x8, Pallas kernels, products_cut(): pl.pallas_call(kernel, grid_spec=pltpu.PrefetchScalarGridSpec(num_scalar_...  125 us
    pallas_call x7, Pallas kernels, grad_product(): pl.pallas_call(kernel, grid=(width // block,), in_specs=[pl.BlockSpec((to...  118 us
    ppermute x19, waiting for transfers between devices, grp_swap(): return lax.ppermute(value, 'grp', [(0, 1), (1, 0)])  118 us
    pallas_call x12, Pallas kernels, head_call(): pl.pallas_call(kernel, grid=(heads[0],), in_specs=[spec(a.shape, kind) fo...  112 us
    ppermute x42, waiting for transfers between devices, tok_swap(): return lax.ppermute(value, 'tok', [(k, k ^ bit) for k in range(count)])  97.2 us
    pallas_call x4, Pallas kernels, over_pieces(): pl.pallas_call(kernel, grid=(total // block,), in_specs=[any_space()] * l...  86.1 us
    dot_general x6, matrix products, times(): return jnp.dot(left, right, preferred_element_type=jnp.float32)  26 us
    convert_element_type x8, other arithmetic, cut(): sum((term[rows // 2:rows].astype(jnp.float32) for term in terms))  24.8 us
  transfers between devices with their start and end apart: 82, of which 30 were waited for; matrix products, arithmetic and copies ran while one was open for 16% of the time, Pallas kernels for 42%

profile of v2, /device:TPU:0, one launch (start us, length us, event | category | flops | bytes accessed | tf_op | source)
XLA Modules:
  0.0 997.8 jit_solution(6624138573328600995)
XLA Ops:
  27.6 30.8 %collective-permute-done.1.refs_1_ = bf16[2,256,2048]{2,1,0:T(8,128)(2,1)} collective-permute-done((bf16[2,256,2048]{2,1,0:T(8,128)(2,1)}, bf16[2,256,2048]{2,1,0:T(8,128)(2,1)}, u32[]{:S(2)}, u32[]{:S(2)}) %collective-permute-start.1) | collective-permute-done | bytes 2097184 | tf_op jit(solution)/shard_map/ppermute | solution.py:46
  58.4 5.5 collective-permute-done.refs_1_
  70.8 6.5 shard_map.229
  77.3 10.3 %all-gather.8.cloned.1.call-done.mine_ref = bf16[2048,256]{1,0:T(8,128)(2,1)} async-done(((bf16[512,256]{1,0:T(8,128)(2,1)}), bf16[2048,256]{1,0:T(8,128)(2,1)}) %all-gather.8.cloned.1.call-update) | async-done | bytes 1048592 | tf_op jit(solution)/shard_map/all_gather | solution.py:410
  90.4 6.3 fusion.33
  96.7 7.5 collective-permute-done.4.got_ref
  109.0 6.3 convolution_convert_fusion.2.key_ref
  130.3 6.4 convolution_convert_fusion.value_ref
  163.8 12.5 %shard_map.234 = (f32[1024,512]{1,0:T(8,128)}, f32[4,1024,1]{2,1,0:T(8,128)}) custom-call(s32[1]{0:T(128)} %bitcast.5.first_ref, bf16[1024,512]{1,0:T(8,128)(2,1)} %convolution_convert_fusion.5.query_ref, bf16[1024,512]{1,0:T(8,128)(2,1)} %convolution_convert_fusion.3.key_ref, bf16[1024,512]{1,0:T(8,128)(2,1)} %convolution_convert_fusion.1.value_ref), custom_call_target="tpu_custom_call" | custom-call | flops 1744830464 | bytes 5259264 | tf_op jit(solution)/shard_map/pallas_call | solution.py:525
  181.7 11.4 %collective-permute-done.9 = bf16[8,129,128]{2,1,0:T(8,128)(2,1)S(1)} collective-permute-done((bf16[8,129,128]{2,1,0:T(8,128)(2,1)S(1)}, bf16[8,129,128]{2,1,0:T(8,128)(2,1)S(1)}, u32[]{:S(2)}, u32[]{:S(2)}) %collective-permute-start.9) | collective-permute-done | bytes 264224 | tf_op jit(solution)/shard_map/ppermute | solution.py:390
  199.1 7.5 shard_map.237
  215.5 12.2 %shard_map.238 = (f32[1024,512]{1,0:T(8,128)}, f32[4,1024,1]{2,1,0:T(8,128)}) custom-call(s32[1]{0:T(128)} %bitcast.6.first_ref, bf16[1024,512]{1,0:T(8,128)(2,1)} %convolution_convert_fusion.4.query_ref, bf16[1024,512]{1,0:T(8,128)(2,1)} %convolution_convert_fusion.2.key_ref, bf16[1024,512]{1,0:T(8,128)(2,1)} %convolution_convert_fusion.value_ref), custom_call_target="tpu_custom_call" | custom-call | flops 1744830464 | bytes 5259264 | tf_op jit(solution)/shard_map/pallas_call | solution.py:525
  232.0 7.5 shard_map.240
  249.6 20.0 %collective-permute-done.15 = bf16[256,2048]{1,0:T(8,128)(2,1)S(1)} collective-permute-done((bf16[256,2048]{1,0:T(8,128)(2,1)S(1)}, bf16[256,2048]{1,0:T(8,128)(2,1)S(1)}, u32[]{:S(2)}, u32[]{:S(2)}) %collective-permute-start.15) | collective-permute-done | bytes 1048608 | tf_op jit(solution)/shard_map/ppermute | solution.py:38
  272.7 21.8 %collective-permute-done.16.refs_2_ = bf16[1,256,2048]{2,1,0:T(8,128)(2,1)} collective-permute-done((bf16[1,256,2048]{2,1,0:T(8,128)(2,1)}, bf16[1,256,2048]{2,1,0:T(8,128)(2,1)}, u32[]{:S(2)}, u32[]{:S(2)}) %collective-permute-start.16) | collective-permute-done | bytes 1048608 | tf_op jit(solution)/shard_map/ppermute | solution.py:38
  297.2 23.6 %collective-permute-done.18.refs_3_ = bf16[1,256,2048]{2,1,0:T(8,128)(2,1)} collective-permute-done((bf16[1,256,2048]{2,1,0:T(8,128)(2,1)}, bf16[1,256,2048]{2,1,0:T(8,128)(2,1)}, u32[]{:S(2)}, u32[]{:S(2)}) %collective-permute-start.18) | collective-permute-done | bytes 1048608 | tf_op jit(solution)/shard_map/ppermute | solution.py:46
  321.5 19.3 %collective-permute-done.23.refs_1_ = bf16[1,256,2048]{2,1,0:T(8,128)(2,1)} collective-permute-done((bf16[1,256,2048]{2,1,0:T(8,128)(2,1)S(1)}, bf16[1,256,2048]{2,1,0:T(8,128)(2,1)}, u32[]{:S(2)}, u32[]{:S(2)}) %collective-permute-start.23) | collective-permute-done | bytes 1048608 | tf_op jit(solution)/shard_map/ppermute | solution.py:46
  341.9 25.5 %shard_map.241 = (bf16[2048,2048]{1,0:T(8,128)(2,1)}, bf16[2048,2048]{1,0:T(8,128)(2,1)}, bf16[2048,1024]{1,0:T(8,128)(2,1)}) custom-call(bf16[1,256,2048]{2,1,0:T(8,128)(2,1)} %bitcast.7.refs_0_, bf16[1,256,2048]{2,1,0:T(8,128)(2,1)} %collective-permute-done.17.refs_1_, bf16[1,256,2048]{2,1,0:T(8,128)(2,1)} %collective-permute-done.16.refs_2_, ...), custom_call_target="tpu_custom_call" | custom-call | flops 17179869184 | bytes 29360128 | tf_op jit(solution)/shard_map/pallas_call | solution.py:223
  371.1 24.9 %shard_map.242 = (bf16[2048,2048]{1,0:T(8,128)(2,1)}, bf16[2048,2048]{1,0:T(8,128)(2,1)}, bf16[2048,1024]{1,0:T(8,128)(2,1)}) custom-call(bf16[1,256,2048]{2,1,0:T(8,128)(2,1)} %bitcast.50, bf16[1,256,2048]{2,1,0:T(8,128)(2,1)} %collective-permute-done.23.refs_1_, bf16[1,256,2048]{2,1,0:T(8,128)(2,1)} %collective-permute-done.24.refs_2_, ...), custom_call_target="tpu_custom_call" | custom-call | flops 17179869184 | bytes 29360128 | tf_op jit(solution)/shard_map/pallas_call | solution.py:223
  396.1 17.7 %shard_map.243 = (bf16[2048,2048]{1,0:T(8,128)(2,1)}, bf16[2048,2048]{1,0:T(8,128)(2,1)}) custom-call(bf16[2,256,2048]{2,1,0:T(8,128)(2,1)} %refs_0_.1, bf16[2,256,2048]{2,1,0:T(8,128)(2,1)} %collective-permute-done.1.refs_1_, bf16[2,256,2048]{2,1,0:T(8,128)(2,1)} %collective-permute-done.6.refs_2_, bf16[2,256,2048]{2,1,0:T(8,128)(2,1)} %collective-permute-done.10.refs_3_, ...), custom_call_target="tpu_custom_call" | custom-call | flops 8589934592 | bytes 29360128 | tf_op jit(solution)/shard_map/pallas_call | solution.py:223
  414.4 25.8 %shard_map.244 = (bf16[1024,2048]{1,0:T(8,128)(2,1)}, bf16[1024,2048]{1,0:T(8,128)(2,1)}) custom-call(s32[8]{0:T(128)} %iota.20.order_ref, bf16[2048,2048]{1,0:T(8,128)(2,1)} %get-tuple-element.1076.refs_0_.refs_2_, bf16[2048,2048]{1,0:T(8,128)(2,1)} %all-gather.12.cloned.1.call-done.refs_8_.refs_1_), custom_call_target="tpu_custom_call" | custom-call | flops 17179869184 | bytes 25165824 | tf_op jit(solution)/shard_map/pallas_call | solution.py:310
  440.3 18.0 %shard_map.245 = (bf16[2048,2048]{1,0:T(8,128)(2,1)}, bf16[2048,2048]{1,0:T(8,128)(2,1)}) custom-call(bf16[2,256,2048]{2,1,0:T(8,128)(2,1)} %refs_0_.1, bf16[2,256,2048]{2,1,0:T(8,128)(2,1)} %collective-permute-done.1.refs_1_, bf16[2,256,2048]{2,1,0:T(8,128)(2,1)} %collective-permute-done.6.refs_2_, bf16[2,256,2048]{2,1,0:T(8,128)(2,1)} %collective-permute-done.10.refs_3_, ...), custom_call_target="tpu_custom_call" | custom-call | flops 8589934592 | bytes 29360128 | tf_op jit(solution)/shard_map/pallas_call | solution.py:223
  464.2 23.9 %shard_map.246 = bf16[2048,1024]{1,0:T(8,128)(2,1)} custom-call(bf16[2048,2048]{1,0:T(8,128)(2,1)} %get-tuple-element.1043.refs_0_, bf16[2048,2048]{1,0:T(8,128)(2,1)} %get-tuple-element.1044.refs_1_, bf16[2048,1024]{1,0:T(8,128)(2,1)} %get-tuple-element.1101.refs_2_.refs_0_, bf16[2048,1024]{1,0:T(8,128)(2,1)} %get-tuple-element.1157.refs_3_.refs_0_), custom_call_target="tpu_custom_call" | custom-call | flops 17179869184 | bytes 29360128 | tf_op jit(solution)/shard_map/pallas_call | solution.py:371
  488.7 25.8 %shard_map.247 = (bf16[1024,2048]{1,0:T(8,128)(2,1)}, bf16[1024,2048]{1,0:T(8,128)(2,1)}) custom-call(s32[8]{0:T(128)} %iota.21.order_ref, bf16[2048,2048]{1,0:T(8,128)(2,1)} %get-tuple-element.1077.refs_0_.refs_3_, bf16[2048,2048]{1,0:T(8,128)(2,1)} %all-gather.12.cloned.1.call-done.refs_8_.refs_1_), custom_call_target="tpu_custom_call" | custom-call | flops 17179869184 | bytes 25165824 | tf_op jit(solution)/shard_map/pallas_call | solution.py:310
  528.7 43.7 %shard_map.248 = bf16[2048,2048]{1,0:T(8,128)(2,1)} custom-call(bf16[2048,2048]{1,0:T(8,128)(2,1)} %get-tuple-element.1074.refs_0_, bf16[2048,2048]{1,0:T(8,128)(2,1)} %get-tuple-element.1075.refs_1_, bf16[2048,2048]{1,0:T(8,128)(2,1)} %get-tuple-element.1076.refs_0_.refs_2_, bf16[2048,2048]{1,0:T(8,128)(2,1)} %get-tuple-element.1077.refs_0_.refs_3_), custom_call_target="tpu_custom_call" | custom-call | flops 34359738368 | bytes 41943040 | tf_op jit(solution)/shard_map/pallas_call | solution.py:371
  591.3 16.1 %shard_map.249 = (bf16[1024,2048]{1,0:T(8,128)(2,1)}, bf16[1024,2048]{1,0:T(8,128)(2,1)}) custom-call(s32[8]{0:T(128)} %iota.19.order_ref, bf16[2048,1024]{1,0:T(8,128)(2,1)} %get-tuple-element.1101.refs_2_.refs_0_, bf16[2048,1024]{1,0:T(8,128)(2,1)} %all-gather.14.cloned.1.call-done.refs_8_.refs_1_), custom_call_target="tpu_custom_call" | custom-call | flops 8589934592 | bytes 16777216 | tf_op jit(solution)/shard_map/pallas_call | solution.py:310
  607.5 6.6 collective-permute-done.40.refs_1_
  629.9 10.9 %shard_map.251 = (f32[4,1,128]{2,1,0:T(1,128)}, bf16[1024,512]{1,0:T(8,128)(2,1)}, f32[1024,512]{1,0:T(8,128)}, f32[4,128,128]{2,1,0:T(8,128)}, f32[4,1,128]{2,1,0:T(1,128)}) custom-call(f32[4]{0:T(128)} %add_divide_fusion.share_ref, bf16[1024,2048]{1,0:T(8,128)(2,1)} %shard_map.250.grad_ref.refs_0_, bf16[2048,512]{1,0:T(8,128)(2,1)} %shard_map.235.refs_1_.weight_ref, ...), custom_call_target="tpu_custom_call" | custom-call | flops 2550136832 | bytes 13113344 | tf_op jit(solution)/shard_map/pallas_call | solution.py:525
  645.8 15.8 %shard_map.252 = (bf16[1024,2048]{1,0:T(8,128)(2,1)}, bf16[1024,2048]{1,0:T(8,128)(2,1)}) custom-call(s32[8]{0:T(128)} %iota.22.order_ref, bf16[2048,1024]{1,0:T(8,128)(2,1)} %get-tuple-element.1157.refs_3_.refs_0_, bf16[2048,1024]{1,0:T(8,128)(2,1)} %all-gather.14.cloned.1.call-done.refs_8_.refs_1_), custom_call_target="tpu_custom_call" | custom-call | flops 8589934592 | bytes 16777216 | tf_op jit(solution)/shard_map/pallas_call | solution.py:310
  664.1 6.3 collective-permute-done.46.refs_2_
  675.6 11.0 %shard_map.254 = (f32[4,1,128]{2,1,0:T(1,128)}, bf16[1024,512]{1,0:T(8,128)(2,1)}, f32[1024,512]{1,0:T(8,128)}, f32[4,128,128]{2,1,0:T(8,128)}, f32[4,1,128]{2,1,0:T(1,128)}) custom-call(f32[4]{0:T(128)} %add_divide_fusion.share_ref, bf16[1024,2048]{1,0:T(8,128)(2,1)} %shard_map.253.grad_ref.refs_1_, bf16[2048,512]{1,0:T(8,128)(2,1)} %shard_map.235.refs_1_.weight_ref, ...), custom_call_target="tpu_custom_call" | custom-call | flops 2550136832 | bytes 13113344 | tf_op jit(solution)/shard_map/pallas_call | solution.py:525
  686.6 8.9 shard_map.255
  704.3 18.9 %shard_map.256 = (bf16[1024,512]{1,0:T(8,128)(2,1)}, f32[1024,512]{1,0:T(8,128)}, f32[1024,512]{1,0:T(8,128)}) custom-call(s32[1]{0:T(128)} %bitcast.14.first_ref, bf16[1024,512]{1,0:T(8,128)(2,1)} %convolution_convert_fusion.5.query_ref, bf16[1024,512]{1,0:T(8,128)(2,1)} %convolution_convert_fusion.3.key_ref, ...), custom_call_target="tpu_custom_call" | custom-call | flops 4362076160 | bytes 11550720 | tf_op jit(solution)/shard_map/pallas_call | solution.py:525
  728.8 18.7 %shard_map.257 = (bf16[1024,512]{1,0:T(8,128)(2,1)}, f32[1024,512]{1,0:T(8,128)}, f32[1024,512]{1,0:T(8,128)}) custom-call(s32[1]{0:T(128)} %bitcast.15.first_ref, bf16[1024,512]{1,0:T(8,128)(2,1)} %convolution_convert_fusion.4.query_ref, bf16[1024,512]{1,0:T(8,128)(2,1)} %convolution_convert_fusion.2.key_ref, ...), custom_call_target="tpu_custom_call" | custom-call | flops 4362076160 | bytes 11550720 | tf_op jit(solution)/shard_map/pallas_call | solution.py:525
  762.8 10.5 %shard_map.258 = bf16[2048,512]{1,0:T(8,128)(2,1)} custom-call(bf16[1024,2048]{1,0:T(8,128)(2,1)} %get-tuple-element.1345.refs_0_, bf16[1024,2048]{1,0:T(8,128)(2,1)} %get-tuple-element.1346.refs_1_, bf16[1024,512]{1,0:T(8,128)(2,1)} %get-tuple-element.1316.refs_2_.refs_0_, bf16[1024,512]{1,0:T(8,128)(2,1)} %get-tuple-element.1326.refs_3_.refs_0_), custom_call_target="tpu_custom_call" | custom-call | flops 4294967296 | bytes 12582912 | tf_op jit(solution)/shard_map/pallas_call | solution.py:371
  777.8 9.1 shard_map.259
  788.5 5.2 shard_map.260
  793.7 5.2 shard_map.261
  798.9 10.6 %shard_map.262 = bf16[2048,512]{1,0:T(8,128)(2,1)} custom-call(bf16[1024,2048]{1,0:T(8,128)(2,1)} %get-tuple-element.1345.refs_0_, bf16[1024,2048]{1,0:T(8,128)(2,1)} %get-tuple-element.1346.refs_1_, bf16[1024,512]{1,0:T(8,128)(2,1)} %get-tuple-element.1347.refs_2_.refs_1_, bf16[1024,512]{1,0:T(8,128)(2,1)} %get-tuple-element.1348.refs_3_.refs_1_, ...), custom_call_target="tpu_custom_call" | custom-call | flops 4294967296 | bytes 14680064 | tf_op jit(solution)/shard_map/pallas_call | solution.py:371
  810.9 13.1 %shard_map.263 = (bf16[512,2048]{1,0:T(8,128)(2,1)}, bf16[512,2048]{1,0:T(8,128)(2,1)}) custom-call(s32[4]{0:T(128)} %broadcast_xor_fusion.order_ref, bf16[1024,512]{1,0:T(8,128)(2,1)} %get-tuple-element.1316.refs_2_.refs_0_, bf16[1024,512]{1,0:T(8,128)(2,1)} %get-tuple-element.1347.refs_2_.refs_1_, bf16[1024,512]{1,0:T(8,128)(2,1)} %get-tuple-element.1349.refs_4_.refs_2_, ...), custom_call_target="tpu_custom_call" | custom-call | flops 6442450944 | bytes 13631488 | tf_op jit(solution)/shard_map/pallas_call | solution.py:310
  824.2 13.1 %shard_map.264 = (bf16[512,2048]{1,0:T(8,128)(2,1)}, bf16[512,2048]{1,0:T(8,128)(2,1)}) custom-call(s32[4]{0:T(128)} %broadcast_xor_fusion.order_ref, bf16[1024,512]{1,0:T(8,128)(2,1)} %get-tuple-element.1326.refs_3_.refs_0_, bf16[1024,512]{1,0:T(8,128)(2,1)} %get-tuple-element.1348.refs_3_.refs_1_, bf16[1024,512]{1,0:T(8,128)(2,1)} %get-tuple-element.1350.refs_5_.refs_2_, ...), custom_call_target="tpu_custom_call" | custom-call | flops 6442450944 | bytes 13631488 | tf_op jit(solution)/shard_map/pallas_call | solution.py:310
  841.2 17.1 %collective-permute-done.59.refs_6_ = bf16[2048,512]{1,0:T(8,128)(2,1)} collective-permute-done((bf16[2048,512]{1,0:T(8,128)(2,1)}, bf16[2048,512]{1,0:T(8,128)(2,1)}, u32[]{:S(2)}, u32[]{:S(2)}) %collective-permute-start.59) | collective-permute-done | bytes 2097184 | tf_op jit(solution)/shard_map/ppermute | solution.py:46
  858.3 11.3 %shard_map.265 = bf16[2048,512]{1,0:T(8,128)(2,1)} custom-call(bf16[1024,2048]{1,0:T(8,128)(2,1)} %get-tuple-element.1345.refs_0_, bf16[1024,2048]{1,0:T(8,128)(2,1)} %get-tuple-element.1346.refs_1_, bf16[1024,512]{1,0:T(8,128)(2,1)} %get-tuple-element.1347.refs_2_.refs_1_, bf16[1024,512]{1,0:T(8,128)(2,1)} %get-tuple-element.1348.refs_3_.refs_1_, ...), custom_call_target="tpu_custom_call" | custom-call | flops 4294967296 | bytes 14680064 | tf_op jit(solution)/shard_map/pallas_call | solution.py:371
  880.8 5.1 fusion.18
  888.2 10.8 %collective-permute-done.62 = bf16[256,2048]{1,0:T(8,128)(2,1)} collective-permute-done((bf16[256,2048]{1,0:T(8,128)(2,1)}, bf16[256,2048]{1,0:T(8,128)(2,1)}, u32[]{:S(2)}, u32[]{:S(2)}) %collective-permute-start.62) | collective-permute-done | bytes 1048608 | tf_op jit(solution)/shard_map/ppermute | solution.py:38
  905.2 11.0 %collective-permute-done.60 = bf16[256,2048]{1,0:T(8,128)(2,1)S(1)} collective-permute-done((bf16[256,2048]{1,0:T(8,128)(2,1)S(1)}, bf16[256,2048]{1,0:T(8,128)(2,1)S(1)}, u32[]{:S(2)}, u32[]{:S(2)}) %collective-permute-start.60) | collective-permute-done | bytes 1048608 | tf_op jit(solution)/shard_map/ppermute | solution.py:38
  936.1 12.1 %collective-permute-done.66 = bf16[512,1024]{1,0:T(8,128)(2,1)} collective-permute-done((bf16[512,1024]{1,0:T(8,128)(2,1)S(1)}, bf16[512,1024]{1,0:T(8,128)(2,1)}, u32[]{:S(2)}, u32[]{:S(2)}) %collective-permute-start.66) | collective-permute-done | bytes 1048608 | tf_op jit(solution)/shard_map/ppermute | solution.py:46
  948.2 16.5 %collective-permute-start.65 = (f32[1,4112]{1,0:T(1,128)S(1)}, f32[1,4112]{1,0:T(1,128)S(1)}, u32[]{:S(2)}, u32[]{:S(2)}) collective-permute-start(f32[1,4112]{1,0:T(1,128)S(1)} %add.360), channel_id=1, source_target_pairs={{0,4},{4,0},{8,12},{12,8},{1,5},{5,1},{9,13},{13,9},{2,6},{6,2},{1... | collective-permute-start | bytes 49352 | tf_op jit(solution)/shard_map/ppermute | solution.py:1140
  (444 shorter events, 296.4 us)
Async XLA Ops:
  7.2 56.8 %all-gather.6.cloned.1.call-start = ((), (), s32[]{:S(2)}) async-start(), calls=%async_computation.5 | async-start | bytes 2621440 | tf_op jit(solution)/shard_map/all_gather | solution.py:410
  9.3 78.3 %all-gather.8.cloned.1.call-start = ((), (), s32[]{:S(2)}) async-start(), calls=%async_computation.6 | async-start | bytes 1310720 | tf_op jit(solution)/shard_map/all_gather | solution.py:410
  9.4 49.0 %collective-permute-start.1 = (bf16[2,256,2048]{2,1,0:T(8,128)(2,1)}, bf16[2,256,2048]{2,1,0:T(8,128)(2,1)}, u32[]{:S(2)}, u32[]{:S(2)}) collective-permute-start(bf16[2,256,2048]{2,1,0:T(8,128)(2,1)} %refs_0_.1), channel_id=1, source_target_pairs={{0,16},{16,0},{1,17},{17,1},{2,18},{18,2},{3,19},{19,3},{4,20},{20... | collective-permute-start | bytes 6291464 | tf_op jit(solution)/shard_map/ppermute | solution.py:46
  16.4 47.4 %collective-permute-start = (bf16[2,256,2048]{2,1,0:T(8,128)(2,1)}, bf16[2,256,2048]{2,1,0:T(8,128)(2,1)}, u32[]{:S(2)}, u32[]{:S(2)}) collective-permute-start(bf16[2,256,2048]{2,1,0:T(8,128)(2,1)} %fusion.2.refs_0_), channel_id=1, source_target_pairs={{0,2},{1,3},{2,0},{3,1},{4,6},{5,7},{6,4},{7,5},{8,10},{9,11},{10,... | collective-permute-start | bytes 6291464 | tf_op jit(solution)/shard_map/ppermute | solution.py:38
  17.9 51.6 %collective-permute-start.2 = (bf16[2,256,2048]{2,1,0:T(8,128)(2,1)}, bf16[2,256,2048]{2,1,0:T(8,128)(2,1)}, u32[]{:S(2)}, u32[]{:S(2)}) collective-permute-start(bf16[2,256,2048]{2,1,0:T(8,128)(2,1)} %fusion.2.refs_0_), channel_id=1, source_target_pairs={{0,1},{1,0},{2,3},{3,2},{4,5},{5,4},{6,7},{7,6},{8,9},{9,8},{10,11... | collective-permute-start | bytes 6291464 | tf_op jit(solution)/shard_map/ppermute | solution.py:38
  18.7 121.4 %all-gather.10.cloned.1.call-start = ((), (), s32[]{:S(2)}) async-start(), calls=%async_computation.7 | async-start | bytes 1310720 | tf_op jit(solution)/shard_map/all_gather | solution.py:410
  63.9 233.4 %all-gather.12.cloned.1.call-start = ((), (), s32[]{:S(2)}) async-start(), calls=%async_computation.8 | async-start | bytes 10485760 | tf_op jit(solution)/shard_map/all_gather | solution.py:410
  66.7 37.5 %collective-permute-start.4 = (bf16[1536,512]{1,0:T(8,128)(2,1)}, bf16[1536,512]{1,0:T(8,128)(2,1)}, u32[]{:S(2)}, u32[]{:S(2)}) collective-permute-start(bf16[1536,512]{1,0:T(8,128)(2,1)} %pad_maximum_fusion.3), channel_id=1, source_target_pairs={{0,16},{16,0},{1,17},{17,1},{2,18},{18,2},{3,19},{19,3},{4,20},{20... | collective-permute-start | bytes 4718600 | tf_op jit(solution)/shard_map/ppermute | solution.py:46
  67.1 328.9 %all-gather.14.cloned.1.call-start = ((), (), s32[]{:S(2)}) async-start(), calls=%async_computation.9 | async-start | bytes 5242880 | tf_op jit(solution)/shard_map/all_gather | solution.py:410
  67.4 57.9 %collective-permute-start.6 = (bf16[2,256,2048]{2,1,0:T(8,128)(2,1)}, bf16[2,256,2048]{2,1,0:T(8,128)(2,1)}, u32[]{:S(2)}, u32[]{:S(2)}) collective-permute-start(bf16[2,256,2048]{2,1,0:T(8,128)(2,1)} %refs_0_.1), channel_id=1, source_target_pairs={{0,2},{1,3},{2,0},{3,1},{4,6},{5,7},{6,4},{7,5},{8,10},{9,11},{10,... | collective-permute-start | bytes 6291464 | tf_op jit(solution)/shard_map/ppermute | solution.py:38
  69.2 111.9 %collective-permute-start.10 = (bf16[2,256,2048]{2,1,0:T(8,128)(2,1)}, bf16[2,256,2048]{2,1,0:T(8,128)(2,1)}, u32[]{:S(2)}, u32[]{:S(2)}) collective-permute-start(bf16[2,256,2048]{2,1,0:T(8,128)(2,1)} %collective-permute-done.1.refs_1_), channel_id=1, source_target_pairs={{0,2},{1,3},{2,0},{3,1},{4,6},{5,7},{6,4},{7,5},{8,10},{9,11},{10,... | collective-permute-start | bytes 6291464 | tf_op jit(solution)/shard_map/ppermute | solution.py:38
  88.9 36.4 %collective-permute-start.5 = (bf16[1536,256]{1,0:T(8,128)(2,1)S(1)}, bf16[1536,256]{1,0:T(8,128)(2,1)S(1)}, u32[]{:S(2)}, u32[]{:S(2)}) collective-permute-start(bf16[1536,256]{1,0:T(8,128)(2,1)S(1)} %pad_maximum_fusion.4), channel_id=1, source_target_pairs={{0,16},{16,0},{1,17},{17,1},{2,18},{18,2},{3,19},{19,3},{4,20},{20... | collective-permute-start | bytes 2359304 | tf_op jit(solution)/shard_map/ppermute | solution.py:46
  141.3 35.0 %collective-permute-start.11 = (bf16[1536,256]{1,0:T(8,128)(2,1)S(1)}, bf16[1536,256]{1,0:T(8,128)(2,1)S(1)}, u32[]{:S(2)}, u32[]{:S(2)}) collective-permute-start(bf16[1536,256]{1,0:T(8,128)(2,1)S(1)} %pad_maximum_fusion.5), channel_id=1, source_target_pairs={{0,16},{16,0},{1,17},{17,1},{2,18},{18,2},{3,19},{19,3},{4,20},{20... | collective-permute-start | bytes 2359304 | tf_op jit(solution)/shard_map/ppermute | solution.py:46
  161.2 31.9 %collective-permute-start.9 = (bf16[8,129,128]{2,1,0:T(8,128)(2,1)S(1)}, bf16[8,129,128]{2,1,0:T(8,128)(2,1)S(1)}, u32[]{:S(2)}, u32[]{:S(2)}) collective-permute-start(bf16[8,129,128]{2,1,0:T(8,128)(2,1)S(1)} %maximum_maximum_fusion), channel_id=1, source_target_pairs={{0,12},{1,13},{2,14},{3,15},{16,28},{17,29},{18,30},{19,31}} | collective-permute-start | bytes 792584 | tf_op jit(solution)/shard_map/ppermute | solution.py:390
  248.5 48.7 %collective-permute-start.17 = (bf16[1,256,2048]{2,1,0:T(8,128)(2,1)}, bf16[1,256,2048]{2,1,0:T(8,128)(2,1)}, u32[]{:S(2)}, u32[]{:S(2)}) collective-permute-start(bf16[1,256,2048]{2,1,0:T(8,128)(2,1)} %bitcast.7.refs_0_), channel_id=1, source_target_pairs={{0,16},{16,0},{1,17},{17,1},{2,18},{18,2},{3,19},{19,3},{4,20},{20... | collective-permute-start | bytes 3145736 | tf_op jit(solution)/shard_map/ppermute | solution.py:46
  295.6 329.0 %reduce-scatter.6.cloned.1.call-start = ((), (), s32[]{:S(2)}) async-start(), calls=%async_computation.10 | async-start | bytes 5242880 | tf_op jit(solution)/shard_map/reduce_scatter | solution.py:461
  295.7 45.1 %collective-permute-start.23 = (bf16[1,256,2048]{2,1,0:T(8,128)(2,1)S(1)}, bf16[1,256,2048]{2,1,0:T(8,128)(2,1)}, u32[]{:S(2)}, u32[]{:S(2)}) collective-permute-start(bf16[1,256,2048]{2,1,0:T(8,128)(2,1)S(1)} %bitcast.47), channel_id=1, source_target_pairs={{0,16},{16,0},{1,17},{17,1},{2,18},{18,2},{3,19},{19,3},{4,20},{20... | collective-permute-start | bytes 3145736 | tf_op jit(solution)/shard_map/ppermute | solution.py:46
  296.6 44.8 %collective-permute-start.24 = (bf16[1,256,2048]{2,1,0:T(8,128)(2,1)S(1)}, bf16[1,256,2048]{2,1,0:T(8,128)(2,1)}, u32[]{:S(2)}, u32[]{:S(2)}) collective-permute-start(bf16[1,256,2048]{2,1,0:T(8,128)(2,1)S(1)} %bitcast.48), channel_id=1, source_target_pairs={{0,2},{1,3},{2,0},{3,1},{4,6},{5,7},{6,4},{7,5},{8,10},{9,11},{10,... | collective-permute-start | bytes 3145736 | tf_op jit(solution)/shard_map/ppermute | solution.py:38
  321.4 46.6 %collective-permute-start.26 = (bf16[1,256,2048]{2,1,0:T(8,128)(2,1)S(1)}, bf16[1,256,2048]{2,1,0:T(8,128)(2,1)}, u32[]{:S(2)}, u32[]{:S(2)}) collective-permute-start(bf16[1,256,2048]{2,1,0:T(8,128)(2,1)S(1)} %bitcast.49), channel_id=1, source_target_pairs={{0,1},{1,0},{2,3},{3,2},{4,5},{5,4},{6,7},{7,6},{8,9},{9,8},{10,11... | collective-permute-start | bytes 3145736 | tf_op jit(solution)/shard_map/ppermute | solution.py:38
  367.6 28.5 %collective-permute-start.30 = (bf16[2,256,2048]{2,1,0:T(8,128)(2,1)S(1)}, bf16[2,256,2048]{2,1,0:T(8,128)(2,1)}, u32[]{:S(2)}, u32[]{:S(2)}) collective-permute-start(bf16[2,256,2048]{2,1,0:T(8,128)(2,1)S(1)} %copy-done.31), channel_id=1, source_target_pairs={{0,1},{1,0},{2,3},{3,2},{4,5},{5,4},{6,7},{7,6},{8,9},{9,8},{10,11... | collective-permute-start | bytes 6291464 | tf_op jit(solution)/shard_map/ppermute | solution.py:38
  368.0 28.0 %collective-permute-start.31 = (bf16[2,256,2048]{2,1,0:T(8,128)(2,1)}, bf16[2,256,2048]{2,1,0:T(8,128)(2,1)}, u32[]{:S(2)}, u32[]{:S(2)}) collective-permute-start(bf16[2,256,2048]{2,1,0:T(8,128)(2,1)} %collective-permute-done.1.refs_1_), channel_id=1, source_target_pairs={{0,1},{1,0},{2,3},{3,2},{4,5},{5,4},{6,7},{7,6},{8,9},{9,8},{10,11... | collective-permute-start | bytes 6291464 | tf_op jit(solution)/shard_map/ppermute | solution.py:38
  368.1 28.0 %collective-permute-start.32 = (bf16[2,256,2048]{2,1,0:T(8,128)(2,1)}, bf16[2,256,2048]{2,1,0:T(8,128)(2,1)}, u32[]{:S(2)}, u32[]{:S(2)}) collective-permute-start(bf16[2,256,2048]{2,1,0:T(8,128)(2,1)} %collective-permute-done.6.refs_2_), channel_id=1, source_target_pairs={{0,1},{1,0},{2,3},{3,2},{4,5},{5,4},{6,7},{7,6},{8,9},{9,8},{10,11... | collective-permute-start | bytes 6291464 | tf_op jit(solution)/shard_map/ppermute | solution.py:38
  462.7 51.7 %collective-permute-start.35 = (bf16[512,2048]{1,0:T(8,128)(2,1)}, bf16[512,2048]{1,0:T(8,128)(2,1)S(1)}, u32[]{:S(2)}, u32[]{:S(2)}) collective-permute-start(bf16[512,2048]{1,0:T(8,128)(2,1)} %add_convert_fusion.3), channel_id=1, source_target_pairs={{0,2},{1,3},{2,0},{3,1},{4,6},{5,7},{6,4},{7,5},{8,10},{9,11},{10,... | collective-permute-start | bytes 6291464 | tf_op jit(solution)/shard_map/ppermute | solution.py:38
  514.5 272.3 %reduce-scatter.8.cloned.1.call-start = ((), (), s32[]{:S(2)}) async-start(), calls=%async_computation.11 | async-start | bytes 10485760 | tf_op jit(solution)/shard_map/reduce_scatter | solution.py:461
  523.2 49.2 %collective-permute-start.38 = (bf16[256,2048]{1,0:T(8,128)(2,1)}, bf16[256,2048]{1,0:T(8,128)(2,1)S(1)}, u32[]{:S(2)}, u32[]{:S(2)}) collective-permute-start(bf16[256,2048]{1,0:T(8,128)(2,1)} %slice.380), channel_id=1, source_target_pairs={{0,16},{16,0},{1,17},{17,1},{2,18},{18,2},{3,19},{19,3},{4,20},{20... | collective-permute-start | bytes 3145736 | tf_op jit(solution)/shard_map/ppermute | solution.py:46
  528.1 47.9 %collective-permute-start.37 = (bf16[512,2048]{1,0:T(8,128)(2,1)}, bf16[512,2048]{1,0:T(8,128)(2,1)S(1)}, u32[]{:S(2)}, u32[]{:S(2)}) collective-permute-start(bf16[512,2048]{1,0:T(8,128)(2,1)} %add_convert_fusion.2), channel_id=1, source_target_pairs={{0,2},{1,3},{2,0},{3,1},{4,6},{5,7},{6,4},{7,5},{8,10},{9,11},{10,... | collective-permute-start | bytes 6291464 | tf_op jit(solution)/shard_map/ppermute | solution.py:38
  582.2 276.1 %reduce-scatter.10.cloned.1.call-start = ((), (), s32[]{:S(2)}) async-start(), calls=%async_computation.12 | async-start | bytes 1310720 | tf_op jit(solution)/shard_map/reduce_scatter | solution.py:461
  623.3 38.3 %collective-permute-start.45 = (bf16[1,256,2048]{2,1,0:T(8,128)(2,1)S(1)}, bf16[1,256,2048]{2,1,0:T(8,128)(2,1)}, u32[]{:S(2)}, u32[]{:S(2)}) collective-permute-start(bf16[1,256,2048]{2,1,0:T(8,128)(2,1)S(1)} %bitcast.40), channel_id=1, source_target_pairs={{0,2},{1,3},{2,0},{3,1},{4,6},{5,7},{6,4},{7,5},{8,10},{9,11},{10,... | collective-permute-start | bytes 3145736 | tf_op jit(solution)/shard_map/ppermute | solution.py:38
  661.6 33.9 %collective-permute-start.49 = (bf16[1024,2048]{1,0:T(8,128)(2,1)}, bf16[1024,2048]{1,0:T(8,128)(2,1)}, u32[]{:S(2)}, u32[]{:S(2)}) collective-permute-start(bf16[1024,2048]{1,0:T(8,128)(2,1)} %get-tuple-element.1195), channel_id=1, source_target_pairs={{0,1},{1,0},{2,3},{3,2},{4,5},{5,4},{6,7},{7,6},{8,9},{9,8},{10,11... | collective-permute-start | bytes 12582920 | tf_op jit(solution)/shard_map/ppermute | solution.py:38
  662.2 61.0 %collective-permute-start.48 = (bf16[512,1024]{1,0:T(8,128)(2,1)}, bf16[512,1024]{1,0:T(8,128)(2,1)}, u32[]{:S(2)}, u32[]{:S(2)}) collective-permute-start(bf16[512,1024]{1,0:T(8,128)(2,1)} %reduce-scatter.6.cloned.1.call-done), channel_id=1, source_target_pairs={{0,16},{16,0},{1,17},{17,1},{2,18},{18,2},{3,19},{19,3},{4,20},{20... | collective-permute-start | bytes 3145736 | tf_op jit(solution)/shard_map/ppermute | solution.py:46
  662.6 84.9 %collective-permute-start.44 = (bf16[512,2048]{1,0:T(8,128)(2,1)}, bf16[512,2048]{1,0:T(8,128)(2,1)}, u32[]{:S(2)}, u32[]{:S(2)}) collective-permute-start(bf16[512,2048]{1,0:T(8,128)(2,1)} %add_convert_fusion.1), channel_id=1, source_target_pairs={{0,2},{1,3},{2,0},{3,1},{4,6},{5,7},{6,4},{7,5},{8,10},{9,11},{10,... | collective-permute-start | bytes 6291464 | tf_op jit(solution)/shard_map/ppermute | solution.py:38
  700.0 55.6 %collective-permute-start.51 = (bf16[512,2048]{1,0:T(8,128)(2,1)}, bf16[512,2048]{1,0:T(8,128)(2,1)}, u32[]{:S(2)}, u32[]{:S(2)}) collective-permute-start(bf16[512,2048]{1,0:T(8,128)(2,1)} %add_convert_fusion), channel_id=1, source_target_pairs={{0,2},{1,3},{2,0},{3,1},{4,6},{5,7},{6,4},{7,5},{8,10},{9,11},{10,... | collective-permute-start | bytes 6291464 | tf_op jit(solution)/shard_map/ppermute | solution.py:38
  701.6 71.6 %collective-permute-start.53 = (bf16[8,129,128]{2,1,0:T(8,128)(2,1)S(1)}, bf16[8,129,128]{2,1,0:T(8,128)(2,1)S(1)}, u32[]{:S(2)}, u32[]{:S(2)}) collective-permute-start(bf16[8,129,128]{2,1,0:T(8,128)(2,1)S(1)} %maximum_maximum_fusion.1), channel_id=1, source_target_pairs={{4,0},{8,4},{12,8},{5,1},{9,5},{13,9},{6,2},{10,6},{14,10},{7,3},{... | collective-permute-start | bytes 792584 | tf_op jit(solution)/shard_map/ppermute | solution.py:390
  702.9 73.7 %collective-permute-start.54 = (bf16[8,129,128]{2,1,0:T(8,128)(2,1)S(1)}, bf16[8,129,128]{2,1,0:T(8,128)(2,1)S(1)}, u32[]{:S(2)}, u32[]{:S(2)}) collective-permute-start(bf16[8,129,128]{2,1,0:T(8,128)(2,1)S(1)} %maximum_maximum_fusion.1), channel_id=1, source_target_pairs={{8,0},{12,4},{9,1},{13,5},{10,2},{14,6},{11,3},{15,7},{24,16},{28,... | collective-permute-start | bytes 792584 | tf_op jit(solution)/shard_map/ppermute | solution.py:390
  723.2 53.5 %collective-permute-start.55 = (bf16[8,129,128]{2,1,0:T(8,128)(2,1)S(1)}, bf16[8,129,128]{2,1,0:T(8,128)(2,1)}, u32[]{:S(2)}, u32[]{:S(2)}) collective-permute-start(bf16[8,129,128]{2,1,0:T(8,128)(2,1)S(1)} %maximum_maximum_fusion.1), channel_id=1, source_target_pairs={{12,0},{13,1},{14,2},{15,3},{28,16},{29,17},{30,18},{31,19}} | collective-permute-start | bytes 792584 | tf_op jit(solution)/shard_map/ppermute | solution.py:390
  747.5 30.3 %collective-permute-start.56 = (bf16[2048,256]{1,0:T(8,128)(2,1)}, bf16[2048,256]{1,0:T(8,128)(2,1)}, u32[]{:S(2)}, u32[]{:S(2)}) collective-permute-start(bf16[2048,256]{1,0:T(8,128)(2,1)} %shard_map.255), channel_id=1, source_target_pairs={{0,16},{16,0},{1,17},{17,1},{2,18},{18,2},{3,19},{19,3},{4,20},{20... | collective-permute-start | bytes 3145736 | tf_op jit(solution)/shard_map/ppermute | solution.py:46
  786.9 144.4 %reduce-scatter.14.cloned.1.call-start = ((), (), s32[]{:S(2)}) async-start(), calls=%async_computation.14 | async-start | bytes 2621440 | tf_op jit(solution)/shard_map/reduce_scatter | solution.py:461
  787.8 148.3 %reduce-scatter.12.cloned.1.call-start = ((), (), s32[]{:S(2)}) async-start(), calls=%async_computation.13 | async-start | bytes 2621440 | tf_op jit(solution)/shard_map/reduce_scatter | solution.py:461
  809.5 48.9 %collective-permute-start.59 = (bf16[2048,512]{1,0:T(8,128)(2,1)}, bf16[2048,512]{1,0:T(8,128)(2,1)}, u32[]{:S(2)}, u32[]{:S(2)}) collective-permute-start(bf16[2048,512]{1,0:T(8,128)(2,1)} %shard_map.262), channel_id=1, source_target_pairs={{0,16},{16,0},{1,17},{17,1},{2,18},{18,2},{3,19},{19,3},{4,20},{20... | collective-permute-start | bytes 6291464 | tf_op jit(solution)/shard_map/ppermute | solution.py:46
  824.1 45.6 %collective-permute-start.58 = (bf16[512,2048]{1,0:T(8,128)(2,1)}, bf16[512,2048]{1,0:T(8,128)(2,1)}, u32[]{:S(2)}, u32[]{:S(2)}) collective-permute-start(bf16[512,2048]{1,0:T(8,128)(2,1)} %get-tuple-element.1338), channel_id=1, source_target_pairs={{0,1},{1,0},{2,3},{3,2},{4,5},{5,4},{6,7},{7,6},{8,9},{9,8},{10,11... | collective-permute-start | bytes 6291464 | tf_op jit(solution)/shard_map/ppermute | solution.py:38
  837.3 38.4 %collective-permute-start.57 = (bf16[512,2048]{1,0:T(8,128)(2,1)}, bf16[512,2048]{1,0:T(8,128)(2,1)}, u32[]{:S(2)}, u32[]{:S(2)}) collective-permute-start(bf16[512,2048]{1,0:T(8,128)(2,1)} %get-tuple-element.1336), channel_id=1, source_target_pairs={{0,1},{1,0},{2,3},{3,2},{4,5},{5,4},{6,7},{7,6},{8,9},{9,8},{10,11... | collective-permute-start | bytes 6291464 | tf_op jit(solution)/shard_map/ppermute | solution.py:38
  840.6 40.2 %collective-permute-start.61 = (bf16[512,1024]{1,0:T(8,128)(2,1)}, bf16[512,1024]{1,0:T(8,128)(2,1)}, u32[]{:S(2)}, u32[]{:S(2)}) collective-permute-start(bf16[512,1024]{1,0:T(8,128)(2,1)} %get-tuple-element.1365), channel_id=1, source_target_pairs={{0,16},{16,0},{1,17},{17,1},{2,18},{18,2},{3,19},{19,3},{4,20},{20... | collective-permute-start | bytes 3145736 | tf_op jit(solution)/shard_map/ppermute | solution.py:46
  873.6 48.0 %collective-permute-start.50 = (bf16[256,2048]{1,0:T(8,128)(2,1)}, bf16[256,2048]{1,0:T(8,128)(2,1)}, u32[]{:S(2)}, u32[]{:S(2)}) collective-permute-start(bf16[256,2048]{1,0:T(8,128)(2,1)} %slice.378), channel_id=1, source_target_pairs={{0,16},{16,0},{1,17},{17,1},{2,18},{18,2},{3,19},{19,3},{4,20},{20... | collective-permute-start | bytes 3145736 | tf_op jit(solution)/shard_map/ppermute | solution.py:46
  875.1 50.6 %collective-permute-start.52 = (bf16[256,2048]{1,0:T(8,128)(2,1)}, bf16[256,2048]{1,0:T(8,128)(2,1)}, u32[]{:S(2)}, u32[]{:S(2)}) collective-permute-start(bf16[256,2048]{1,0:T(8,128)(2,1)} %slice.377), channel_id=1, source_target_pairs={{0,16},{16,0},{1,17},{17,1},{2,18},{18,2},{3,19},{19,3},{4,20},{20... | collective-permute-start | bytes 3145736 | tf_op jit(solution)/shard_map/ppermute | solution.py:46
  885.9 30.3 %collective-permute-start.60 = (bf16[256,2048]{1,0:T(8,128)(2,1)S(1)}, bf16[256,2048]{1,0:T(8,128)(2,1)S(1)}, u32[]{:S(2)}, u32[]{:S(2)}) collective-permute-start(bf16[256,2048]{1,0:T(8,128)(2,1)S(1)} %add_convert_fusion.6), channel_id=1, source_target_pairs={{0,2},{1,3},{2,0},{3,1},{4,6},{5,7},{6,4},{7,5},{8,10},{9,11},{10,... | collective-permute-start | bytes 3145736 | tf_op jit(solution)/shard_map/ppermute | solution.py:38
  886.8 61.5 %collective-permute-start.66 = (bf16[512,1024]{1,0:T(8,128)(2,1)S(1)}, bf16[512,1024]{1,0:T(8,128)(2,1)}, u32[]{:S(2)}, u32[]{:S(2)}) collective-permute-start(bf16[512,1024]{1,0:T(8,128)(2,1)S(1)} %get-tuple-element.1421), channel_id=1, source_target_pairs={{0,16},{16,0},{1,17},{17,1},{2,18},{18,2},{3,19},{19,3},{4,20},{20... | collective-permute-start | bytes 3145736 | tf_op jit(solution)/shard_map/ppermute | solution.py:46
  925.9 62.7 %collective-permute-start.71 = (bf16[512,256]{1,0:T(8,128)(2,1)S(1)}, bf16[512,256]{1,0:T(8,128)(2,1)}, u32[]{:S(2)}, u32[]{:S(2)}) collective-permute-start(bf16[512,256]{1,0:T(8,128)(2,1)S(1)} %copy-done.54), channel_id=1, source_target_pairs={{0,16},{16,0},{1,17},{17,1},{2,18},{18,2},{3,19},{19,3},{4,20},{20... | collective-permute-start | bytes 786440 | tf_op jit(solution)/shard_map/ppermute | solution.py:46
  931.3 48.6 %collective-permute-start.67 = (bf16[512,512]{1,0:T(8,128)(2,1)}, bf16[512,512]{1,0:T(8,128)(2,1)}, u32[]{:S(2)}, u32[]{:S(2)}) collective-permute-start(bf16[512,512]{1,0:T(8,128)(2,1)} %reduce-scatter.14.cloned.1.call-done), channel_id=1, source_target_pairs={{0,16},{16,0},{1,17},{17,1},{2,18},{18,2},{3,19},{19,3},{4,20},{20... | collective-permute-start | bytes 1572872 | tf_op jit(solution)/shard_map/ppermute | solution.py:46
  (107 other events, 1372.8 us)
Sparse Core Ops, SparseCore 0:
  10.2 48.6 all-gather.5
  61.0 26.6 all-gather.7
  89.2 27.4 all-gather.9
  118.1 162.7 all-gather.11
  295.7 98.2 all-gather.13
  514.6 94.4 reduce-scatter.5
  611.6 162.7 reduce-scatter.7
  787.0 42.9 reduce-scatter.9
  832.3 42.2 reduce-scatter.13
  877.4 58.6 reduce-scatter.11

commit v3 on v2

--- a/solution.py
+++ b/solution.py
@@ -1043,6 +1043,7 @@
         )
 
     local_grad(0)
+    out_far = line.hold(out_far)
     down_out = line(whole_columns, down_grad, down_rest)
     local_grad(1)
     query_low, key_sums, value_sums = zip(*local_back)
@@ -1051,7 +1052,9 @@
         own, far = line(own_and_far, feed_out[m].terms)
         feed_parts.append((own, grp_swap(far)))
     query_raw = line(lambda a, b: grad_product(a, [b]), gathered_a, query_low)
-    grad_contrib, grad_count = line(seg_sum, back_arrived)
+    feed_parts[0], grad_contrib, grad_count = line.hold(
+        (feed_parts[0],) + line(seg_sum, back_arrived)
+    )
     out_raw = line(lambda a, b, far: grad_product(a, [b], 0, far), grad_att, mixes, out_far)
     feed_grad, out_raw = line.hold((feed_grad, out_raw))
     feed_half = gate_weight.shape[1] // 2
@@ -1072,9 +1075,9 @@
             for m in micros
         ]
     )
-    pair_far = grp_swap(
-        line(lambda a, c, d: grad_product(a, [c, d], 1), gathered_a, key_low, value_low)
-    )
+    pair_far = line(lambda a, c, d: grad_product(a, [c, d], 1), gathered_a, key_low, value_low)
+    pair_far, gate_rest = line.hold((pair_far, gate_rest))
+    pair_far = grp_swap(pair_far)
     query_sum = seg_scatter(query_raw)
     grad_normed_a = []
     for m in micros:

time: 1010 us -> 994 us (0.984)
    ppermute x19, waiting for transfers between devices: 118 us -> 99.5 us  [grp_swap(): return lax.ppermute(value, 'grp', [(0, 1), (1, 0)])]
  transfers between devices with their start and end apart: 82 -> 82, of which waited for: 30 -> 28; matrix products, arithmetic and copies ran while one was open for 16% -> 17% of each run, Pallas kernels for 42% -> 43%
where the time goes in v3:
time: 994 us; the launch traced here: 985 us
  Pallas kernels  467 us (47%)
  waiting for transfers between devices  240 us (24%)
  other arithmetic  105 us (11%)
  starting transfers between devices  72.1 us (7%)
  local copies, waits for them, and re-layouts  57.2 us (6%)
  matrix products  26 us (3%)
  between operations  17.1 us (2%)
    pallas_call x8, Pallas kernels, products_cut(): pl.pallas_call(kernel, grid_spec=pltpu.PrefetchScalarGridSpec(num_scalar_...  125 us
    pallas_call x7, Pallas kernels, grad_product(): pl.pallas_call(kernel, grid=(width // block,), in_specs=[pl.BlockSpec((to...  118 us
    pallas_call x12, Pallas kernels, head_call(): pl.pallas_call(kernel, grid=(heads[0],), in_specs=[spec(a.shape, kind) fo...  111 us
    ppermute x42, waiting for transfers between devices, tok_swap(): return lax.ppermute(value, 'tok', [(k, k ^ bit) for k in range(count)])  104 us
    ppermute x19, waiting for transfers between devices, grp_swap(): return lax.ppermute(value, 'grp', [(0, 1), (1, 0)])  99.5 us
    pallas_call x4, Pallas kernels, over_pieces(): pl.pallas_call(kernel, grid=(total // block,), in_specs=[any_space()] * l...  86.1 us
    dot_general x6, matrix products, times(): return jnp.dot(left, right, preferred_element_type=jnp.float32)  26 us
    convert_element_type x8, other arithmetic, cut(): sum((term[rows // 2:rows].astype(jnp.float32) for term in terms))  24.8 us
  transfers between devices with their start and end apart: 82, of which 28 were waited for; matrix products, arithmetic and copies ran while one was open for 17% of the time, Pallas kernels for 43%

profile of v3, /device:TPU:0, one launch (start us, length us, event | category | flops | bytes accessed | tf_op | source)
XLA Modules:
  0.0 984.8 jit_solution(16539410656981655572)
XLA Ops:
  27.6 30.8 %collective-permute-done.1.refs_1_ = bf16[2,256,2048]{2,1,0:T(8,128)(2,1)} collective-permute-done((bf16[2,256,2048]{2,1,0:T(8,128)(2,1)}, bf16[2,256,2048]{2,1,0:T(8,128)(2,1)}, u32[]{:S(2)}, u32[]{:S(2)}) %collective-permute-start.1) | collective-permute-done | bytes 2097184 | tf_op jit(solution)/shard_map/ppermute | solution.py:46
  58.4 5.5 collective-permute-done.refs_1_
  70.8 6.5 shard_map.229
  77.3 10.3 %all-gather.8.cloned.1.call-done.mine_ref = bf16[2048,256]{1,0:T(8,128)(2,1)} async-done(((bf16[512,256]{1,0:T(8,128)(2,1)}), bf16[2048,256]{1,0:T(8,128)(2,1)}) %all-gather.8.cloned.1.call-update) | async-done | bytes 1048592 | tf_op jit(solution)/shard_map/all_gather | solution.py:410
  90.4 6.3 fusion.33
  96.7 7.5 collective-permute-done.4.got_ref
  109.0 6.3 convolution_convert_fusion.2.key_ref
  130.3 6.4 convolution_convert_fusion.value_ref
  163.9 12.5 %shard_map.234 = (f32[1024,512]{1,0:T(8,128)}, f32[4,1024,1]{2,1,0:T(8,128)}) custom-call(s32[1]{0:T(128)} %bitcast.5.first_ref, bf16[1024,512]{1,0:T(8,128)(2,1)} %convolution_convert_fusion.5.query_ref, bf16[1024,512]{1,0:T(8,128)(2,1)} %convolution_convert_fusion.3.key_ref, bf16[1024,512]{1,0:T(8,128)(2,1)} %convolution_convert_fusion.1.value_ref), custom_call_target="tpu_custom_call" | custom-call | flops 1744830464 | bytes 5259264 | tf_op jit(solution)/shard_map/pallas_call | solution.py:525
  181.7 11.4 %collective-permute-done.9 = bf16[8,129,128]{2,1,0:T(8,128)(2,1)S(1)} collective-permute-done((bf16[8,129,128]{2,1,0:T(8,128)(2,1)S(1)}, bf16[8,129,128]{2,1,0:T(8,128)(2,1)S(1)}, u32[]{:S(2)}, u32[]{:S(2)}) %collective-permute-start.9) | collective-permute-done | bytes 264224 | tf_op jit(solution)/shard_map/ppermute | solution.py:390
  199.1 7.5 shard_map.237
  215.5 12.2 %shard_map.238 = (f32[1024,512]{1,0:T(8,128)}, f32[4,1024,1]{2,1,0:T(8,128)}) custom-call(s32[1]{0:T(128)} %bitcast.6.first_ref, bf16[1024,512]{1,0:T(8,128)(2,1)} %convolution_convert_fusion.4.query_ref, bf16[1024,512]{1,0:T(8,128)(2,1)} %convolution_convert_fusion.2.key_ref, bf16[1024,512]{1,0:T(8,128)(2,1)} %convolution_convert_fusion.value_ref), custom_call_target="tpu_custom_call" | custom-call | flops 1744830464 | bytes 5259264 | tf_op jit(solution)/shard_map/pallas_call | solution.py:525
  232.0 7.5 shard_map.240
  249.6 20.0 %collective-permute-done.15 = bf16[256,2048]{1,0:T(8,128)(2,1)S(1)} collective-permute-done((bf16[256,2048]{1,0:T(8,128)(2,1)S(1)}, bf16[256,2048]{1,0:T(8,128)(2,1)S(1)}, u32[]{:S(2)}, u32[]{:S(2)}) %collective-permute-start.15) | collective-permute-done | bytes 1048608 | tf_op jit(solution)/shard_map/ppermute | solution.py:38
  272.6 21.9 %collective-permute-done.16.refs_2_ = bf16[1,256,2048]{2,1,0:T(8,128)(2,1)} collective-permute-done((bf16[1,256,2048]{2,1,0:T(8,128)(2,1)}, bf16[1,256,2048]{2,1,0:T(8,128)(2,1)}, u32[]{:S(2)}, u32[]{:S(2)}) %collective-permute-start.16) | collective-permute-done | bytes 1048608 | tf_op jit(solution)/shard_map/ppermute | solution.py:38
  297.2 23.6 %collective-permute-done.18.refs_3_ = bf16[1,256,2048]{2,1,0:T(8,128)(2,1)} collective-permute-done((bf16[1,256,2048]{2,1,0:T(8,128)(2,1)}, bf16[1,256,2048]{2,1,0:T(8,128)(2,1)}, u32[]{:S(2)}, u32[]{:S(2)}) %collective-permute-start.18) | collective-permute-done | bytes 1048608 | tf_op jit(solution)/shard_map/ppermute | solution.py:46
  321.5 19.3 %collective-permute-done.23.refs_1_ = bf16[1,256,2048]{2,1,0:T(8,128)(2,1)} collective-permute-done((bf16[1,256,2048]{2,1,0:T(8,128)(2,1)S(1)}, bf16[1,256,2048]{2,1,0:T(8,128)(2,1)}, u32[]{:S(2)}, u32[]{:S(2)}) %collective-permute-start.23) | collective-permute-done | bytes 1048608 | tf_op jit(solution)/shard_map/ppermute | solution.py:46
  341.9 25.5 %shard_map.241 = (bf16[2048,2048]{1,0:T(8,128)(2,1)}, bf16[2048,2048]{1,0:T(8,128)(2,1)}, bf16[2048,1024]{1,0:T(8,128)(2,1)}) custom-call(bf16[1,256,2048]{2,1,0:T(8,128)(2,1)} %bitcast.7.refs_0_, bf16[1,256,2048]{2,1,0:T(8,128)(2,1)} %collective-permute-done.17.refs_1_, bf16[1,256,2048]{2,1,0:T(8,128)(2,1)} %collective-permute-done.16.refs_2_, ...), custom_call_target="tpu_custom_call" | custom-call | flops 17179869184 | bytes 29360128 | tf_op jit(solution)/shard_map/pallas_call | solution.py:223
  371.1 24.9 %shard_map.242 = (bf16[2048,2048]{1,0:T(8,128)(2,1)}, bf16[2048,2048]{1,0:T(8,128)(2,1)}, bf16[2048,1024]{1,0:T(8,128)(2,1)}) custom-call(bf16[1,256,2048]{2,1,0:T(8,128)(2,1)} %bitcast.50, bf16[1,256,2048]{2,1,0:T(8,128)(2,1)} %collective-permute-done.23.refs_1_, bf16[1,256,2048]{2,1,0:T(8,128)(2,1)} %collective-permute-done.24.refs_2_, ...), custom_call_target="tpu_custom_call" | custom-call | flops 17179869184 | bytes 29360128 | tf_op jit(solution)/shard_map/pallas_call | solution.py:223
  396.1 17.7 %shard_map.243 = (bf16[2048,2048]{1,0:T(8,128)(2,1)}, bf16[2048,2048]{1,0:T(8,128)(2,1)}) custom-call(bf16[2,256,2048]{2,1,0:T(8,128)(2,1)} %refs_0_.1, bf16[2,256,2048]{2,1,0:T(8,128)(2,1)} %collective-permute-done.1.refs_1_, bf16[2,256,2048]{2,1,0:T(8,128)(2,1)} %collective-permute-done.6.refs_2_, bf16[2,256,2048]{2,1,0:T(8,128)(2,1)} %collective-permute-done.10.refs_3_, ...), custom_call_target="tpu_custom_call" | custom-call | flops 8589934592 | bytes 29360128 | tf_op jit(solution)/shard_map/pallas_call | solution.py:223
  414.4 25.8 %shard_map.244 = (bf16[1024,2048]{1,0:T(8,128)(2,1)}, bf16[1024,2048]{1,0:T(8,128)(2,1)}) custom-call(s32[8]{0:T(128)} %iota.20.order_ref, bf16[2048,2048]{1,0:T(8,128)(2,1)} %get-tuple-element.1086.refs_0_.refs_2_, bf16[2048,2048]{1,0:T(8,128)(2,1)} %all-gather.12.cloned.1.call-done.refs_8_.refs_1_), custom_call_target="tpu_custom_call" | custom-call | flops 17179869184 | bytes 25165824 | tf_op jit(solution)/shard_map/pallas_call | solution.py:310
  440.3 18.0 %shard_map.245 = (bf16[2048,2048]{1,0:T(8,128)(2,1)}, bf16[2048,2048]{1,0:T(8,128)(2,1)}) custom-call(bf16[2,256,2048]{2,1,0:T(8,128)(2,1)} %refs_0_.1, bf16[2,256,2048]{2,1,0:T(8,128)(2,1)} %collective-permute-done.1.refs_1_, bf16[2,256,2048]{2,1,0:T(8,128)(2,1)} %collective-permute-done.6.refs_2_, bf16[2,256,2048]{2,1,0:T(8,128)(2,1)} %collective-permute-done.10.refs_3_, ...), custom_call_target="tpu_custom_call" | custom-call | flops 8589934592 | bytes 29360128 | tf_op jit(solution)/shard_map/pallas_call | solution.py:223
  464.2 23.9 %shard_map.246 = bf16[2048,1024]{1,0:T(8,128)(2,1)} custom-call(bf16[2048,2048]{1,0:T(8,128)(2,1)} %get-tuple-element.1053.refs_0_, bf16[2048,2048]{1,0:T(8,128)(2,1)} %get-tuple-element.1054.refs_1_, bf16[2048,1024]{1,0:T(8,128)(2,1)} %get-tuple-element.1111.refs_2_.refs_0_, bf16[2048,1024]{1,0:T(8,128)(2,1)} %get-tuple-element.1167.refs_3_.refs_0_), custom_call_target="tpu_custom_call" | custom-call | flops 17179869184 | bytes 29360128 | tf_op jit(solution)/shard_map/pallas_call | solution.py:371
  488.7 25.8 %shard_map.247 = (bf16[1024,2048]{1,0:T(8,128)(2,1)}, bf16[1024,2048]{1,0:T(8,128)(2,1)}) custom-call(s32[8]{0:T(128)} %iota.21.order_ref, bf16[2048,2048]{1,0:T(8,128)(2,1)} %get-tuple-element.1087.refs_0_.refs_3_, bf16[2048,2048]{1,0:T(8,128)(2,1)} %all-gather.12.cloned.1.call-done.refs_8_.refs_1_), custom_call_target="tpu_custom_call" | custom-call | flops 17179869184 | bytes 25165824 | tf_op jit(solution)/shard_map/pallas_call | solution.py:310
  528.7 43.7 %shard_map.248 = bf16[2048,2048]{1,0:T(8,128)(2,1)} custom-call(bf16[2048,2048]{1,0:T(8,128)(2,1)} %get-tuple-element.1084.refs_0_, bf16[2048,2048]{1,0:T(8,128)(2,1)} %get-tuple-element.1085.refs_1_, bf16[2048,2048]{1,0:T(8,128)(2,1)} %get-tuple-element.1086.refs_0_.refs_2_, bf16[2048,2048]{1,0:T(8,128)(2,1)} %get-tuple-element.1087.refs_0_.refs_3_), custom_call_target="tpu_custom_call" | custom-call | flops 34359738368 | bytes 41943040 | tf_op jit(solution)/shard_map/pallas_call | solution.py:371
  591.2 16.1 %shard_map.249 = (bf16[1024,2048]{1,0:T(8,128)(2,1)}, bf16[1024,2048]{1,0:T(8,128)(2,1)}) custom-call(s32[8]{0:T(128)} %iota.19.order_ref, bf16[2048,1024]{1,0:T(8,128)(2,1)} %get-tuple-element.1111.refs_2_.refs_0_, bf16[2048,1024]{1,0:T(8,128)(2,1)} %all-gather.14.cloned.1.call-done.refs_8_.refs_1_), custom_call_target="tpu_custom_call" | custom-call | flops 8589934592 | bytes 16777216 | tf_op jit(solution)/shard_map/pallas_call | solution.py:310
  607.3 6.7 collective-permute-done.40.refs_1_
  629.7 10.8 %shard_map.251 = (f32[4,1,128]{2,1,0:T(1,128)}, bf16[1024,512]{1,0:T(8,128)(2,1)}, f32[1024,512]{1,0:T(8,128)}, f32[4,128,128]{2,1,0:T(8,128)}, f32[4,1,128]{2,1,0:T(1,128)}) custom-call(f32[4]{0:T(128)} %add_divide_fusion.share_ref, bf16[1024,2048]{1,0:T(8,128)(2,1)} %shard_map.250.grad_ref.refs_0_, bf16[2048,512]{1,0:T(8,128)(2,1)} %shard_map.235.refs_1_.weight_ref, ...), custom_call_target="tpu_custom_call" | custom-call | flops 2550136832 | bytes 13113344 | tf_op jit(solution)/shard_map/pallas_call | solution.py:525
  645.6 15.8 %shard_map.252 = (bf16[1024,2048]{1,0:T(8,128)(2,1)}, bf16[1024,2048]{1,0:T(8,128)(2,1)}) custom-call(s32[8]{0:T(128)} %iota.22.order_ref, bf16[2048,1024]{1,0:T(8,128)(2,1)} %get-tuple-element.1167.refs_3_.refs_0_, bf16[2048,1024]{1,0:T(8,128)(2,1)} %all-gather.14.cloned.1.call-done.refs_8_.refs_1_), custom_call_target="tpu_custom_call" | custom-call | flops 8589934592 | bytes 16777216 | tf_op jit(solution)/shard_map/pallas_call | solution.py:310
  664.1 5.6 collective-permute-done.46.refs_2_
  675.5 11.0 %shard_map.254 = (f32[4,1,128]{2,1,0:T(1,128)}, bf16[1024,512]{1,0:T(8,128)(2,1)}, f32[1024,512]{1,0:T(8,128)}, f32[4,128,128]{2,1,0:T(8,128)}, f32[4,1,128]{2,1,0:T(1,128)}) custom-call(f32[4]{0:T(128)} %add_divide_fusion.share_ref, bf16[1024,2048]{1,0:T(8,128)(2,1)} %shard_map.253.grad_ref.refs_1_, bf16[2048,512]{1,0:T(8,128)(2,1)} %shard_map.235.refs_1_.weight_ref, ...), custom_call_target="tpu_custom_call" | custom-call | flops 2550136832 | bytes 13113344 | tf_op jit(solution)/shard_map/pallas_call | solution.py:525
  686.4 8.9 shard_map.255
  703.5 18.9 %shard_map.256 = (bf16[1024,512]{1,0:T(8,128)(2,1)}, f32[1024,512]{1,0:T(8,128)}, f32[1024,512]{1,0:T(8,128)}) custom-call(s32[1]{0:T(128)} %bitcast.14.first_ref, bf16[1024,512]{1,0:T(8,128)(2,1)} %convolution_convert_fusion.5.query_ref, bf16[1024,512]{1,0:T(8,128)(2,1)} %convolution_convert_fusion.3.key_ref, ...), custom_call_target="tpu_custom_call" | custom-call | flops 4362076160 | bytes 11550720 | tf_op jit(solution)/shard_map/pallas_call | solution.py:525
  729.3 18.7 %shard_map.257 = (bf16[1024,512]{1,0:T(8,128)(2,1)}, f32[1024,512]{1,0:T(8,128)}, f32[1024,512]{1,0:T(8,128)}) custom-call(s32[1]{0:T(128)} %bitcast.15.first_ref, bf16[1024,512]{1,0:T(8,128)(2,1)} %convolution_convert_fusion.4.query_ref, bf16[1024,512]{1,0:T(8,128)(2,1)} %convolution_convert_fusion.2.key_ref, ...), custom_call_target="tpu_custom_call" | custom-call | flops 4362076160 | bytes 11550720 | tf_op jit(solution)/shard_map/pallas_call | solution.py:525
  762.2 10.5 %shard_map.258 = bf16[2048,512]{1,0:T(8,128)(2,1)} custom-call(bf16[1024,2048]{1,0:T(8,128)(2,1)} %get-tuple-element.1364.refs_0_, bf16[1024,2048]{1,0:T(8,128)(2,1)} %get-tuple-element.1365.refs_1_, bf16[1024,512]{1,0:T(8,128)(2,1)} %get-tuple-element.1336.refs_2_.refs_0_, bf16[1024,512]{1,0:T(8,128)(2,1)} %get-tuple-element.1346.refs_3_.refs_0_), custom_call_target="tpu_custom_call" | custom-call | flops 4294967296 | bytes 12582912 | tf_op jit(solution)/shard_map/pallas_call | solution.py:371
  772.7 5.5 collective-permute-done.53
  780.3 9.1 shard_map.259
  795.5 5.3 shard_map.260
  800.7 5.2 shard_map.261
  805.9 10.6 %shard_map.262 = bf16[2048,512]{1,0:T(8,128)(2,1)} custom-call(bf16[1024,2048]{1,0:T(8,128)(2,1)} %get-tuple-element.1364.refs_0_, bf16[1024,2048]{1,0:T(8,128)(2,1)} %get-tuple-element.1365.refs_1_, bf16[1024,512]{1,0:T(8,128)(2,1)} %get-tuple-element.1366.refs_2_.refs_1_, bf16[1024,512]{1,0:T(8,128)(2,1)} %get-tuple-element.1367.refs_3_.refs_1_, ...), custom_call_target="tpu_custom_call" | custom-call | flops 4294967296 | bytes 14680064 | tf_op jit(solution)/shard_map/pallas_call | solution.py:371
  817.7 13.2 %shard_map.263 = (bf16[512,2048]{1,0:T(8,128)(2,1)}, bf16[512,2048]{1,0:T(8,128)(2,1)}) custom-call(s32[4]{0:T(128)} %broadcast_xor_fusion.order_ref, bf16[1024,512]{1,0:T(8,128)(2,1)} %get-tuple-element.1336.refs_2_.refs_0_, bf16[1024,512]{1,0:T(8,128)(2,1)} %get-tuple-element.1366.refs_2_.refs_1_, bf16[1024,512]{1,0:T(8,128)(2,1)} %get-tuple-element.1368.refs_4_.refs_2_, ...), custom_call_target="tpu_custom_call" | custom-call | flops 6442450944 | bytes 13631488 | tf_op jit(solution)/shard_map/pallas_call | solution.py:310
  831.0 13.1 %shard_map.264 = (bf16[512,2048]{1,0:T(8,128)(2,1)}, bf16[512,2048]{1,0:T(8,128)(2,1)}) custom-call(s32[4]{0:T(128)} %broadcast_xor_fusion.order_ref, bf16[1024,512]{1,0:T(8,128)(2,1)} %get-tuple-element.1346.refs_3_.refs_0_, bf16[1024,512]{1,0:T(8,128)(2,1)} %get-tuple-element.1367.refs_3_.refs_1_, bf16[1024,512]{1,0:T(8,128)(2,1)} %get-tuple-element.1369.refs_5_.refs_2_, ...), custom_call_target="tpu_custom_call" | custom-call | flops 6442450944 | bytes 13631488 | tf_op jit(solution)/shard_map/pallas_call | solution.py:310
  844.8 18.1 %collective-permute-done.60.refs_6_ = bf16[2048,512]{1,0:T(8,128)(2,1)} collective-permute-done((bf16[2048,512]{1,0:T(8,128)(2,1)}, bf16[2048,512]{1,0:T(8,128)(2,1)}, u32[]{:S(2)}, u32[]{:S(2)}) %collective-permute-start.60) | collective-permute-done | bytes 2097184 | tf_op jit(solution)/shard_map/ppermute | solution.py:46
  862.9 11.3 %shard_map.265 = bf16[2048,512]{1,0:T(8,128)(2,1)} custom-call(bf16[1024,2048]{1,0:T(8,128)(2,1)} %get-tuple-element.1364.refs_0_, bf16[1024,2048]{1,0:T(8,128)(2,1)} %get-tuple-element.1365.refs_1_, bf16[1024,512]{1,0:T(8,128)(2,1)} %get-tuple-element.1366.refs_2_.refs_1_, bf16[1024,512]{1,0:T(8,128)(2,1)} %get-tuple-element.1367.refs_3_.refs_1_, ...), custom_call_target="tpu_custom_call" | custom-call | flops 4294967296 | bytes 14680064 | tf_op jit(solution)/shard_map/pallas_call | solution.py:371
  888.5 15.1 %collective-permute-done.62 = bf16[256,2048]{1,0:T(8,128)(2,1)} collective-permute-done((bf16[256,2048]{1,0:T(8,128)(2,1)}, bf16[256,2048]{1,0:T(8,128)(2,1)}, u32[]{:S(2)}, u32[]{:S(2)}) %collective-permute-start.62) | collective-permute-done | bytes 1048608 | tf_op jit(solution)/shard_map/ppermute | solution.py:38
  909.8 13.8 %collective-permute-done.61 = bf16[256,2048]{1,0:T(8,128)(2,1)S(1)} collective-permute-done((bf16[256,2048]{1,0:T(8,128)(2,1)S(1)}, bf16[256,2048]{1,0:T(8,128)(2,1)S(1)}, u32[]{:S(2)}, u32[]{:S(2)}) %collective-permute-start.61) | collective-permute-done | bytes 1048608 | tf_op jit(solution)/shard_map/ppermute | solution.py:38
  935.2 5.8 reduce-scatter.12.cloned.1.call-done
  941.0 10.1 %collective-permute-start.65 = (f32[1,4112]{1,0:T(1,128)S(1)}, f32[1,4112]{1,0:T(1,128)S(1)}, u32[]{:S(2)}, u32[]{:S(2)}) collective-permute-start(f32[1,4112]{1,0:T(1,128)S(1)} %add.360), channel_id=1, source_target_pairs={{0,4},{4,0},{8,12},{12,8},{1,5},{5,1},{9,13},{13,9},{2,6},{6,2},{1... | collective-permute-start | bytes 49352 | tf_op jit(solution)/shard_map/ppermute | solution.py:1143
  (444 shorter events, 287.9 us)
Async XLA Ops:
  7.2 56.8 %all-gather.6.cloned.1.call-start = ((), (), s32[]{:S(2)}) async-start(), calls=%async_computation.5 | async-start | bytes 2621440 | tf_op jit(solution)/shard_map/all_gather | solution.py:410
  9.3 78.3 %all-gather.8.cloned.1.call-start = ((), (), s32[]{:S(2)}) async-start(), calls=%async_computation.6 | async-start | bytes 1310720 | tf_op jit(solution)/shard_map/all_gather | solution.py:410
  9.4 49.0 %collective-permute-start.1 = (bf16[2,256,2048]{2,1,0:T(8,128)(2,1)}, bf16[2,256,2048]{2,1,0:T(8,128)(2,1)}, u32[]{:S(2)}, u32[]{:S(2)}) collective-permute-start(bf16[2,256,2048]{2,1,0:T(8,128)(2,1)} %refs_0_.1), channel_id=1, source_target_pairs={{0,16},{16,0},{1,17},{17,1},{2,18},{18,2},{3,19},{19,3},{4,20},{20... | collective-permute-start | bytes 6291464 | tf_op jit(solution)/shard_map/ppermute | solution.py:46
  16.4 47.4 %collective-permute-start = (bf16[2,256,2048]{2,1,0:T(8,128)(2,1)}, bf16[2,256,2048]{2,1,0:T(8,128)(2,1)}, u32[]{:S(2)}, u32[]{:S(2)}) collective-permute-start(bf16[2,256,2048]{2,1,0:T(8,128)(2,1)} %fusion.2.refs_0_), channel_id=1, source_target_pairs={{0,2},{1,3},{2,0},{3,1},{4,6},{5,7},{6,4},{7,5},{8,10},{9,11},{10,... | collective-permute-start | bytes 6291464 | tf_op jit(solution)/shard_map/ppermute | solution.py:38
  17.9 51.6 %collective-permute-start.2 = (bf16[2,256,2048]{2,1,0:T(8,128)(2,1)}, bf16[2,256,2048]{2,1,0:T(8,128)(2,1)}, u32[]{:S(2)}, u32[]{:S(2)}) collective-permute-start(bf16[2,256,2048]{2,1,0:T(8,128)(2,1)} %fusion.2.refs_0_), channel_id=1, source_target_pairs={{0,1},{1,0},{2,3},{3,2},{4,5},{5,4},{6,7},{7,6},{8,9},{9,8},{10,11... | collective-permute-start | bytes 6291464 | tf_op jit(solution)/shard_map/ppermute | solution.py:38
  18.7 121.4 %all-gather.10.cloned.1.call-start = ((), (), s32[]{:S(2)}) async-start(), calls=%async_computation.7 | async-start | bytes 1310720 | tf_op jit(solution)/shard_map/all_gather | solution.py:410
  63.9 233.4 %all-gather.12.cloned.1.call-start = ((), (), s32[]{:S(2)}) async-start(), calls=%async_computation.8 | async-start | bytes 10485760 | tf_op jit(solution)/shard_map/all_gather | solution.py:410
  66.7 37.5 %collective-permute-start.4 = (bf16[1536,512]{1,0:T(8,128)(2,1)}, bf16[1536,512]{1,0:T(8,128)(2,1)}, u32[]{:S(2)}, u32[]{:S(2)}) collective-permute-start(bf16[1536,512]{1,0:T(8,128)(2,1)} %pad_maximum_fusion.3), channel_id=1, source_target_pairs={{0,16},{16,0},{1,17},{17,1},{2,18},{18,2},{3,19},{19,3},{4,20},{20... | collective-permute-start | bytes 4718600 | tf_op jit(solution)/shard_map/ppermute | solution.py:46
  67.1 328.9 %all-gather.14.cloned.1.call-start = ((), (), s32[]{:S(2)}) async-start(), calls=%async_computation.9 | async-start | bytes 5242880 | tf_op jit(solution)/shard_map/all_gather | solution.py:410
  67.4 57.9 %collective-permute-start.6 = (bf16[2,256,2048]{2,1,0:T(8,128)(2,1)}, bf16[2,256,2048]{2,1,0:T(8,128)(2,1)}, u32[]{:S(2)}, u32[]{:S(2)}) collective-permute-start(bf16[2,256,2048]{2,1,0:T(8,128)(2,1)} %refs_0_.1), channel_id=1, source_target_pairs={{0,2},{1,3},{2,0},{3,1},{4,6},{5,7},{6,4},{7,5},{8,10},{9,11},{10,... | collective-permute-start | bytes 6291464 | tf_op jit(solution)/shard_map/ppermute | solution.py:38
  69.2 111.9 %collective-permute-start.10 = (bf16[2,256,2048]{2,1,0:T(8,128)(2,1)}, bf16[2,256,2048]{2,1,0:T(8,128)(2,1)}, u32[]{:S(2)}, u32[]{:S(2)}) collective-permute-start(bf16[2,256,2048]{2,1,0:T(8,128)(2,1)} %collective-permute-done.1.refs_1_), channel_id=1, source_target_pairs={{0,2},{1,3},{2,0},{3,1},{4,6},{5,7},{6,4},{7,5},{8,10},{9,11},{10,... | collective-permute-start | bytes 6291464 | tf_op jit(solution)/shard_map/ppermute | solution.py:38
  88.9 36.4 %collective-permute-start.5 = (bf16[1536,256]{1,0:T(8,128)(2,1)S(1)}, bf16[1536,256]{1,0:T(8,128)(2,1)S(1)}, u32[]{:S(2)}, u32[]{:S(2)}) collective-permute-start(bf16[1536,256]{1,0:T(8,128)(2,1)S(1)} %pad_maximum_fusion.4), channel_id=1, source_target_pairs={{0,16},{16,0},{1,17},{17,1},{2,18},{18,2},{3,19},{19,3},{4,20},{20... | collective-permute-start | bytes 2359304 | tf_op jit(solution)/shard_map/ppermute | solution.py:46
  141.3 35.1 %collective-permute-start.11 = (bf16[1536,256]{1,0:T(8,128)(2,1)S(1)}, bf16[1536,256]{1,0:T(8,128)(2,1)S(1)}, u32[]{:S(2)}, u32[]{:S(2)}) collective-permute-start(bf16[1536,256]{1,0:T(8,128)(2,1)S(1)} %pad_maximum_fusion.5), channel_id=1, source_target_pairs={{0,16},{16,0},{1,17},{17,1},{2,18},{18,2},{3,19},{19,3},{4,20},{20... | collective-permute-start | bytes 2359304 | tf_op jit(solution)/shard_map/ppermute | solution.py:46
  153.2 28.0 %collective-permute-start.7 = (bf16[8,129,128]{2,1,0:T(8,128)(2,1)S(1)}, bf16[8,129,128]{2,1,0:T(8,128)(2,1)S(1)}, u32[]{:S(2)}, u32[]{:S(2)}) collective-permute-start(bf16[8,129,128]{2,1,0:T(8,128)(2,1)S(1)} %maximum_maximum_fusion), channel_id=1, source_target_pairs={{0,4},{4,8},{8,12},{1,5},{5,9},{9,13},{2,6},{6,10},{10,14},{3,7},{... | collective-permute-start | bytes 792584 | tf_op jit(solution)/shard_map/ppermute | solution.py:390
  161.2 31.9 %collective-permute-start.9 = (bf16[8,129,128]{2,1,0:T(8,128)(2,1)S(1)}, bf16[8,129,128]{2,1,0:T(8,128)(2,1)S(1)}, u32[]{:S(2)}, u32[]{:S(2)}) collective-permute-start(bf16[8,129,128]{2,1,0:T(8,128)(2,1)S(1)} %maximum_maximum_fusion), channel_id=1, source_target_pairs={{0,12},{1,13},{2,14},{3,15},{16,28},{17,29},{18,30},{19,31}} | collective-permute-start | bytes 792584 | tf_op jit(solution)/shard_map/ppermute | solution.py:390
  248.5 48.7 %collective-permute-start.17 = (bf16[1,256,2048]{2,1,0:T(8,128)(2,1)}, bf16[1,256,2048]{2,1,0:T(8,128)(2,1)}, u32[]{:S(2)}, u32[]{:S(2)}) collective-permute-start(bf16[1,256,2048]{2,1,0:T(8,128)(2,1)} %bitcast.7.refs_0_), channel_id=1, source_target_pairs={{0,16},{16,0},{1,17},{17,1},{2,18},{18,2},{3,19},{19,3},{4,20},{20... | collective-permute-start | bytes 3145736 | tf_op jit(solution)/shard_map/ppermute | solution.py:46
  295.7 328.8 %reduce-scatter.6.cloned.1.call-start = ((), (), s32[]{:S(2)}) async-start(), calls=%async_computation.10 | async-start | bytes 5242880 | tf_op jit(solution)/shard_map/reduce_scatter | solution.py:461
  295.7 45.1 %collective-permute-start.23 = (bf16[1,256,2048]{2,1,0:T(8,128)(2,1)S(1)}, bf16[1,256,2048]{2,1,0:T(8,128)(2,1)}, u32[]{:S(2)}, u32[]{:S(2)}) collective-permute-start(bf16[1,256,2048]{2,1,0:T(8,128)(2,1)S(1)} %bitcast.47), channel_id=1, source_target_pairs={{0,16},{16,0},{1,17},{17,1},{2,18},{18,2},{3,19},{19,3},{4,20},{20... | collective-permute-start | bytes 3145736 | tf_op jit(solution)/shard_map/ppermute | solution.py:46
  296.6 44.8 %collective-permute-start.24 = (bf16[1,256,2048]{2,1,0:T(8,128)(2,1)S(1)}, bf16[1,256,2048]{2,1,0:T(8,128)(2,1)}, u32[]{:S(2)}, u32[]{:S(2)}) collective-permute-start(bf16[1,256,2048]{2,1,0:T(8,128)(2,1)S(1)} %bitcast.48), channel_id=1, source_target_pairs={{0,2},{1,3},{2,0},{3,1},{4,6},{5,7},{6,4},{7,5},{8,10},{9,11},{10,... | collective-permute-start | bytes 3145736 | tf_op jit(solution)/shard_map/ppermute | solution.py:38
  321.4 46.6 %collective-permute-start.26 = (bf16[1,256,2048]{2,1,0:T(8,128)(2,1)S(1)}, bf16[1,256,2048]{2,1,0:T(8,128)(2,1)}, u32[]{:S(2)}, u32[]{:S(2)}) collective-permute-start(bf16[1,256,2048]{2,1,0:T(8,128)(2,1)S(1)} %bitcast.49), channel_id=1, source_target_pairs={{0,1},{1,0},{2,3},{3,2},{4,5},{5,4},{6,7},{7,6},{8,9},{9,8},{10,11... | collective-permute-start | bytes 3145736 | tf_op jit(solution)/shard_map/ppermute | solution.py:38
  341.4 27.1 %collective-permute-start.28 = (bf16[1,256,2048]{2,1,0:T(8,128)(2,1)}, bf16[1,256,2048]{2,1,0:T(8,128)(2,1)}, u32[]{:S(2)}, u32[]{:S(2)}) collective-permute-start(bf16[1,256,2048]{2,1,0:T(8,128)(2,1)} %collective-permute-done.24.refs_2_), channel_id=1, source_target_pairs={{0,1},{1,0},{2,3},{3,2},{4,5},{5,4},{6,7},{7,6},{8,9},{9,8},{10,11... | collective-permute-start | bytes 3145736 | tf_op jit(solution)/shard_map/ppermute | solution.py:38
  367.6 28.5 %collective-permute-start.30 = (bf16[2,256,2048]{2,1,0:T(8,128)(2,1)S(1)}, bf16[2,256,2048]{2,1,0:T(8,128)(2,1)}, u32[]{:S(2)}, u32[]{:S(2)}) collective-permute-start(bf16[2,256,2048]{2,1,0:T(8,128)(2,1)S(1)} %copy-done.31), channel_id=1, source_target_pairs={{0,1},{1,0},{2,3},{3,2},{4,5},{5,4},{6,7},{7,6},{8,9},{9,8},{10,11... | collective-permute-start | bytes 6291464 | tf_op jit(solution)/shard_map/ppermute | solution.py:38
  368.0 28.0 %collective-permute-start.31 = (bf16[2,256,2048]{2,1,0:T(8,128)(2,1)}, bf16[2,256,2048]{2,1,0:T(8,128)(2,1)}, u32[]{:S(2)}, u32[]{:S(2)}) collective-permute-start(bf16[2,256,2048]{2,1,0:T(8,128)(2,1)} %collective-permute-done.1.refs_1_), channel_id=1, source_target_pairs={{0,1},{1,0},{2,3},{3,2},{4,5},{5,4},{6,7},{7,6},{8,9},{9,8},{10,11... | collective-permute-start | bytes 6291464 | tf_op jit(solution)/shard_map/ppermute | solution.py:38
  368.1 28.0 %collective-permute-start.32 = (bf16[2,256,2048]{2,1,0:T(8,128)(2,1)}, bf16[2,256,2048]{2,1,0:T(8,128)(2,1)}, u32[]{:S(2)}, u32[]{:S(2)}) collective-permute-start(bf16[2,256,2048]{2,1,0:T(8,128)(2,1)} %collective-permute-done.6.refs_2_), channel_id=1, source_target_pairs={{0,1},{1,0},{2,3},{3,2},{4,5},{5,4},{6,7},{7,6},{8,9},{9,8},{10,11... | collective-permute-start | bytes 6291464 | tf_op jit(solution)/shard_map/ppermute | solution.py:38
  368.5 27.6 %collective-permute-start.33 = (bf16[2,256,2048]{2,1,0:T(8,128)(2,1)}, bf16[2,256,2048]{2,1,0:T(8,128)(2,1)}, u32[]{:S(2)}, u32[]{:S(2)}) collective-permute-start(bf16[2,256,2048]{2,1,0:T(8,128)(2,1)} %collective-permute-done.10.refs_3_), channel_id=1, source_target_pairs={{0,1},{1,0},{2,3},{3,2},{4,5},{5,4},{6,7},{7,6},{8,9},{9,8},{10,11... | collective-permute-start | bytes 6291464 | tf_op jit(solution)/shard_map/ppermute | solution.py:38
  462.7 51.7 %collective-permute-start.35 = (bf16[512,2048]{1,0:T(8,128)(2,1)}, bf16[512,2048]{1,0:T(8,128)(2,1)S(1)}, u32[]{:S(2)}, u32[]{:S(2)}) collective-permute-start(bf16[512,2048]{1,0:T(8,128)(2,1)} %add_convert_fusion.3), channel_id=1, source_target_pairs={{0,2},{1,3},{2,0},{3,1},{4,6},{5,7},{6,4},{7,5},{8,10},{9,11},{10,... | collective-permute-start | bytes 6291464 | tf_op jit(solution)/shard_map/ppermute | solution.py:38
  514.5 274.8 %reduce-scatter.8.cloned.1.call-start = ((), (), s32[]{:S(2)}) async-start(), calls=%async_computation.11 | async-start | bytes 10485760 | tf_op jit(solution)/shard_map/reduce_scatter | solution.py:461
  523.2 49.2 %collective-permute-start.38 = (bf16[256,2048]{1,0:T(8,128)(2,1)}, bf16[256,2048]{1,0:T(8,128)(2,1)S(1)}, u32[]{:S(2)}, u32[]{:S(2)}) collective-permute-start(bf16[256,2048]{1,0:T(8,128)(2,1)} %slice.380), channel_id=1, source_target_pairs={{0,16},{16,0},{1,17},{17,1},{2,18},{18,2},{3,19},{19,3},{4,20},{20... | collective-permute-start | bytes 3145736 | tf_op jit(solution)/shard_map/ppermute | solution.py:46
  528.1 47.9 %collective-permute-start.37 = (bf16[512,2048]{1,0:T(8,128)(2,1)}, bf16[512,2048]{1,0:T(8,128)(2,1)S(1)}, u32[]{:S(2)}, u32[]{:S(2)}) collective-permute-start(bf16[512,2048]{1,0:T(8,128)(2,1)} %add_convert_fusion.2), channel_id=1, source_target_pairs={{0,2},{1,3},{2,0},{3,1},{4,6},{5,7},{6,4},{7,5},{8,10},{9,11},{10,... | collective-permute-start | bytes 6291464 | tf_op jit(solution)/shard_map/ppermute | solution.py:38
  582.2 262.6 %reduce-scatter.10.cloned.1.call-start = ((), (), s32[]{:S(2)}) async-start(), calls=%async_computation.12 | async-start | bytes 1310720 | tf_op jit(solution)/shard_map/reduce_scatter | solution.py:461
  623.2 38.2 %collective-permute-start.45 = (bf16[1,256,2048]{2,1,0:T(8,128)(2,1)S(1)}, bf16[1,256,2048]{2,1,0:T(8,128)(2,1)}, u32[]{:S(2)}, u32[]{:S(2)}) collective-permute-start(bf16[1,256,2048]{2,1,0:T(8,128)(2,1)S(1)} %bitcast.40), channel_id=1, source_target_pairs={{0,2},{1,3},{2,0},{3,1},{4,6},{5,7},{6,4},{7,5},{8,10},{9,11},{10,... | collective-permute-start | bytes 3145736 | tf_op jit(solution)/shard_map/ppermute | solution.py:38
  661.4 34.2 %collective-permute-start.50 = (bf16[1024,2048]{1,0:T(8,128)(2,1)}, bf16[1024,2048]{1,0:T(8,128)(2,1)}, u32[]{:S(2)}, u32[]{:S(2)}) collective-permute-start(bf16[1024,2048]{1,0:T(8,128)(2,1)} %get-tuple-element.1212), channel_id=1, source_target_pairs={{0,1},{1,0},{2,3},{3,2},{4,5},{5,4},{6,7},{7,6},{8,9},{9,8},{10,11... | collective-permute-start | bytes 12582920 | tf_op jit(solution)/shard_map/ppermute | solution.py:38
  662.0 61.7 %collective-permute-start.48 = (bf16[512,1024]{1,0:T(8,128)(2,1)}, bf16[512,1024]{1,0:T(8,128)(2,1)}, u32[]{:S(2)}, u32[]{:S(2)}) collective-permute-start(bf16[512,1024]{1,0:T(8,128)(2,1)} %reduce-scatter.6.cloned.1.call-done), channel_id=1, source_target_pairs={{0,16},{16,0},{1,17},{17,1},{2,18},{18,2},{3,19},{19,3},{4,20},{20... | collective-permute-start | bytes 3145736 | tf_op jit(solution)/shard_map/ppermute | solution.py:46
  662.4 85.5 %collective-permute-start.44 = (bf16[512,2048]{1,0:T(8,128)(2,1)}, bf16[512,2048]{1,0:T(8,128)(2,1)}, u32[]{:S(2)}, u32[]{:S(2)}) collective-permute-start(bf16[512,2048]{1,0:T(8,128)(2,1)} %add_convert_fusion.1), channel_id=1, source_target_pairs={{0,2},{1,3},{2,0},{3,1},{4,6},{5,7},{6,4},{7,5},{8,10},{9,11},{10,... | collective-permute-start | bytes 6291464 | tf_op jit(solution)/shard_map/ppermute | solution.py:38
  700.1 55.7 %collective-permute-start.55 = (bf16[512,2048]{1,0:T(8,128)(2,1)}, bf16[512,2048]{1,0:T(8,128)(2,1)}, u32[]{:S(2)}, u32[]{:S(2)}) collective-permute-start(bf16[512,2048]{1,0:T(8,128)(2,1)} %add_convert_fusion), channel_id=1, source_target_pairs={{0,2},{1,3},{2,0},{3,1},{4,6},{5,7},{6,4},{7,5},{8,10},{9,11},{10,... | collective-permute-start | bytes 6291464 | tf_op jit(solution)/shard_map/ppermute | solution.py:38
  702.2 70.6 %collective-permute-start.52 = (bf16[8,129,128]{2,1,0:T(8,128)(2,1)S(1)}, bf16[8,129,128]{2,1,0:T(8,128)(2,1)}, u32[]{:S(2)}, u32[]{:S(2)}) collective-permute-start(bf16[8,129,128]{2,1,0:T(8,128)(2,1)S(1)} %maximum_maximum_fusion.1), channel_id=1, source_target_pairs={{4,0},{8,4},{12,8},{5,1},{9,5},{13,9},{6,2},{10,6},{14,10},{7,3},{... | collective-permute-start | bytes 792584 | tf_op jit(solution)/shard_map/ppermute | solution.py:390
  722.4 55.8 %collective-permute-start.53 = (bf16[8,129,128]{2,1,0:T(8,128)(2,1)S(1)}, bf16[8,129,128]{2,1,0:T(8,128)(2,1)}, u32[]{:S(2)}, u32[]{:S(2)}) collective-permute-start(bf16[8,129,128]{2,1,0:T(8,128)(2,1)S(1)} %maximum_maximum_fusion.1), channel_id=1, source_target_pairs={{8,0},{12,4},{9,1},{13,5},{10,2},{14,6},{11,3},{15,7},{24,16},{28,... | collective-permute-start | bytes 792584 | tf_op jit(solution)/shard_map/ppermute | solution.py:390
  723.7 54.5 %collective-permute-start.54 = (bf16[8,129,128]{2,1,0:T(8,128)(2,1)S(1)}, bf16[8,129,128]{2,1,0:T(8,128)(2,1)}, u32[]{:S(2)}, u32[]{:S(2)}) collective-permute-start(bf16[8,129,128]{2,1,0:T(8,128)(2,1)S(1)} %maximum_maximum_fusion.1), channel_id=1, source_target_pairs={{12,0},{13,1},{14,2},{15,3},{28,16},{29,17},{30,18},{31,19}} | collective-permute-start | bytes 792584 | tf_op jit(solution)/shard_map/ppermute | solution.py:390
  789.4 144.8 %reduce-scatter.14.cloned.1.call-start = ((), (), s32[]{:S(2)}) async-start(), calls=%async_computation.14 | async-start | bytes 2621440 | tf_op jit(solution)/shard_map/reduce_scatter | solution.py:461
  793.0 148.1 %reduce-scatter.12.cloned.1.call-start = ((), (), s32[]{:S(2)}) async-start(), calls=%async_computation.13 | async-start | bytes 2621440 | tf_op jit(solution)/shard_map/reduce_scatter | solution.py:461
  816.5 46.4 %collective-permute-start.60 = (bf16[2048,512]{1,0:T(8,128)(2,1)}, bf16[2048,512]{1,0:T(8,128)(2,1)}, u32[]{:S(2)}, u32[]{:S(2)}) collective-permute-start(bf16[2048,512]{1,0:T(8,128)(2,1)} %shard_map.262), channel_id=1, source_target_pairs={{0,16},{16,0},{1,17},{17,1},{2,18},{18,2},{3,19},{19,3},{4,20},{20... | collective-permute-start | bytes 6291464 | tf_op jit(solution)/shard_map/ppermute | solution.py:46
  830.9 43.3 %collective-permute-start.59 = (bf16[512,2048]{1,0:T(8,128)(2,1)}, bf16[512,2048]{1,0:T(8,128)(2,1)}, u32[]{:S(2)}, u32[]{:S(2)}) collective-permute-start(bf16[512,2048]{1,0:T(8,128)(2,1)} %get-tuple-element.1358), channel_id=1, source_target_pairs={{0,1},{1,0},{2,3},{3,2},{4,5},{5,4},{6,7},{7,6},{8,9},{9,8},{10,11... | collective-permute-start | bytes 6291464 | tf_op jit(solution)/shard_map/ppermute | solution.py:38
  844.1 36.0 %collective-permute-start.58 = (bf16[512,2048]{1,0:T(8,128)(2,1)}, bf16[512,2048]{1,0:T(8,128)(2,1)}, u32[]{:S(2)}, u32[]{:S(2)}) collective-permute-start(bf16[512,2048]{1,0:T(8,128)(2,1)} %get-tuple-element.1356), channel_id=1, source_target_pairs={{0,1},{1,0},{2,3},{3,2},{4,5},{5,4},{6,7},{7,6},{8,9},{9,8},{10,11... | collective-permute-start | bytes 6291464 | tf_op jit(solution)/shard_map/ppermute | solution.py:38
  879.0 50.0 %collective-permute-start.56 = (bf16[256,2048]{1,0:T(8,128)(2,1)}, bf16[256,2048]{1,0:T(8,128)(2,1)}, u32[]{:S(2)}, u32[]{:S(2)}) collective-permute-start(bf16[256,2048]{1,0:T(8,128)(2,1)} %slice.377), channel_id=1, source_target_pairs={{0,16},{16,0},{1,17},{17,1},{2,18},{18,2},{3,19},{19,3},{4,20},{20... | collective-permute-start | bytes 3145736 | tf_op jit(solution)/shard_map/ppermute | solution.py:46
  887.2 36.3 %collective-permute-start.61 = (bf16[256,2048]{1,0:T(8,128)(2,1)S(1)}, bf16[256,2048]{1,0:T(8,128)(2,1)S(1)}, u32[]{:S(2)}, u32[]{:S(2)}) collective-permute-start(bf16[256,2048]{1,0:T(8,128)(2,1)S(1)} %add_convert_fusion.6), channel_id=1, source_target_pairs={{0,2},{1,3},{2,0},{3,1},{4,6},{5,7},{6,4},{7,5},{8,10},{9,11},{10,... | collective-permute-start | bytes 3145736 | tf_op jit(solution)/shard_map/ppermute | solution.py:38
  887.3 53.8 %collective-permute-start.66 = (bf16[512,1024]{1,0:T(8,128)(2,1)S(1)}, bf16[512,1024]{1,0:T(8,128)(2,1)}, u32[]{:S(2)}, u32[]{:S(2)}) collective-permute-start(bf16[512,1024]{1,0:T(8,128)(2,1)S(1)} %get-tuple-element.1441), channel_id=1, source_target_pairs={{0,16},{16,0},{1,17},{17,1},{2,18},{18,2},{3,19},{19,3},{4,20},{20... | collective-permute-start | bytes 3145736 | tf_op jit(solution)/shard_map/ppermute | solution.py:46
  929.1 46.4 %collective-permute-start.71 = (bf16[512,256]{1,0:T(8,128)(2,1)S(1)}, bf16[512,256]{1,0:T(8,128)(2,1)}, u32[]{:S(2)}, u32[]{:S(2)}) collective-permute-start(bf16[512,256]{1,0:T(8,128)(2,1)S(1)} %copy-done.54), channel_id=1, source_target_pairs={{0,16},{16,0},{1,17},{17,1},{2,18},{18,2},{3,19},{19,3},{4,20},{20... | collective-permute-start | bytes 786440 | tf_op jit(solution)/shard_map/ppermute | solution.py:46
  934.2 32.7 %collective-permute-start.67 = (bf16[512,512]{1,0:T(8,128)(2,1)}, bf16[512,512]{1,0:T(8,128)(2,1)}, u32[]{:S(2)}, u32[]{:S(2)}) collective-permute-start(bf16[512,512]{1,0:T(8,128)(2,1)} %reduce-scatter.14.cloned.1.call-done), channel_id=1, source_target_pairs={{0,16},{16,0},{1,17},{17,1},{2,18},{18,2},{3,19},{19,3},{4,20},{20... | collective-permute-start | bytes 1572872 | tf_op jit(solution)/shard_map/ppermute | solution.py:46
  (107 other events, 1331.0 us)
Sparse Core Ops, SparseCore 0:
  10.2 48.6 all-gather.5
  61.0 26.6 all-gather.7
  89.2 27.4 all-gather.9
  118.1 162.7 all-gather.11
  295.8 98.2 all-gather.13
  514.6 94.5 reduce-scatter.5
  611.7 162.6 reduce-scatter.7
  789.5 45.2 reduce-scatter.9
  837.1 42.4 reduce-scatter.13
  882.4 58.6 reduce-scatter.11

commit v4 on v3

--- a/solution.py
+++ b/solution.py
@@ -1150,13 +1150,13 @@
     pair_grad, small = line.hold((pair_grad, small))
     pair_rest = grp_swap(pair_grad)
     up_out = line(whole_columns, up_grad, up_rest)
-    small = add_small(small, *small_steps[-3])
     output_rows = [
         line(
             lambda r, own, far: (r + added(own, far)).astype(jnp.bfloat16), resid[m], *feed_parts[m]
         )
         for m in micros
     ]
+    small = add_small(line.hold(small), *small_steps[-3])
     small = add_small(small, *small_steps[-2])
     query_grad = line(whole_sum, query_sum, query_rest)
     small = add_small(small, *small_steps[-1])

time: 994 us -> 996 us (level)
  no operation moved by 1% of the time
where the time goes in v4:
time: 996 us; the launch traced here: 988 us
  Pallas kernels  467 us (47%)
  waiting for transfers between devices  242 us (24%)
  other arithmetic  107 us (11%)
  starting transfers between devices  72.5 us (7%)
  local copies, waits for them, and re-layouts  57 us (6%)
  matrix products  26 us (3%)
  between operations  16.9 us (2%)
    pallas_call x8, Pallas kernels, products_cut(): pl.pallas_call(kernel, grid_spec=pltpu.PrefetchScalarGridSpec(num_scalar_...  125 us
    pallas_call x7, Pallas kernels, grad_product(): pl.pallas_call(kernel, grid=(width // block,), in_specs=[pl.BlockSpec((to...  118 us
    pallas_call x12, Pallas kernels, head_call(): pl.pallas_call(kernel, grid=(heads[0],), in_specs=[spec(a.shape, kind) fo...  111 us
    ppermute x42, waiting for transfers between devices, tok_swap(): return lax.ppermute(value, 'tok', [(k, k ^ bit) for k in range(count)])  104 us
    ppermute x19, waiting for transfers between devices, grp_swap(): return lax.ppermute(value, 'grp', [(0, 1), (1, 0)])  99.9 us
    pallas_call x4, Pallas kernels, over_pieces(): pl.pallas_call(kernel, grid=(total // block,), in_specs=[any_space()] * l...  86.1 us
    dot_general x6, matrix products, times(): return jnp.dot(left, right, preferred_element_type=jnp.float32)  26 us
    convert_element_type x8, other arithmetic, cut(): sum((term[rows // 2:rows].astype(jnp.float32) for term in terms))  24.7 us
  transfers between devices with their start and end apart: 82, of which 28 were waited for; matrix products, arithmetic and copies ran while one was open for 17% of the time, Pallas kernels for 43%

profile of v4, /device:TPU:0, one launch (start us, length us, event | category | flops | bytes accessed | tf_op | source)
XLA Modules:
  0.0 988.0 jit_solution(4609076780227117848)
XLA Ops:
  27.5 30.8 %collective-permute-done.1.refs_1_ = bf16[2,256,2048]{2,1,0:T(8,128)(2,1)} collective-permute-done((bf16[2,256,2048]{2,1,0:T(8,128)(2,1)}, bf16[2,256,2048]{2,1,0:T(8,128)(2,1)}, u32[]{:S(2)}, u32[]{:S(2)}) %collective-permute-start.1) | collective-permute-done | bytes 2097184 | tf_op jit(solution)/shard_map/ppermute | solution.py:46
  58.4 5.5 collective-permute-done.refs_1_
  70.8 6.5 shard_map.229
  77.3 10.3 %all-gather.8.cloned.1.call-done.mine_ref = bf16[2048,256]{1,0:T(8,128)(2,1)} async-done(((bf16[512,256]{1,0:T(8,128)(2,1)}), bf16[2048,256]{1,0:T(8,128)(2,1)}) %all-gather.8.cloned.1.call-update) | async-done | bytes 1048592 | tf_op jit(solution)/shard_map/all_gather | solution.py:410
  90.4 6.3 fusion.33
  96.7 7.5 collective-permute-done.4.got_ref
  109.0 6.3 convolution_convert_fusion.2.key_ref
  130.3 6.4 convolution_convert_fusion.value_ref
  163.7 12.5 %shard_map.234 = (f32[1024,512]{1,0:T(8,128)}, f32[4,1024,1]{2,1,0:T(8,128)}) custom-call(s32[1]{0:T(128)} %bitcast.5.first_ref, bf16[1024,512]{1,0:T(8,128)(2,1)} %convolution_convert_fusion.5.query_ref, bf16[1024,512]{1,0:T(8,128)(2,1)} %convolution_convert_fusion.3.key_ref, bf16[1024,512]{1,0:T(8,128)(2,1)} %convolution_convert_fusion.1.value_ref), custom_call_target="tpu_custom_call" | custom-call | flops 1744830464 | bytes 5259264 | tf_op jit(solution)/shard_map/pallas_call | solution.py:525
  181.6 11.4 %collective-permute-done.9 = bf16[8,129,128]{2,1,0:T(8,128)(2,1)S(1)} collective-permute-done((bf16[8,129,128]{2,1,0:T(8,128)(2,1)S(1)}, bf16[8,129,128]{2,1,0:T(8,128)(2,1)S(1)}, u32[]{:S(2)}, u32[]{:S(2)}) %collective-permute-start.9) | collective-permute-done | bytes 264224 | tf_op jit(solution)/shard_map/ppermute | solution.py:390
  198.9 7.5 shard_map.237
  215.3 12.2 %shard_map.238 = (f32[1024,512]{1,0:T(8,128)}, f32[4,1024,1]{2,1,0:T(8,128)}) custom-call(s32[1]{0:T(128)} %bitcast.6.first_ref, bf16[1024,512]{1,0:T(8,128)(2,1)} %convolution_convert_fusion.4.query_ref, bf16[1024,512]{1,0:T(8,128)(2,1)} %convolution_convert_fusion.2.key_ref, bf16[1024,512]{1,0:T(8,128)(2,1)} %convolution_convert_fusion.value_ref), custom_call_target="tpu_custom_call" | custom-call | flops 1744830464 | bytes 5259264 | tf_op jit(solution)/shard_map/pallas_call | solution.py:525
  231.8 7.5 shard_map.240
  249.5 20.0 %collective-permute-done.15 = bf16[256,2048]{1,0:T(8,128)(2,1)S(1)} collective-permute-done((bf16[256,2048]{1,0:T(8,128)(2,1)S(1)}, bf16[256,2048]{1,0:T(8,128)(2,1)S(1)}, u32[]{:S(2)}, u32[]{:S(2)}) %collective-permute-start.15) | collective-permute-done | bytes 1048608 | tf_op jit(solution)/shard_map/ppermute | solution.py:38
  272.4 21.9 %collective-permute-done.16.refs_2_ = bf16[1,256,2048]{2,1,0:T(8,128)(2,1)} collective-permute-done((bf16[1,256,2048]{2,1,0:T(8,128)(2,1)}, bf16[1,256,2048]{2,1,0:T(8,128)(2,1)}, u32[]{:S(2)}, u32[]{:S(2)}) %collective-permute-start.16) | collective-permute-done | bytes 1048608 | tf_op jit(solution)/shard_map/ppermute | solution.py:38
  297.1 23.6 %collective-permute-done.18.refs_3_ = bf16[1,256,2048]{2,1,0:T(8,128)(2,1)} collective-permute-done((bf16[1,256,2048]{2,1,0:T(8,128)(2,1)}, bf16[1,256,2048]{2,1,0:T(8,128)(2,1)}, u32[]{:S(2)}, u32[]{:S(2)}) %collective-permute-start.18) | collective-permute-done | bytes 1048608 | tf_op jit(solution)/shard_map/ppermute | solution.py:46
  321.3 19.3 %collective-permute-done.23.refs_1_ = bf16[1,256,2048]{2,1,0:T(8,128)(2,1)} collective-permute-done((bf16[1,256,2048]{2,1,0:T(8,128)(2,1)S(1)}, bf16[1,256,2048]{2,1,0:T(8,128)(2,1)}, u32[]{:S(2)}, u32[]{:S(2)}) %collective-permute-start.23) | collective-permute-done | bytes 1048608 | tf_op jit(solution)/shard_map/ppermute | solution.py:46
  341.7 25.5 %shard_map.241 = (bf16[2048,2048]{1,0:T(8,128)(2,1)}, bf16[2048,2048]{1,0:T(8,128)(2,1)}, bf16[2048,1024]{1,0:T(8,128)(2,1)}) custom-call(bf16[1,256,2048]{2,1,0:T(8,128)(2,1)} %bitcast.7.refs_0_, bf16[1,256,2048]{2,1,0:T(8,128)(2,1)} %collective-permute-done.17.refs_1_, bf16[1,256,2048]{2,1,0:T(8,128)(2,1)} %collective-permute-done.16.refs_2_, ...), custom_call_target="tpu_custom_call" | custom-call | flops 17179869184 | bytes 29360128 | tf_op jit(solution)/shard_map/pallas_call | solution.py:223
  370.9 24.9 %shard_map.242 = (bf16[2048,2048]{1,0:T(8,128)(2,1)}, bf16[2048,2048]{1,0:T(8,128)(2,1)}, bf16[2048,1024]{1,0:T(8,128)(2,1)}) custom-call(bf16[1,256,2048]{2,1,0:T(8,128)(2,1)} %bitcast.50, bf16[1,256,2048]{2,1,0:T(8,128)(2,1)} %collective-permute-done.23.refs_1_, bf16[1,256,2048]{2,1,0:T(8,128)(2,1)} %collective-permute-done.24.refs_2_, ...), custom_call_target="tpu_custom_call" | custom-call | flops 17179869184 | bytes 29360128 | tf_op jit(solution)/shard_map/pallas_call | solution.py:223
  395.9 17.7 %shard_map.243 = (bf16[2048,2048]{1,0:T(8,128)(2,1)}, bf16[2048,2048]{1,0:T(8,128)(2,1)}) custom-call(bf16[2,256,2048]{2,1,0:T(8,128)(2,1)} %refs_0_.1, bf16[2,256,2048]{2,1,0:T(8,128)(2,1)} %collective-permute-done.1.refs_1_, bf16[2,256,2048]{2,1,0:T(8,128)(2,1)} %collective-permute-done.6.refs_2_, bf16[2,256,2048]{2,1,0:T(8,128)(2,1)} %collective-permute-done.10.refs_3_, ...), custom_call_target="tpu_custom_call" | custom-call | flops 8589934592 | bytes 29360128 | tf_op jit(solution)/shard_map/pallas_call | solution.py:223
  414.2 25.8 %shard_map.244 = (bf16[1024,2048]{1,0:T(8,128)(2,1)}, bf16[1024,2048]{1,0:T(8,128)(2,1)}) custom-call(s32[8]{0:T(128)} %iota.20.order_ref, bf16[2048,2048]{1,0:T(8,128)(2,1)} %get-tuple-element.1088.refs_0_.refs_2_, bf16[2048,2048]{1,0:T(8,128)(2,1)} %all-gather.12.cloned.1.call-done.refs_8_.refs_1_), custom_call_target="tpu_custom_call" | custom-call | flops 17179869184 | bytes 25165824 | tf_op jit(solution)/shard_map/pallas_call | solution.py:310
  440.1 17.9 %shard_map.245 = (bf16[2048,2048]{1,0:T(8,128)(2,1)}, bf16[2048,2048]{1,0:T(8,128)(2,1)}) custom-call(bf16[2,256,2048]{2,1,0:T(8,128)(2,1)} %refs_0_.1, bf16[2,256,2048]{2,1,0:T(8,128)(2,1)} %collective-permute-done.1.refs_1_, bf16[2,256,2048]{2,1,0:T(8,128)(2,1)} %collective-permute-done.6.refs_2_, bf16[2,256,2048]{2,1,0:T(8,128)(2,1)} %collective-permute-done.10.refs_3_, ...), custom_call_target="tpu_custom_call" | custom-call | flops 8589934592 | bytes 29360128 | tf_op jit(solution)/shard_map/pallas_call | solution.py:223
  464.0 23.9 %shard_map.246 = bf16[2048,1024]{1,0:T(8,128)(2,1)} custom-call(bf16[2048,2048]{1,0:T(8,128)(2,1)} %get-tuple-element.1055.refs_0_, bf16[2048,2048]{1,0:T(8,128)(2,1)} %get-tuple-element.1056.refs_1_, bf16[2048,1024]{1,0:T(8,128)(2,1)} %get-tuple-element.1113.refs_2_.refs_0_, bf16[2048,1024]{1,0:T(8,128)(2,1)} %get-tuple-element.1169.refs_3_.refs_0_), custom_call_target="tpu_custom_call" | custom-call | flops 17179869184 | bytes 29360128 | tf_op jit(solution)/shard_map/pallas_call | solution.py:371
  488.4 25.7 %shard_map.247 = (bf16[1024,2048]{1,0:T(8,128)(2,1)}, bf16[1024,2048]{1,0:T(8,128)(2,1)}) custom-call(s32[8]{0:T(128)} %iota.21.order_ref, bf16[2048,2048]{1,0:T(8,128)(2,1)} %get-tuple-element.1089.refs_0_.refs_3_, bf16[2048,2048]{1,0:T(8,128)(2,1)} %all-gather.12.cloned.1.call-done.refs_8_.refs_1_), custom_call_target="tpu_custom_call" | custom-call | flops 17179869184 | bytes 25165824 | tf_op jit(solution)/shard_map/pallas_call | solution.py:310
  528.4 43.8 %shard_map.248 = bf16[2048,2048]{1,0:T(8,128)(2,1)} custom-call(bf16[2048,2048]{1,0:T(8,128)(2,1)} %get-tuple-element.1086.refs_0_, bf16[2048,2048]{1,0:T(8,128)(2,1)} %get-tuple-element.1087.refs_1_, bf16[2048,2048]{1,0:T(8,128)(2,1)} %get-tuple-element.1088.refs_0_.refs_2_, bf16[2048,2048]{1,0:T(8,128)(2,1)} %get-tuple-element.1089.refs_0_.refs_3_), custom_call_target="tpu_custom_call" | custom-call | flops 34359738368 | bytes 41943040 | tf_op jit(solution)/shard_map/pallas_call | solution.py:371
  590.9 16.1 %shard_map.249 = (bf16[1024,2048]{1,0:T(8,128)(2,1)}, bf16[1024,2048]{1,0:T(8,128)(2,1)}) custom-call(s32[8]{0:T(128)} %iota.19.order_ref, bf16[2048,1024]{1,0:T(8,128)(2,1)} %get-tuple-element.1113.refs_2_.refs_0_, bf16[2048,1024]{1,0:T(8,128)(2,1)} %all-gather.14.cloned.1.call-done.refs_8_.refs_1_), custom_call_target="tpu_custom_call" | custom-call | flops 8589934592 | bytes 16777216 | tf_op jit(solution)/shard_map/pallas_call | solution.py:310
  607.1 6.6 collective-permute-done.40.refs_1_
  629.5 10.8 %shard_map.251 = (f32[4,1,128]{2,1,0:T(1,128)}, bf16[1024,512]{1,0:T(8,128)(2,1)}, f32[1024,512]{1,0:T(8,128)}, f32[4,128,128]{2,1,0:T(8,128)}, f32[4,1,128]{2,1,0:T(1,128)}) custom-call(f32[4]{0:T(128)} %add_divide_fusion.share_ref, bf16[1024,2048]{1,0:T(8,128)(2,1)} %shard_map.250.grad_ref.refs_0_, bf16[2048,512]{1,0:T(8,128)(2,1)} %shard_map.235.refs_1_.weight_ref, ...), custom_call_target="tpu_custom_call" | custom-call | flops 2550136832 | bytes 13113344 | tf_op jit(solution)/shard_map/pallas_call | solution.py:525
  645.3 15.8 %shard_map.252 = (bf16[1024,2048]{1,0:T(8,128)(2,1)}, bf16[1024,2048]{1,0:T(8,128)(2,1)}) custom-call(s32[8]{0:T(128)} %iota.22.order_ref, bf16[2048,1024]{1,0:T(8,128)(2,1)} %get-tuple-element.1169.refs_3_.refs_0_, bf16[2048,1024]{1,0:T(8,128)(2,1)} %all-gather.14.cloned.1.call-done.refs_8_.refs_1_), custom_call_target="tpu_custom_call" | custom-call | flops 8589934592 | bytes 16777216 | tf_op jit(solution)/shard_map/pallas_call | solution.py:310
  663.5 5.9 collective-permute-done.46.refs_2_
  675.2 11.0 %shard_map.254 = (f32[4,1,128]{2,1,0:T(1,128)}, bf16[1024,512]{1,0:T(8,128)(2,1)}, f32[1024,512]{1,0:T(8,128)}, f32[4,128,128]{2,1,0:T(8,128)}, f32[4,1,128]{2,1,0:T(1,128)}) custom-call(f32[4]{0:T(128)} %add_divide_fusion.share_ref, bf16[1024,2048]{1,0:T(8,128)(2,1)} %shard_map.253.grad_ref.refs_1_, bf16[2048,512]{1,0:T(8,128)(2,1)} %shard_map.235.refs_1_.weight_ref, ...), custom_call_target="tpu_custom_call" | custom-call | flops 2550136832 | bytes 13113344 | tf_op jit(solution)/shard_map/pallas_call | solution.py:525
  686.2 8.9 shard_map.255
  702.7 18.9 %shard_map.256 = (bf16[1024,512]{1,0:T(8,128)(2,1)}, f32[1024,512]{1,0:T(8,128)}, f32[1024,512]{1,0:T(8,128)}) custom-call(s32[1]{0:T(128)} %bitcast.14.first_ref, bf16[1024,512]{1,0:T(8,128)(2,1)} %convolution_convert_fusion.5.query_ref, bf16[1024,512]{1,0:T(8,128)(2,1)} %convolution_convert_fusion.3.key_ref, ...), custom_call_target="tpu_custom_call" | custom-call | flops 4362076160 | bytes 11550720 | tf_op jit(solution)/shard_map/pallas_call | solution.py:525
  728.6 18.6 %shard_map.257 = (bf16[1024,512]{1,0:T(8,128)(2,1)}, f32[1024,512]{1,0:T(8,128)}, f32[1024,512]{1,0:T(8,128)}) custom-call(s32[1]{0:T(128)} %bitcast.15.first_ref, bf16[1024,512]{1,0:T(8,128)(2,1)} %convolution_convert_fusion.4.query_ref, bf16[1024,512]{1,0:T(8,128)(2,1)} %convolution_convert_fusion.2.key_ref, ...), custom_call_target="tpu_custom_call" | custom-call | flops 4362076160 | bytes 11550720 | tf_op jit(solution)/shard_map/pallas_call | solution.py:525
  761.9 10.5 %shard_map.258 = bf16[2048,512]{1,0:T(8,128)(2,1)} custom-call(bf16[1024,2048]{1,0:T(8,128)(2,1)} %get-tuple-element.1366.refs_0_, bf16[1024,2048]{1,0:T(8,128)(2,1)} %get-tuple-element.1367.refs_1_, bf16[1024,512]{1,0:T(8,128)(2,1)} %get-tuple-element.1338.refs_2_.refs_0_, bf16[1024,512]{1,0:T(8,128)(2,1)} %get-tuple-element.1348.refs_3_.refs_0_), custom_call_target="tpu_custom_call" | custom-call | flops 4294967296 | bytes 12582912 | tf_op jit(solution)/shard_map/pallas_call | solution.py:371
  772.4 5.5 collective-permute-done.53
  779.9 9.1 shard_map.259
  795.0 5.3 shard_map.260
  800.3 5.2 shard_map.261
  805.5 10.6 %shard_map.262 = bf16[2048,512]{1,0:T(8,128)(2,1)} custom-call(bf16[1024,2048]{1,0:T(8,128)(2,1)} %get-tuple-element.1366.refs_0_, bf16[1024,2048]{1,0:T(8,128)(2,1)} %get-tuple-element.1367.refs_1_, bf16[1024,512]{1,0:T(8,128)(2,1)} %get-tuple-element.1368.refs_2_.refs_1_, bf16[1024,512]{1,0:T(8,128)(2,1)} %get-tuple-element.1369.refs_3_.refs_1_, ...), custom_call_target="tpu_custom_call" | custom-call | flops 4294967296 | bytes 14680064 | tf_op jit(solution)/shard_map/pallas_call | solution.py:371
  817.5 13.1 %shard_map.263 = (bf16[512,2048]{1,0:T(8,128)(2,1)}, bf16[512,2048]{1,0:T(8,128)(2,1)}) custom-call(s32[4]{0:T(128)} %broadcast_xor_fusion.order_ref, bf16[1024,512]{1,0:T(8,128)(2,1)} %get-tuple-element.1338.refs_2_.refs_0_, bf16[1024,512]{1,0:T(8,128)(2,1)} %get-tuple-element.1368.refs_2_.refs_1_, bf16[1024,512]{1,0:T(8,128)(2,1)} %get-tuple-element.1370.refs_4_.refs_2_, ...), custom_call_target="tpu_custom_call" | custom-call | flops 6442450944 | bytes 13631488 | tf_op jit(solution)/shard_map/pallas_call | solution.py:310
  830.7 13.1 %shard_map.264 = (bf16[512,2048]{1,0:T(8,128)(2,1)}, bf16[512,2048]{1,0:T(8,128)(2,1)}) custom-call(s32[4]{0:T(128)} %broadcast_xor_fusion.order_ref, bf16[1024,512]{1,0:T(8,128)(2,1)} %get-tuple-element.1348.refs_3_.refs_0_, bf16[1024,512]{1,0:T(8,128)(2,1)} %get-tuple-element.1369.refs_3_.refs_1_, bf16[1024,512]{1,0:T(8,128)(2,1)} %get-tuple-element.1371.refs_5_.refs_2_, ...), custom_call_target="tpu_custom_call" | custom-call | flops 6442450944 | bytes 13631488 | tf_op jit(solution)/shard_map/pallas_call | solution.py:310
  844.5 18.3 %collective-permute-done.60.refs_6_ = bf16[2048,512]{1,0:T(8,128)(2,1)} collective-permute-done((bf16[2048,512]{1,0:T(8,128)(2,1)}, bf16[2048,512]{1,0:T(8,128)(2,1)}, u32[]{:S(2)}, u32[]{:S(2)}) %collective-permute-start.60) | collective-permute-done | bytes 2097184 | tf_op jit(solution)/shard_map/ppermute | solution.py:46
  862.8 11.3 %shard_map.265 = bf16[2048,512]{1,0:T(8,128)(2,1)} custom-call(bf16[1024,2048]{1,0:T(8,128)(2,1)} %get-tuple-element.1366.refs_0_, bf16[1024,2048]{1,0:T(8,128)(2,1)} %get-tuple-element.1367.refs_1_, bf16[1024,512]{1,0:T(8,128)(2,1)} %get-tuple-element.1368.refs_2_.refs_1_, bf16[1024,512]{1,0:T(8,128)(2,1)} %get-tuple-element.1369.refs_3_.refs_1_, ...), custom_call_target="tpu_custom_call" | custom-call | flops 4294967296 | bytes 14680064 | tf_op jit(solution)/shard_map/pallas_call | solution.py:371
  888.4 15.1 %collective-permute-done.62 = bf16[256,2048]{1,0:T(8,128)(2,1)} collective-permute-done((bf16[256,2048]{1,0:T(8,128)(2,1)}, bf16[256,2048]{1,0:T(8,128)(2,1)}, u32[]{:S(2)}, u32[]{:S(2)}) %collective-permute-start.62) | collective-permute-done | bytes 1048608 | tf_op jit(solution)/shard_map/ppermute | solution.py:38
  910.6 12.8 %collective-permute-done.61 = bf16[256,2048]{1,0:T(8,128)(2,1)S(1)} collective-permute-done((bf16[256,2048]{1,0:T(8,128)(2,1)S(1)}, bf16[256,2048]{1,0:T(8,128)(2,1)S(1)}, u32[]{:S(2)}, u32[]{:S(2)}) %collective-permute-start.61) | collective-permute-done | bytes 1048608 | tf_op jit(solution)/shard_map/ppermute | solution.py:38
  935.6 5.4 reduce-scatter.12.cloned.1.call-done
  949.9 11.2 %collective-permute-start.67 = (f32[1,4112]{1,0:T(1,128)S(1)}, f32[1,4112]{1,0:T(1,128)S(1)}, u32[]{:S(2)}, u32[]{:S(2)}) collective-permute-start(f32[1,4112]{1,0:T(1,128)S(1)} %add.360), channel_id=1, source_target_pairs={{0,4},{4,0},{8,12},{12,8},{1,5},{5,1},{9,13},{13,9},{2,6},{6,2},{1... | collective-permute-start | bytes 49352 | tf_op jit(solution)/shard_map/ppermute | solution.py:1143
  (448 shorter events, 291.1 us)
Async XLA Ops:
  7.2 56.8 %all-gather.6.cloned.1.call-start = ((), (), s32[]{:S(2)}) async-start(), calls=%async_computation.5 | async-start | bytes 2621440 | tf_op jit(solution)/shard_map/all_gather | solution.py:410
  9.3 78.3 %all-gather.8.cloned.1.call-start = ((), (), s32[]{:S(2)}) async-start(), calls=%async_computation.6 | async-start | bytes 1310720 | tf_op jit(solution)/shard_map/all_gather | solution.py:410
  9.4 49.0 %collective-permute-start.1 = (bf16[2,256,2048]{2,1,0:T(8,128)(2,1)}, bf16[2,256,2048]{2,1,0:T(8,128)(2,1)}, u32[]{:S(2)}, u32[]{:S(2)}) collective-permute-start(bf16[2,256,2048]{2,1,0:T(8,128)(2,1)} %refs_0_.1), channel_id=1, source_target_pairs={{0,16},{16,0},{1,17},{17,1},{2,18},{18,2},{3,19},{19,3},{4,20},{20... | collective-permute-start | bytes 6291464 | tf_op jit(solution)/shard_map/ppermute | solution.py:46
  16.4 47.4 %collective-permute-start = (bf16[2,256,2048]{2,1,0:T(8,128)(2,1)}, bf16[2,256,2048]{2,1,0:T(8,128)(2,1)}, u32[]{:S(2)}, u32[]{:S(2)}) collective-permute-start(bf16[2,256,2048]{2,1,0:T(8,128)(2,1)} %fusion.2.refs_0_), channel_id=1, source_target_pairs={{0,2},{1,3},{2,0},{3,1},{4,6},{5,7},{6,4},{7,5},{8,10},{9,11},{10,... | collective-permute-start | bytes 6291464 | tf_op jit(solution)/shard_map/ppermute | solution.py:38
  17.9 51.6 %collective-permute-start.2 = (bf16[2,256,2048]{2,1,0:T(8,128)(2,1)}, bf16[2,256,2048]{2,1,0:T(8,128)(2,1)}, u32[]{:S(2)}, u32[]{:S(2)}) collective-permute-start(bf16[2,256,2048]{2,1,0:T(8,128)(2,1)} %fusion.2.refs_0_), channel_id=1, source_target_pairs={{0,1},{1,0},{2,3},{3,2},{4,5},{5,4},{6,7},{7,6},{8,9},{9,8},{10,11... | collective-permute-start | bytes 6291464 | tf_op jit(solution)/shard_map/ppermute | solution.py:38
  18.7 121.4 %all-gather.10.cloned.1.call-start = ((), (), s32[]{:S(2)}) async-start(), calls=%async_computation.7 | async-start | bytes 1310720 | tf_op jit(solution)/shard_map/all_gather | solution.py:410
  63.9 233.2 %all-gather.12.cloned.1.call-start = ((), (), s32[]{:S(2)}) async-start(), calls=%async_computation.8 | async-start | bytes 10485760 | tf_op jit(solution)/shard_map/all_gather | solution.py:410
  66.7 37.5 %collective-permute-start.4 = (bf16[1536,512]{1,0:T(8,128)(2,1)}, bf16[1536,512]{1,0:T(8,128)(2,1)}, u32[]{:S(2)}, u32[]{:S(2)}) collective-permute-start(bf16[1536,512]{1,0:T(8,128)(2,1)} %pad_maximum_fusion.3), channel_id=1, source_target_pairs={{0,16},{16,0},{1,17},{17,1},{2,18},{18,2},{3,19},{19,3},{4,20},{20... | collective-permute-start | bytes 4718600 | tf_op jit(solution)/shard_map/ppermute | solution.py:46
  67.1 328.7 %all-gather.14.cloned.1.call-start = ((), (), s32[]{:S(2)}) async-start(), calls=%async_computation.9 | async-start | bytes 5242880 | tf_op jit(solution)/shard_map/all_gather | solution.py:410
  67.4 57.9 %collective-permute-start.6 = (bf16[2,256,2048]{2,1,0:T(8,128)(2,1)}, bf16[2,256,2048]{2,1,0:T(8,128)(2,1)}, u32[]{:S(2)}, u32[]{:S(2)}) collective-permute-start(bf16[2,256,2048]{2,1,0:T(8,128)(2,1)} %refs_0_.1), channel_id=1, source_target_pairs={{0,2},{1,3},{2,0},{3,1},{4,6},{5,7},{6,4},{7,5},{8,10},{9,11},{10,... | collective-permute-start | bytes 6291464 | tf_op jit(solution)/shard_map/ppermute | solution.py:38
  69.2 111.7 %collective-permute-start.10 = (bf16[2,256,2048]{2,1,0:T(8,128)(2,1)}, bf16[2,256,2048]{2,1,0:T(8,128)(2,1)}, u32[]{:S(2)}, u32[]{:S(2)}) collective-permute-start(bf16[2,256,2048]{2,1,0:T(8,128)(2,1)} %collective-permute-done.1.refs_1_), channel_id=1, source_target_pairs={{0,2},{1,3},{2,0},{3,1},{4,6},{5,7},{6,4},{7,5},{8,10},{9,11},{10,... | collective-permute-start | bytes 6291464 | tf_op jit(solution)/shard_map/ppermute | solution.py:38
  88.9 36.4 %collective-permute-start.5 = (bf16[1536,256]{1,0:T(8,128)(2,1)S(1)}, bf16[1536,256]{1,0:T(8,128)(2,1)S(1)}, u32[]{:S(2)}, u32[]{:S(2)}) collective-permute-start(bf16[1536,256]{1,0:T(8,128)(2,1)S(1)} %pad_maximum_fusion.4), channel_id=1, source_target_pairs={{0,16},{16,0},{1,17},{17,1},{2,18},{18,2},{3,19},{19,3},{4,20},{20... | collective-permute-start | bytes 2359304 | tf_op jit(solution)/shard_map/ppermute | solution.py:46
  141.3 34.8 %collective-permute-start.11 = (bf16[1536,256]{1,0:T(8,128)(2,1)S(1)}, bf16[1536,256]{1,0:T(8,128)(2,1)S(1)}, u32[]{:S(2)}, u32[]{:S(2)}) collective-permute-start(bf16[1536,256]{1,0:T(8,128)(2,1)S(1)} %pad_maximum_fusion.5), channel_id=1, source_target_pairs={{0,16},{16,0},{1,17},{17,1},{2,18},{18,2},{3,19},{19,3},{4,20},{20... | collective-permute-start | bytes 2359304 | tf_op jit(solution)/shard_map/ppermute | solution.py:46
  153.0 27.9 %collective-permute-start.7 = (bf16[8,129,128]{2,1,0:T(8,128)(2,1)S(1)}, bf16[8,129,128]{2,1,0:T(8,128)(2,1)S(1)}, u32[]{:S(2)}, u32[]{:S(2)}) collective-permute-start(bf16[8,129,128]{2,1,0:T(8,128)(2,1)S(1)} %maximum_maximum_fusion), channel_id=1, source_target_pairs={{0,4},{4,8},{8,12},{1,5},{5,9},{9,13},{2,6},{6,10},{10,14},{3,7},{... | collective-permute-start | bytes 792584 | tf_op jit(solution)/shard_map/ppermute | solution.py:390
  161.1 31.8 %collective-permute-start.9 = (bf16[8,129,128]{2,1,0:T(8,128)(2,1)S(1)}, bf16[8,129,128]{2,1,0:T(8,128)(2,1)S(1)}, u32[]{:S(2)}, u32[]{:S(2)}) collective-permute-start(bf16[8,129,128]{2,1,0:T(8,128)(2,1)S(1)} %maximum_maximum_fusion), channel_id=1, source_target_pairs={{0,12},{1,13},{2,14},{3,15},{16,28},{17,29},{18,30},{19,31}} | collective-permute-start | bytes 792584 | tf_op jit(solution)/shard_map/ppermute | solution.py:390
  248.3 48.7 %collective-permute-start.17 = (bf16[1,256,2048]{2,1,0:T(8,128)(2,1)}, bf16[1,256,2048]{2,1,0:T(8,128)(2,1)}, u32[]{:S(2)}, u32[]{:S(2)}) collective-permute-start(bf16[1,256,2048]{2,1,0:T(8,128)(2,1)} %bitcast.7.refs_0_), channel_id=1, source_target_pairs={{0,16},{16,0},{1,17},{17,1},{2,18},{18,2},{3,19},{19,3},{4,20},{20... | collective-permute-start | bytes 3145736 | tf_op jit(solution)/shard_map/ppermute | solution.py:46
  295.4 328.6 %reduce-scatter.6.cloned.1.call-start = ((), (), s32[]{:S(2)}) async-start(), calls=%async_computation.10 | async-start | bytes 5242880 | tf_op jit(solution)/shard_map/reduce_scatter | solution.py:461
  295.5 45.1 %collective-permute-start.23 = (bf16[1,256,2048]{2,1,0:T(8,128)(2,1)S(1)}, bf16[1,256,2048]{2,1,0:T(8,128)(2,1)}, u32[]{:S(2)}, u32[]{:S(2)}) collective-permute-start(bf16[1,256,2048]{2,1,0:T(8,128)(2,1)S(1)} %bitcast.47), channel_id=1, source_target_pairs={{0,16},{16,0},{1,17},{17,1},{2,18},{18,2},{3,19},{19,3},{4,20},{20... | collective-permute-start | bytes 3145736 | tf_op jit(solution)/shard_map/ppermute | solution.py:46
  296.5 44.8 %collective-permute-start.24 = (bf16[1,256,2048]{2,1,0:T(8,128)(2,1)S(1)}, bf16[1,256,2048]{2,1,0:T(8,128)(2,1)}, u32[]{:S(2)}, u32[]{:S(2)}) collective-permute-start(bf16[1,256,2048]{2,1,0:T(8,128)(2,1)S(1)} %bitcast.48), channel_id=1, source_target_pairs={{0,2},{1,3},{2,0},{3,1},{4,6},{5,7},{6,4},{7,5},{8,10},{9,11},{10,... | collective-permute-start | bytes 3145736 | tf_op jit(solution)/shard_map/ppermute | solution.py:38
  321.2 46.6 %collective-permute-start.26 = (bf16[1,256,2048]{2,1,0:T(8,128)(2,1)S(1)}, bf16[1,256,2048]{2,1,0:T(8,128)(2,1)}, u32[]{:S(2)}, u32[]{:S(2)}) collective-permute-start(bf16[1,256,2048]{2,1,0:T(8,128)(2,1)S(1)} %bitcast.49), channel_id=1, source_target_pairs={{0,1},{1,0},{2,3},{3,2},{4,5},{5,4},{6,7},{7,6},{8,9},{9,8},{10,11... | collective-permute-start | bytes 3145736 | tf_op jit(solution)/shard_map/ppermute | solution.py:38
  341.2 27.1 %collective-permute-start.28 = (bf16[1,256,2048]{2,1,0:T(8,128)(2,1)}, bf16[1,256,2048]{2,1,0:T(8,128)(2,1)}, u32[]{:S(2)}, u32[]{:S(2)}) collective-permute-start(bf16[1,256,2048]{2,1,0:T(8,128)(2,1)} %collective-permute-done.24.refs_2_), channel_id=1, source_target_pairs={{0,1},{1,0},{2,3},{3,2},{4,5},{5,4},{6,7},{7,6},{8,9},{9,8},{10,11... | collective-permute-start | bytes 3145736 | tf_op jit(solution)/shard_map/ppermute | solution.py:38
  367.4 28.5 %collective-permute-start.30 = (bf16[2,256,2048]{2,1,0:T(8,128)(2,1)S(1)}, bf16[2,256,2048]{2,1,0:T(8,128)(2,1)}, u32[]{:S(2)}, u32[]{:S(2)}) collective-permute-start(bf16[2,256,2048]{2,1,0:T(8,128)(2,1)S(1)} %copy-done.33), channel_id=1, source_target_pairs={{0,1},{1,0},{2,3},{3,2},{4,5},{5,4},{6,7},{7,6},{8,9},{9,8},{10,11... | collective-permute-start | bytes 6291464 | tf_op jit(solution)/shard_map/ppermute | solution.py:38
  367.8 28.0 %collective-permute-start.31 = (bf16[2,256,2048]{2,1,0:T(8,128)(2,1)}, bf16[2,256,2048]{2,1,0:T(8,128)(2,1)}, u32[]{:S(2)}, u32[]{:S(2)}) collective-permute-start(bf16[2,256,2048]{2,1,0:T(8,128)(2,1)} %collective-permute-done.1.refs_1_), channel_id=1, source_target_pairs={{0,1},{1,0},{2,3},{3,2},{4,5},{5,4},{6,7},{7,6},{8,9},{9,8},{10,11... | collective-permute-start | bytes 6291464 | tf_op jit(solution)/shard_map/ppermute | solution.py:38
  367.9 28.0 %collective-permute-start.32 = (bf16[2,256,2048]{2,1,0:T(8,128)(2,1)}, bf16[2,256,2048]{2,1,0:T(8,128)(2,1)}, u32[]{:S(2)}, u32[]{:S(2)}) collective-permute-start(bf16[2,256,2048]{2,1,0:T(8,128)(2,1)} %collective-permute-done.6.refs_2_), channel_id=1, source_target_pairs={{0,1},{1,0},{2,3},{3,2},{4,5},{5,4},{6,7},{7,6},{8,9},{9,8},{10,11... | collective-permute-start | bytes 6291464 | tf_op jit(solution)/shard_map/ppermute | solution.py:38
  368.3 27.6 %collective-permute-start.33 = (bf16[2,256,2048]{2,1,0:T(8,128)(2,1)}, bf16[2,256,2048]{2,1,0:T(8,128)(2,1)}, u32[]{:S(2)}, u32[]{:S(2)}) collective-permute-start(bf16[2,256,2048]{2,1,0:T(8,128)(2,1)} %collective-permute-done.10.refs_3_), channel_id=1, source_target_pairs={{0,1},{1,0},{2,3},{3,2},{4,5},{5,4},{6,7},{7,6},{8,9},{9,8},{10,11... | collective-permute-start | bytes 6291464 | tf_op jit(solution)/shard_map/ppermute | solution.py:38
  462.5 51.6 %collective-permute-start.35 = (bf16[512,2048]{1,0:T(8,128)(2,1)}, bf16[512,2048]{1,0:T(8,128)(2,1)S(1)}, u32[]{:S(2)}, u32[]{:S(2)}) collective-permute-start(bf16[512,2048]{1,0:T(8,128)(2,1)} %add_convert_fusion.3), channel_id=1, source_target_pairs={{0,2},{1,3},{2,0},{3,1},{4,6},{5,7},{6,4},{7,5},{8,10},{9,11},{10,... | collective-permute-start | bytes 6291464 | tf_op jit(solution)/shard_map/ppermute | solution.py:38
  514.3 274.8 %reduce-scatter.8.cloned.1.call-start = ((), (), s32[]{:S(2)}) async-start(), calls=%async_computation.11 | async-start | bytes 10485760 | tf_op jit(solution)/shard_map/reduce_scatter | solution.py:461
  523.0 49.2 %collective-permute-start.38 = (bf16[256,2048]{1,0:T(8,128)(2,1)}, bf16[256,2048]{1,0:T(8,128)(2,1)S(1)}, u32[]{:S(2)}, u32[]{:S(2)}) collective-permute-start(bf16[256,2048]{1,0:T(8,128)(2,1)} %slice.380), channel_id=1, source_target_pairs={{0,16},{16,0},{1,17},{17,1},{2,18},{18,2},{3,19},{19,3},{4,20},{20... | collective-permute-start | bytes 3145736 | tf_op jit(solution)/shard_map/ppermute | solution.py:46
  527.8 47.9 %collective-permute-start.37 = (bf16[512,2048]{1,0:T(8,128)(2,1)}, bf16[512,2048]{1,0:T(8,128)(2,1)S(1)}, u32[]{:S(2)}, u32[]{:S(2)}) collective-permute-start(bf16[512,2048]{1,0:T(8,128)(2,1)} %add_convert_fusion.2), channel_id=1, source_target_pairs={{0,2},{1,3},{2,0},{3,1},{4,6},{5,7},{6,4},{7,5},{8,10},{9,11},{10,... | collective-permute-start | bytes 6291464 | tf_op jit(solution)/shard_map/ppermute | solution.py:38
  581.9 262.6 %reduce-scatter.10.cloned.1.call-start = ((), (), s32[]{:S(2)}) async-start(), calls=%async_computation.12 | async-start | bytes 1310720 | tf_op jit(solution)/shard_map/reduce_scatter | solution.py:461
  622.9 38.2 %collective-permute-start.45 = (bf16[1,256,2048]{2,1,0:T(8,128)(2,1)S(1)}, bf16[1,256,2048]{2,1,0:T(8,128)(2,1)}, u32[]{:S(2)}, u32[]{:S(2)}) collective-permute-start(bf16[1,256,2048]{2,1,0:T(8,128)(2,1)S(1)} %bitcast.40), channel_id=1, source_target_pairs={{0,2},{1,3},{2,0},{3,1},{4,6},{5,7},{6,4},{7,5},{8,10},{9,11},{10,... | collective-permute-start | bytes 3145736 | tf_op jit(solution)/shard_map/ppermute | solution.py:38
  661.1 34.2 %collective-permute-start.50 = (bf16[1024,2048]{1,0:T(8,128)(2,1)}, bf16[1024,2048]{1,0:T(8,128)(2,1)}, u32[]{:S(2)}, u32[]{:S(2)}) collective-permute-start(bf16[1024,2048]{1,0:T(8,128)(2,1)} %get-tuple-element.1214), channel_id=1, source_target_pairs={{0,1},{1,0},{2,3},{3,2},{4,5},{5,4},{6,7},{7,6},{8,9},{9,8},{10,11... | collective-permute-start | bytes 12582920 | tf_op jit(solution)/shard_map/ppermute | solution.py:38
  661.7 61.2 %collective-permute-start.48 = (bf16[512,1024]{1,0:T(8,128)(2,1)}, bf16[512,1024]{1,0:T(8,128)(2,1)}, u32[]{:S(2)}, u32[]{:S(2)}) collective-permute-start(bf16[512,1024]{1,0:T(8,128)(2,1)} %reduce-scatter.6.cloned.1.call-done), channel_id=1, source_target_pairs={{0,16},{16,0},{1,17},{17,1},{2,18},{18,2},{3,19},{19,3},{4,20},{20... | collective-permute-start | bytes 3145736 | tf_op jit(solution)/shard_map/ppermute | solution.py:46
  662.2 85.1 %collective-permute-start.44 = (bf16[512,2048]{1,0:T(8,128)(2,1)}, bf16[512,2048]{1,0:T(8,128)(2,1)}, u32[]{:S(2)}, u32[]{:S(2)}) collective-permute-start(bf16[512,2048]{1,0:T(8,128)(2,1)} %add_convert_fusion.1), channel_id=1, source_target_pairs={{0,2},{1,3},{2,0},{3,1},{4,6},{5,7},{6,4},{7,5},{8,10},{9,11},{10,... | collective-permute-start | bytes 6291464 | tf_op jit(solution)/shard_map/ppermute | solution.py:38
  699.8 55.5 %collective-permute-start.55 = (bf16[512,2048]{1,0:T(8,128)(2,1)}, bf16[512,2048]{1,0:T(8,128)(2,1)}, u32[]{:S(2)}, u32[]{:S(2)}) collective-permute-start(bf16[512,2048]{1,0:T(8,128)(2,1)} %add_convert_fusion), channel_id=1, source_target_pairs={{0,2},{1,3},{2,0},{3,1},{4,6},{5,7},{6,4},{7,5},{8,10},{9,11},{10,... | collective-permute-start | bytes 6291464 | tf_op jit(solution)/shard_map/ppermute | solution.py:38
  701.4 71.0 %collective-permute-start.52 = (bf16[8,129,128]{2,1,0:T(8,128)(2,1)S(1)}, bf16[8,129,128]{2,1,0:T(8,128)(2,1)}, u32[]{:S(2)}, u32[]{:S(2)}) collective-permute-start(bf16[8,129,128]{2,1,0:T(8,128)(2,1)S(1)} %maximum_maximum_fusion.1), channel_id=1, source_target_pairs={{4,0},{8,4},{12,8},{5,1},{9,5},{13,9},{6,2},{10,6},{14,10},{7,3},{... | collective-permute-start | bytes 792584 | tf_op jit(solution)/shard_map/ppermute | solution.py:390
  721.6 56.2 %collective-permute-start.53 = (bf16[8,129,128]{2,1,0:T(8,128)(2,1)S(1)}, bf16[8,129,128]{2,1,0:T(8,128)(2,1)}, u32[]{:S(2)}, u32[]{:S(2)}) collective-permute-start(bf16[8,129,128]{2,1,0:T(8,128)(2,1)S(1)} %maximum_maximum_fusion.1), channel_id=1, source_target_pairs={{8,0},{12,4},{9,1},{13,5},{10,2},{14,6},{11,3},{15,7},{24,16},{28,... | collective-permute-start | bytes 792584 | tf_op jit(solution)/shard_map/ppermute | solution.py:390
  723.0 54.9 %collective-permute-start.54 = (bf16[8,129,128]{2,1,0:T(8,128)(2,1)S(1)}, bf16[8,129,128]{2,1,0:T(8,128)(2,1)}, u32[]{:S(2)}, u32[]{:S(2)}) collective-permute-start(bf16[8,129,128]{2,1,0:T(8,128)(2,1)S(1)} %maximum_maximum_fusion.1), channel_id=1, source_target_pairs={{12,0},{13,1},{14,2},{15,3},{28,16},{29,17},{30,18},{31,19}} | collective-permute-start | bytes 792584 | tf_op jit(solution)/shard_map/ppermute | solution.py:390
  789.1 145.9 %reduce-scatter.14.cloned.1.call-start = ((), (), s32[]{:S(2)}) async-start(), calls=%async_computation.14 | async-start | bytes 2621440 | tf_op jit(solution)/shard_map/reduce_scatter | solution.py:461
  792.5 148.5 %reduce-scatter.12.cloned.1.call-start = ((), (), s32[]{:S(2)}) async-start(), calls=%async_computation.13 | async-start | bytes 2621440 | tf_op jit(solution)/shard_map/reduce_scatter | solution.py:461
  816.1 46.7 %collective-permute-start.60 = (bf16[2048,512]{1,0:T(8,128)(2,1)}, bf16[2048,512]{1,0:T(8,128)(2,1)}, u32[]{:S(2)}, u32[]{:S(2)}) collective-permute-start(bf16[2048,512]{1,0:T(8,128)(2,1)} %shard_map.262), channel_id=1, source_target_pairs={{0,16},{16,0},{1,17},{17,1},{2,18},{18,2},{3,19},{19,3},{4,20},{20... | collective-permute-start | bytes 6291464 | tf_op jit(solution)/shard_map/ppermute | solution.py:46
  830.6 43.5 %collective-permute-start.59 = (bf16[512,2048]{1,0:T(8,128)(2,1)}, bf16[512,2048]{1,0:T(8,128)(2,1)}, u32[]{:S(2)}, u32[]{:S(2)}) collective-permute-start(bf16[512,2048]{1,0:T(8,128)(2,1)} %get-tuple-element.1360), channel_id=1, source_target_pairs={{0,1},{1,0},{2,3},{3,2},{4,5},{5,4},{6,7},{7,6},{8,9},{9,8},{10,11... | collective-permute-start | bytes 6291464 | tf_op jit(solution)/shard_map/ppermute | solution.py:38
  843.8 36.1 %collective-permute-start.58 = (bf16[512,2048]{1,0:T(8,128)(2,1)}, bf16[512,2048]{1,0:T(8,128)(2,1)}, u32[]{:S(2)}, u32[]{:S(2)}) collective-permute-start(bf16[512,2048]{1,0:T(8,128)(2,1)} %get-tuple-element.1358), channel_id=1, source_target_pairs={{0,1},{1,0},{2,3},{3,2},{4,5},{5,4},{6,7},{7,6},{8,9},{9,8},{10,11... | collective-permute-start | bytes 6291464 | tf_op jit(solution)/shard_map/ppermute | solution.py:38
  878.8 51.0 %collective-permute-start.56 = (bf16[256,2048]{1,0:T(8,128)(2,1)}, bf16[256,2048]{1,0:T(8,128)(2,1)}, u32[]{:S(2)}, u32[]{:S(2)}) collective-permute-start(bf16[256,2048]{1,0:T(8,128)(2,1)} %slice.377), channel_id=1, source_target_pairs={{0,16},{16,0},{1,17},{17,1},{2,18},{18,2},{3,19},{19,3},{4,20},{20... | collective-permute-start | bytes 3145736 | tf_op jit(solution)/shard_map/ppermute | solution.py:46
  887.0 36.3 %collective-permute-start.61 = (bf16[256,2048]{1,0:T(8,128)(2,1)S(1)}, bf16[256,2048]{1,0:T(8,128)(2,1)S(1)}, u32[]{:S(2)}, u32[]{:S(2)}) collective-permute-start(bf16[256,2048]{1,0:T(8,128)(2,1)S(1)} %add_convert_fusion.6), channel_id=1, source_target_pairs={{0,2},{1,3},{2,0},{3,1},{4,6},{5,7},{6,4},{7,5},{8,10},{9,11},{10,... | collective-permute-start | bytes 3145736 | tf_op jit(solution)/shard_map/ppermute | solution.py:38
  887.1 53.9 %collective-permute-start.63 = (bf16[512,1024]{1,0:T(8,128)(2,1)S(1)}, bf16[512,1024]{1,0:T(8,128)(2,1)}, u32[]{:S(2)}, u32[]{:S(2)}) collective-permute-start(bf16[512,1024]{1,0:T(8,128)(2,1)S(1)} %get-tuple-element.1442), channel_id=1, source_target_pairs={{0,16},{16,0},{1,17},{17,1},{2,18},{18,2},{3,19},{19,3},{4,20},{20... | collective-permute-start | bytes 3145736 | tf_op jit(solution)/shard_map/ppermute | solution.py:46
  932.9 45.8 %collective-permute-start.71 = (bf16[512,256]{1,0:T(8,128)(2,1)S(1)}, bf16[512,256]{1,0:T(8,128)(2,1)}, u32[]{:S(2)}, u32[]{:S(2)}) collective-permute-start(bf16[512,256]{1,0:T(8,128)(2,1)S(1)} %copy-done.56), channel_id=1, source_target_pairs={{0,16},{16,0},{1,17},{17,1},{2,18},{18,2},{3,19},{19,3},{4,20},{20... | collective-permute-start | bytes 786440 | tf_op jit(solution)/shard_map/ppermute | solution.py:46
  935.0 34.0 %collective-permute-start.66 = (bf16[512,512]{1,0:T(8,128)(2,1)}, bf16[512,512]{1,0:T(8,128)(2,1)}, u32[]{:S(2)}, u32[]{:S(2)}) collective-permute-start(bf16[512,512]{1,0:T(8,128)(2,1)} %reduce-scatter.14.cloned.1.call-done), channel_id=1, source_target_pairs={{0,16},{16,0},{1,17},{17,1},{2,18},{18,2},{3,19},{19,3},{4,20},{20... | collective-permute-start | bytes 1572872 | tf_op jit(solution)/shard_map/ppermute | solution.py:46
  (109 other events, 1330.1 us)
Sparse Core Ops, SparseCore 0:
  10.2 48.6 all-gather.5
  61.0 26.6 all-gather.7
  89.2 27.4 all-gather.9
  118.1 162.7 all-gather.11
  295.6 98.2 all-gather.13
  514.4 94.5 reduce-scatter.5
  611.4 162.6 reduce-scatter.7
  789.2 45.2 reduce-scatter.9
  836.8 42.4 reduce-scatter.13
  882.2 58.7 reduce-scatter.11
